TPU v7x, 32 devices: a whole 2x2x4 slice. The times are simulated.
32 devices in a mesh: shard: 8 (over y, x, core), grp: 4 (over z).
Axes of the slice: x: 2, y: 2, z: 4, core: 2. Of those that a mesh axis runs over, the one named last changes fastest.
Arguments:
- embeddings: float32 [16384, 1024], P(('shard', 'grp')), may hold values from -6 to 6
- cluster: int32 [16384, 1], P(('shard', 'grp')), may hold values from 0 to 7; in each aligned block of 512 rows (0 to 511, 512 to 1023, ...) at most 128 rows name the same one
Outputs:
- duplicate: float32 [16384], P(('shard', 'grp'))
- neighbour: float32 [16384, 1024], P(('shard', 'grp'))
Inputs may be any that keep to these rules, and one draw needn't show every extreme that they name: Among the pages of one device, at most 128 belong to any one cluster.
All inputs are finite; a program needn't handle non-finite values.
Results may differ from a plain program's by a relative error of at most 0.0075.
Values may be sent and summed in bfloat16 or wider, within the bound.
No kernel may reach another device: no remote copies, remote signals or barrier semaphores. Data moves between devices by JAX's collectives and lax.ppermute only.
A program may use at most 128 MiB of HBM per device.

v0:
```python
import jax
import jax.numpy as jnp
from jax import lax
from jax.sharding import PartitionSpec as P


def row_terms(rows_unit, cols_unit, cols_flag, keep):
    scores = jnp.dot(rows_unit, cols_unit.T, preferred_element_type=jnp.float32) * (
        64.0 / rows_unit.shape[1]
    )
    weight = jnp.exp(scores) * cols_flag.astype(jnp.float32)[None, :] * keep
    count = jnp.sum(weight, axis=1)
    pull = jnp.dot(weight.astype(jnp.bfloat16), cols_unit, preferred_element_type=jnp.float32)
    return (count, pull)


def local(embeddings, cluster):
    npages, width = embeddings.shape
    nclus = lax.axis_size("shard")
    slots = 2 * npages // nclus
    blk_rows = nclus * slots
    scale = lax.rsqrt(jnp.mean(embeddings * embeddings, axis=1, keepdims=True) + 1e-06)
    units = (embeddings * scale).astype(jnp.bfloat16)
    ids = cluster[:, 0]
    onehot = (ids[:, None] == jnp.arange(nclus, dtype=jnp.int32)[None, :]).astype(jnp.int32)
    rank = jnp.sum(jnp.cumsum(onehot, axis=0) * onehot, axis=1) - 1
    outbox = jnp.zeros((nclus, slots, width), jnp.bfloat16).at[ids, rank].set(units)
    flags = (
        jnp.zeros((nclus, slots), jnp.bfloat16).at[ids, rank].set(jnp.ones((npages,), jnp.bfloat16))
    )
    inbox, inflags = (
        lax.all_to_all(outbox, "shard", split_axis=0, concat_axis=0, tiled=True),
        lax.all_to_all(flags, "shard", split_axis=0, concat_axis=0, tiled=True),
    )
    own_unit = inbox.reshape(blk_rows, width)
    own_flag = inflags.reshape(blk_rows)
    member = lax.axis_index("grp")
    row_index = member * blk_rows + jnp.arange(blk_rows, dtype=jnp.int32)
    piece_unit = lax.all_gather(own_unit, "grp", axis=0, tiled=True)
    piece_flag = lax.all_gather(own_flag, "grp", axis=0, tiled=True)
    col_index = jnp.arange(piece_unit.shape[0], dtype=jnp.int32)
    keep = (row_index[:, None] != col_index[None, :]).astype(jnp.float32)
    part_count, part_pull = row_terms(own_unit, piece_unit, piece_flag, keep)
    dup_rows = jnp.log1p(part_count)
    near_rows = part_pull / (1.0 + part_count)[:, None]
    back_near, back_dup = (
        lax.all_to_all(
            near_rows.reshape(nclus, slots, width), "shard", split_axis=0, concat_axis=0, tiled=True
        ),
        lax.all_to_all(
            dup_rows.reshape(nclus, slots), "shard", split_axis=0, concat_axis=0, tiled=True
        ),
    )
    return (back_dup[ids, rank], back_near[ids, rank])


def solution(mesh):
    return jax.shard_map(
        local,
        mesh=mesh,
        in_specs=(P(("shard", "grp"), None), P(("shard", "grp"), None)),
        out_specs=(P(("shard", "grp")), P(("shard", "grp"), None)),
        check_vma=False,
    )
```

profile of v0, /device:TPU:0, one launch (start us, length us, event | category | flops | bytes accessed | tf_op | source)
XLA Modules:
  0.0 338.5 jit_solution(13841268420126997272)
XLA Ops:
  7.2 0.0 all-gather.2.cloned.1.call-start
  7.2 0.7 fusion.11
  7.9 1.1 reduce-window.6
  9.0 0.2 slice_reduce_fusion
  9.3 0.8 fusion.10
  10.1 1.8 multiply_reduce_fusion
  11.9 1.8 multiply_convert_fusion
  13.7 0.7 or_select_fusion
  14.4 0.3 broadcast_in_dim.6
  14.6 33.0 %scatter_fusion = bf16[8,128,1024]{2,1,0:T(8,128)(2,1)S(1)} fusion(bf16[8,128,1024]{2,1,0:T(8,128)(2,1)S(1)} %broadcast_in_dim.6, s32[512]{0:T(512)S(1)} %bitcast.23, bf16[512,1024]{1,0:T(8,128)(2,1)S(1)} %multiply_convert_fusion), kind=kCustom, calls=%fused_computation.2 | custom fusion | bytes 3149824 | tf_op jit(solution)/shard_map/scatter | solution.py:27
  47.7 31.7 %all_to_all.28 = bf16[8,128,1024]{2,1,0:T(8,128)(2,1)} all-to-all(bf16[8,128,1024]{2,1,0:T(8,128)(2,1)S(1)} %scatter_fusion), channel_id=1, replica_groups=mesh['shard'=8,'grp'=4] {'shard'}, dimensions={0} | all-to-all | bytes 4194304 | tf_op jit(solution)/shard_map/all_to_all | solution.py:32
  79.4 0.0 all-gather.2.cloned.1.call-update
  79.4 22.6 %scatter_fusion.1 = bf16[8,128]{1,0:T(8,128)(2,1)S(1)} fusion(bf16[8,128]{1,0:T(8,128)(2,1)S(1)} %broadcast_in_dim.7, s32[512]{0:T(512)S(1)} %bitcast.24, bf16[512]{0:T(512)(128)(2,1)S(1)} %broadcast.139), kind=kCustom, calls=%fused_computation.3 | custom fusion | bytes 7168 | tf_op jit(solution)/shard_map/scatter | solution.py:29
  102.0 0.6 copy.5
  102.6 3.3 all-to-all-start.1
  105.9 4.5 %all-to-all-done.1 = bf16[8,1,128]{2,1,0:T(2,128)(2,1)S(1)} async-done(((bf16[8,1,128]{2,1,0:T(2,128)(2,1)}), bf16[8,1,128]{2,1,0:T(2,128)(2,1)S(1)}, u32[]{:S(2)}, u32[]{:S(2)}) %all-to-all-start.1) | async-done | bytes 2080 | tf_op jit(solution)/shard_map/all_to_all | solution.py:33
  110.5 16.5 %all_gather.7 = bf16[4096]{0:T(1024)(128)(2,1)S(1)} all-gather(bf16[1024]{0:T(1024)(128)(2,1)S(1)} %bitcast.34), channel_id=1, replica_groups=mesh['shard'=8,'grp'=4] {'grp'}, dimensions={0}, use_global_device_ids=true | all-gather | bytes 10240 | tf_op jit(solution)/shard_map/all_gather | solution.py:40
  127.0 101.7 %all-gather.2.cloned.1.call-done = bf16[4096,1024]{1,0:T(8,128)(2,1)} async-done(((bf16[1024,1024]{1,0:T(8,128)(2,1)}), bf16[4096,1024]{1,0:T(8,128)(2,1)}) %all-gather.2.cloned.1.call-update) | async-done | bytes 8388624 | tf_op jit(solution)/shard_map/all_gather | solution.py:39
  228.6 18.1 %fusion.1 = (f32[1024]{0:T(1024)S(1)}, f32[1024,4096]{1,0:T(8,128)}) fusion(f32[4096]{0:T(1024)S(1)} %convert_element_type.17, s32[1024]{0:T(1024)S(1)} %iota_add_fusion, bf16[1024,1024]{1,0:T(8,128)(2,1)} %bitcast.28, bf16[4096,1024]{1,0:T(8,128)(2,1)} %all-gather.2.cloned.1.call-done), kind=kOutput, calls=%fused_computation.7 | convolution fusion | flops 8610905088 | bytes 27287552 | tf_op jit(solution)/shard_map/dot_general | solution.py:8
  246.7 0.6 broadcast_add_fusion
  247.3 3.7 %all-to-all-start.2 = ((f32[8,1,128]{2,1,0:T(1,128)}), f32[8,1,128]{2,1,0:T(1,128)S(1)}, u32[]{:S(2)}, u32[]{:S(2)}) async-start(f32[8,1,128]{2,1,0:T(1,128)} %bitcast.9), calls=%async_computation.2 | async-start | bytes 8192 | tf_op jit(solution)/shard_map/all_to_all | solution.py:50
  251.0 16.5 %broadcast_divide_fusion = f32[1024,1024]{1,0:T(8,128)} fusion(f32[1024]{0:T(1024)S(1)} %get-tuple-element.4, bf16[4096,1024]{1,0:T(8,128)(2,1)} %all-gather.2.cloned.1.call-done, f32[1024,4096]{1,0:T(8,128)} %get-tuple-element.9, f32[4096]{0:T(1024)S(1)} %convert_element_type.17, s32[1024]{0:T(1024)S(1)} %iota_add_fusion), kind=kOutput, calls=%fused_computation.13 | convolution fusion | flops 8611954688 | bytes 29384704 | tf_op jit(solution)/shard_map/dot_general | solution.py:13
  267.5 0.0 all-to-all-done.2
  267.5 4.5 %all-to-all-start.3 = ((f32[8,128,1024]{2,1,0:T(8,128)}), f32[8,128,1024]{2,1,0:T(8,128)}, u32[]{:S(2)}, u32[]{:S(2)}) async-start(f32[8,128,1024]{2,1,0:T(8,128)} %bitcast.29), calls=%async_computation.3 | async-start | bytes 8388608 | tf_op jit(solution)/shard_map/all_to_all | solution.py:47
  272.0 4.7 %gather_fusion = f32[512]{0:T(512)} fusion(f32[8,128]{1,0:T(8,128)S(1)} %bitcast.21, s32[512]{0:T(512)S(1)} %bitcast.25), kind=kCustom, calls=%fused_computation | custom fusion | bytes 8192 | tf_op jit(solution)/shard_map/gather | solution.py:54
  276.7 44.5 %all-to-all-done.3 = f32[8,128,1024]{2,1,0:T(8,128)} async-done(((f32[8,128,1024]{2,1,0:T(8,128)}), f32[8,128,1024]{2,1,0:T(8,128)}, u32[]{:S(2)}, u32[]{:S(2)}) %all-to-all-start.3) | async-done | bytes 4194336 | tf_op jit(solution)/shard_map/all_to_all | solution.py:47
  321.2 10.4 %gather_fusion.1 = f32[512,1024]{1,0:T(8,128)} fusion(f32[8,128,1024]{2,1,0:T(8,128)} %all-to-all-done.3, s32[512]{0:T(512)S(1)} %bitcast.26), kind=kCustom, calls=%fused_computation.1 | custom fusion | bytes 4198400 | tf_op jit(solution)/shard_map/gather | solution.py:54
  (9 shorter events, 0.1 us)
Async XLA Ops:
  7.2 221.5 %all-gather.2.cloned.1.call-start = ((), (), s32[]{:S(2)}) async-start(), calls=%async_computation.4 | async-start | bytes 10485760 | tf_op jit(solution)/shard_map/all_gather | solution.py:39
  102.6 7.8 %all-to-all-start.1 = ((bf16[8,1,128]{2,1,0:T(2,128)(2,1)}), bf16[8,1,128]{2,1,0:T(2,128)(2,1)S(1)}, u32[]{:S(2)}, u32[]{:S(2)}) async-start(bf16[8,1,128]{2,1,0:T(2,128)(2,1)} %copy.5), calls=%async_computation.1 | async-start | bytes 8192 | tf_op jit(solution)/shard_map/all_to_all | solution.py:33
  247.3 20.2 %all-to-all-start.2 = ((f32[8,1,128]{2,1,0:T(1,128)}), f32[8,1,128]{2,1,0:T(1,128)S(1)}, u32[]{:S(2)}, u32[]{:S(2)}) async-start(f32[8,1,128]{2,1,0:T(1,128)} %bitcast.9), calls=%async_computation.2 | async-start | bytes 8192 | tf_op jit(solution)/shard_map/all_to_all | solution.py:50
  267.5 53.7 %all-to-all-start.3 = ((f32[8,128,1024]{2,1,0:T(8,128)}), f32[8,128,1024]{2,1,0:T(8,128)}, u32[]{:S(2)}, u32[]{:S(2)}) async-start(f32[8,128,1024]{2,1,0:T(8,128)} %bitcast.29), calls=%async_computation.3 | async-start | bytes 8388608 | tf_op jit(solution)/shard_map/all_to_all | solution.py:47
Sparse Core Ops, SparseCore 0:
  79.5 149.1 all-gather.1
where the time goes:
time: 339 us; the launch traced here: 338 us
  waiting for transfers between devices  151 us (45%)
  local copies, waits for them, and re-layouts  71.8 us (21%)
  blocking collectives  48.2 us (14%)
  matrix products  34.6 us (10%)
  between operations  14.1 us (4%)
  starting transfers between devices  11.6 us (3%)
  other arithmetic  7.54 us (2%)
    all_gather x1, waiting for transfers between devices, local(): piece_unit = lax.all_gather(own_unit, 'grp', axis=0, tiled=True)  102 us
    all_to_all x1, waiting for transfers between devices, local(): lax.all_to_all(near_rows.reshape(nclus, slots, width), 'shard', split_axi...  44.5 us
    scatter x1, local copies, waits for them, and re-layouts, local(): jnp.zeros((nclus, slots, width), jnp.bfloat16).at[ids, rank].set(units)  33 us
    all_to_all x1, blocking collectives, local(): lax.all_to_all(outbox, 'shard', split_axis=0, concat_axis=0, tiled=True)  31.7 us
    scatter x1, local copies, waits for them, and re-layouts, local(): jnp.zeros((nclus, slots), jnp.bfloat16).at[ids, rank]  22.6 us
    dot_general x1, matrix products, row_terms(): jnp.dot(rows_unit, cols_unit.T, preferred_element_type=jnp.float32)  18.1 us
    all_gather x1, blocking collectives, local(): piece_flag = lax.all_gather(own_flag, 'grp', axis=0, tiled=True)  16.5 us
    dot_general x1, matrix products, row_terms(): jnp.dot(weight.astype(jnp.bfloat16), cols_unit, preferred_element_type=jn...  16.5 us
  transfers between devices with their start and end apart: 4, of which 3 were waited for; matrix products, arithmetic and copies ran while one was open for 13% of the time, Pallas kernels for 0%

commit v1 on v0

v1 whole, which is shorter than its diff:
```python
import functools

import jax
import jax.numpy as jnp
from jax import lax
from jax.experimental import pallas as pl
from jax.experimental.pallas import tpu as pltpu
from jax.sharding import PartitionSpec as P

AXES = ("shard", "grp")
EXTRA = 8
MIB = 1 << 20


def hop_order(ng):
    return sorted(range(ng), key=lambda d: (min(d, ng - d), d))


def pack_kernel(hi_n, ng, slots, emb_ref, ids_ref, pos_ref, *out_refs):
    n, width = emb_ref.shape
    nb = hi_n * ng
    emb = emb_ref[...]
    scale = lax.rsqrt(jnp.mean(emb * emb, axis=1, keepdims=True) + 1e-06)
    units = (emb * scale).astype(jnp.bfloat16)
    hi = lax.axis_index("shard") // ng
    z = lax.axis_index("grp")
    ids = ids_ref[...]
    blk = jnp.zeros((1, n), jnp.int32)
    for k, dz in enumerate(hop_order(ng)):
        for dh in range(hi_n):
            owner = lax.rem(hi + dh, hi_n) * ng + lax.rem(z + dz, ng)
            blk = jnp.where(ids == owner, k * hi_n + dh, blk)
    onehot = lax.broadcasted_iota(jnp.int32, (nb, n), 0) == blk
    upto = lax.broadcasted_iota(jnp.int32, (n, n), 0) <= lax.broadcasted_iota(jnp.int32, (n, n), 1)
    cum = jnp.dot(
        onehot.astype(jnp.bfloat16), upto.astype(jnp.bfloat16), preferred_element_type=jnp.float32
    )
    rank = jnp.sum(jnp.where(onehot, cum, 0.0), axis=0, keepdims=True).astype(jnp.int32) - 1
    pos = blk * slots + rank
    pos_ref[...] = pos
    mark = float(2.0 * width**0.5)
    for k in range(nb):
        pick = lax.broadcasted_iota(jnp.int32, (slots, n), 0) + k * slots == pos
        rows = jnp.dot(pick.astype(jnp.bfloat16), units, preferred_element_type=jnp.float32)
        used = cum[k : k + 1, n - 1 : n].astype(jnp.int32)
        empty = lax.broadcasted_iota(jnp.int32, (slots, width), 0) >= used
        first = lax.broadcasted_iota(jnp.int32, (slots, width), 1) == 0
        out_refs[k][...] = jnp.where(empty & first, mark, rows).astype(jnp.bfloat16)


def weigh_kernel(sizes, blocks, own, slots, chunk, *refs):
    ncol = len(sizes)
    cols, outs = refs[:ncol], refs[ncol : ncol + len(blocks)]
    units, rows, pull, count, sems = refs[ncol + len(blocks) :]
    total, width = units.shape
    nrows = len(blocks) * slots
    starts = [sum(sizes[:i]) for i in range(ncol)]
    copies = [
        pltpu.make_async_copy(cols[i], units.at[pl.ds(starts[i], sizes[i])], sems.at[i])
        for i in range(ncol)
    ]
    for c in copies:
        c.start()
    waited = 0
    limit = 1.5 * width**0.5
    probe = lax.broadcasted_iota(jnp.int32, (16, width), 1) == 0
    rows[pl.ds(nrows, 16), :] = probe.astype(jnp.bfloat16)
    for at in range(0, total, chunk):
        need = own if at == 0 else at + chunk
        while waited < ncol and starts[waited] < need:
            copies[waited].wait()
            waited += 1
        if at == 0:
            for i, b in enumerate(blocks):
                rows[pl.ds(i * slots, slots), :] = units[pl.ds(b * slots, slots), :]
        part = units[pl.ds(at, chunk), :]
        scores = lax.dot_general(
            rows[...], part, (((1,), (1,)), ((), ())), preferred_element_type=jnp.float32
        )
        keep = jnp.broadcast_to(scores[nrows : nrows + 1, :] < limit, (nrows, chunk))
        if at < own:
            col = lax.broadcasted_iota(jnp.int32, (slots, chunk), 1) + at
            row = lax.broadcasted_iota(jnp.int32, (slots, chunk), 0)
            off = jnp.concatenate([col != row + b * slots for b in blocks], axis=0)
            keep = keep & off
        weight = jnp.where(keep, jnp.exp(scores[:nrows] * (64.0 / width)), 0.0)
        add_count = jnp.sum(weight, axis=1, keepdims=True)
        add_pull = jnp.dot(weight.astype(jnp.bfloat16), part, preferred_element_type=jnp.float32)
        if at == 0:
            count[...] = jnp.broadcast_to(add_count, count.shape)
            pull[...] = add_pull
        else:
            count[...] += jnp.broadcast_to(add_count, count.shape)
            pull[...] += add_pull
    valid = rows[pl.ds(0, nrows), 0:128].astype(jnp.float32)[:, 0:1] < limit
    for i in range(len(blocks)):
        at = i * slots
        ok = valid[at : at + slots]
        cnt = count[pl.ds(at, slots), :]
        near = pull[pl.ds(at, slots), :] / (1.0 + cnt[:, 0:1])
        outs[i][pl.ds(0, slots), :] = jnp.where(ok, near, 0.0).astype(jnp.bfloat16)
        dup = jnp.where(ok, jnp.log1p(cnt), 0.0)
        if slots < 128:
            dup = jnp.concatenate([dup, jnp.zeros((128 - slots, 128), jnp.float32)], axis=0)
        dup = dup.T[0:EXTRA]
        high = dup.astype(jnp.bfloat16).astype(jnp.float32)
        line = lax.broadcasted_iota(jnp.int32, (EXTRA, 128), 0)
        two = jnp.where(line == 0, high, jnp.where(line == 1, dup - high, 0.0))
        outs[i][pl.ds(slots, EXTRA), pl.ds(0, 128)] = two.astype(jnp.bfloat16)


def unpack_kernel(slots, pos_ref, *refs):
    blocks, dup_ref, near_ref = refs[:-2], refs[-2], refs[-1]
    n = pos_ref.shape[1]
    pos = pos_ref[...]
    dup = jnp.zeros((EXTRA, n), jnp.float32)
    for k, ref in enumerate(blocks):
        pick = lax.broadcasted_iota(jnp.int32, (slots, n), 0) + k * slots == pos
        pick = pick.astype(jnp.bfloat16)
        near = lax.dot_general(
            pick,
            ref[pl.ds(0, slots), :],
            (((0,), (0,)), ((), ())),
            preferred_element_type=jnp.float32,
        )
        if k == 0:
            near_ref[...] = near
        else:
            near_ref[...] += near
        two = ref[pl.ds(slots, EXTRA), pl.ds(0, 128)][:, :slots]
        dup = dup + jnp.dot(two, pick, preferred_element_type=jnp.float32)
    dup_ref[...] = dup[0:1] + dup[1:2]


def after(value, *deps):
    return lax.optimization_barrier((value,) + deps)[0]


def local(embeddings, cluster):
    n, width = embeddings.shape
    ns, ng = lax.axis_size("shard"), lax.axis_size("grp")
    hi_n = ns // ng
    nb = ns
    slots = 2 * n // ns
    own = nb * slots

    def moved(f):
        return [(s * ng + z, f(s, z)) for s in range(ns) for z in range(ng)]

    def to_owner(dh, dz, sign):
        return moved(
            lambda s, z: ((s // ng + sign * dh) % hi_n * ng + s % ng) * ng + (z + sign * dz) % ng
        )

    def beside(bit):
        return moved(lambda s, z: (s ^ bit) * ng + z)

    hops = [(dh, dz) for dz in hop_order(ng) for dh in range(hi_n)]
    vmem = pl.BlockSpec(memory_space=pltpu.VMEM)
    anyspace = pl.BlockSpec(memory_space=pl.ANY)
    ids = cluster.reshape(1, n)
    pos, *outbox = pl.pallas_call(
        functools.partial(pack_kernel, hi_n, ng, slots),
        out_shape=[jax.ShapeDtypeStruct((1, n), jnp.int32)]
        + [jax.ShapeDtypeStruct((slots, width), jnp.bfloat16)] * nb,
        in_specs=[vmem, vmem],
        out_specs=[vmem] * (nb + 1),
        compiler_params=pltpu.CompilerParams(vmem_limit_bytes=40 * MIB),
        name="pack",
    )(embeddings, ids)

    window = 3
    inbox = [outbox[0]]
    for k in range(1, nb):
        src = outbox[k]
        if k > window:
            src = after(src, inbox[k - window])
        inbox.append(lax.ppermute(src, AXES, to_owner(*hops[k], 1)))
    per = max(1, nb // 8)
    groups = [inbox[i : i + per] for i in range(0, nb, per)]
    near_by = [g[0] if len(g) == 1 else jnp.concatenate(g, axis=0) for g in groups]
    beyond = [lax.ppermute(g, AXES, beside(2)) for g in near_by]
    other = []
    for i in range(0, len(groups), 2):
        both = jnp.concatenate(near_by[i : i + 2] + beyond[i : i + 2], axis=0)
        other.append(lax.ppermute(both, AXES, beside(1)))
    columns = inbox + beyond + other
    sizes = [c.shape[0] for c in columns]
    total = sum(sizes)

    def weigh(blocks):
        nrows = len(blocks) * slots
        return pl.pallas_call(
            functools.partial(weigh_kernel, sizes, blocks, own, slots, 512),
            out_shape=[jax.ShapeDtypeStruct((slots + EXTRA, width), jnp.bfloat16)] * len(blocks),
            in_specs=[anyspace] * len(columns),
            out_specs=[vmem] * len(blocks),
            scratch_shapes=[
                pltpu.VMEM((total, width), jnp.bfloat16),
                pltpu.VMEM((nrows + 16, width), jnp.bfloat16),
                pltpu.VMEM((nrows, width), jnp.float32),
                pltpu.VMEM((nrows, 128), jnp.float32),
                pltpu.SemaphoreType.DMA((len(columns),)),
            ],
            compiler_params=pltpu.CompilerParams(vmem_limit_bytes=48 * MIB),
            cost_estimate=pl.CostEstimate(
                flops=4 * nrows * total * width,
                bytes_accessed=2 * total * width,
                transcendentals=nrows * total,
            ),
            name="weigh",
        )(*columns)

    result = [None] * nb
    far = list(range(nb - nb // 4, nb))
    rest = list(range(nb // 4, nb - nb // 4)) + list(range(nb // 4))
    for part in (far, rest):
        for b, r in zip(part, weigh(part)):
            result[b] = r
    back = [result[0]] + [None] * (nb - 1)
    for b in far + rest:
        if b:
            back[b] = lax.ppermute(result[b], AXES, to_owner(*hops[b], -1))
    dup, near = pl.pallas_call(
        functools.partial(unpack_kernel, slots),
        out_shape=[
            jax.ShapeDtypeStruct((1, n), jnp.float32),
            jax.ShapeDtypeStruct((n, width), jnp.float32),
        ],
        in_specs=[vmem] * (nb + 1),
        out_specs=[vmem, vmem],
        compiler_params=pltpu.CompilerParams(vmem_limit_bytes=40 * MIB),
        name="unpack",
    )(pos, *back)
    return dup.reshape(n), near


def solution(mesh):
    return jax.shard_map(
        local,
        mesh=mesh,
        in_specs=(P(("shard", "grp"), None), P(("shard", "grp"), None)),
        out_specs=(P(("shard", "grp")), P(("shard", "grp"), None)),
        check_vma=False,
    )
```

time: 339 us -> 153 us (0.45)
  waiting for transfers between devices: 151 us -> 65.6 us
  local copies, waits for them, and re-layouts: 71.8 us -> 4.48 us
  blocking collectives: 48.2 us -> 0 us
  starting transfers between devices: 11.6 us -> 52.2 us
  matrix products: 34.6 us -> 0 us
  Pallas kernels: 0 us -> 29.8 us
  between operations: 14.1 us -> 0.81 us
  other arithmetic: 7.54 us -> 0.28 us
    all_gather x1 -> x0, waiting for transfers between devices: 102 us -> none  [local(): piece_unit = lax.all_gather(own_unit, 'grp', axis=0, tiled=True)]
    ppermute x0 -> x26, waiting for transfers between devices: none -> 65.6 us  [the longest x7 33.8 us: local(): back[b] = lax.ppermute(result[b], AXES, to_owner(*hops[b], -1))]
    scatter x2 -> x0, local copies, waits for them, and re-layouts: 55.6 us -> none  [the longest x1 33 us: local(): jnp.zeros((nclus, slots, width), jnp.bfloat16).at[ids, rank].set(units)]
    ppermute x0 -> x26, starting transfers between devices: none -> 52.2 us  [the longest x7 33.2 us: local(): inbox.append(lax.ppermute(src, AXES, to_owner(*hops[k], 1)))]
    all_to_all x3 -> x0, waiting for transfers between devices: 49 us -> none  [the longest x1 44.5 us: local(): lax.all_to_all(near_rows.reshape(nclus, slots, width), 'shard', split_axi...]
    dot_general x2 -> x0, matrix products: 34.6 us -> none  [the longest x1 18.1 us: row_terms(): jnp.dot(rows_unit, cols_unit.T, preferred_element_type=jnp.float32)]
    all_to_all x1 -> x0, blocking collectives: 31.7 us -> none  [local(): lax.all_to_all(outbox, 'shard', split_axis=0, concat_axis=0, tiled=True)]
    pallas_call x0 -> x4, Pallas kernels: none -> 29.8 us  [the longest x2 24.4 us: weigh(): pl.pallas_call(functools.partial(weigh_kernel, sizes, blocks, own, slots,...]
  transfers between devices with their start and end apart: 4 -> 26, of which waited for: 3 -> 13; matrix products, arithmetic and copies ran while one was open for 13% -> 0% of each run, Pallas kernels for 0% -> 5%
where the time goes in v1:
time: 153 us
  waiting for transfers between devices  65.6 us (43%)
  starting transfers between devices  52.2 us (34%)
  Pallas kernels  29.8 us (19%)
  local copies, waits for them, and re-layouts  4.48 us (3%)
    ppermute x7, waiting for transfers between devices, local(): back[b] = lax.ppermute(result[b], AXES, to_owner(*hops[b], -1))  33.8 us
    ppermute x7, starting transfers between devices, local(): inbox.append(lax.ppermute(src, AXES, to_owner(*hops[k], 1)))  33.2 us
    pallas_call x2, Pallas kernels, weigh(): pl.pallas_call(functools.partial(weigh_kernel, sizes, blocks, own, slots,...  24.4 us
    ppermute x8, waiting for transfers between devices, local(): beyond = [lax.ppermute(g, AXES, beside(2)) for g in near_by]  17.7 us
    ppermute x7, waiting for transfers between devices, local(): inbox.append(lax.ppermute(src, AXES, to_owner(*hops[k], 1)))  11.5 us
    ppermute x7, starting transfers between devices, local(): back[b] = lax.ppermute(result[b], AXES, to_owner(*hops[b], -1))  10.3 us
    ppermute x8, starting transfers between devices, local(): beyond = [lax.ppermute(g, AXES, beside(2)) for g in near_by]  8.55 us
    unnamed x14, local copies, waits for them, and re-layouts  4.48 us
  transfers between devices with their start and end apart: 26, of which 13 were waited for; matrix products, arithmetic and copies ran while one was open for 0% of the time, Pallas kernels for 5%

profile of v1, /device:TPU:0, one launch (start us, length us, event | category | flops | bytes accessed | tf_op | source)
XLA Modules:
  0.0 153.2 jit_solution(16931282006098492280)
XLA Ops:
  0.6 1.6 %copy-done = f32[512,1024]{1,0:T(8,128)S(1)} copy-done((f32[512,1024]{1,0:T(8,128)S(1)}, f32[512,1024]{1,0:T(8,128)}, u32[]{:S(2)}) %copy-start) | copy-done | bytes 2097176
  2.2 0.7 copy-done.1
  2.9 1.5 pack.1
  4.4 3.0 %collective-permute-start = (bf16[128,1024]{1,0:T(8,128)(2,1)S(1)}, bf16[128,1024]{1,0:T(8,128)(2,1)S(1)}, u32[]{:S(2)}, u32[]{:S(2)}) collective-permute-start(bf16[128,1024]{1,0:T(8,128)(2,1)S(1)} %get-tuple-element.27), channel_id=1, source_target_pairs={{0,16},{1,17},{2,18},{3,19},{4,20},{5,21},{6,22},{7,23},{8,24},{9,... | collective-permute-start | bytes 786440 | tf_op jit(solution)/shard_map/ppermute | solution.py:178
  7.5 1.6 %collective-permute-start.1 = (bf16[128,1024]{1,0:T(8,128)(2,1)S(1)}, bf16[128,1024]{1,0:T(8,128)(2,1)S(1)}, u32[]{:S(2)}, u32[]{:S(2)}) collective-permute-start(bf16[128,1024]{1,0:T(8,128)(2,1)S(1)} %get-tuple-element.28), channel_id=1, source_target_pairs={{0,1},{1,2},{2,3},{3,0},{4,5},{5,6},{6,7},{7,4},{8,9},{9,10},{10,1... | collective-permute-start | bytes 786440 | tf_op jit(solution)/shard_map/ppermute | solution.py:178
  9.0 1.5 collective-permute-start.2
  10.5 3.2 %collective-permute-done.refs_1_ = bf16[128,1024]{1,0:T(8,128)(2,1)S(1)} collective-permute-done((bf16[128,1024]{1,0:T(8,128)(2,1)S(1)}, bf16[128,1024]{1,0:T(8,128)(2,1)S(1)}, u32[]{:S(2)}, u32[]{:S(2)}) %collective-permute-start) | collective-permute-done | bytes 262176 | tf_op jit(solution)/shard_map/ppermute | solution.py:178
  13.8 4.1 %collective-permute-start.3 = (bf16[128,1024]{1,0:T(8,128)(2,1)S(1)}, bf16[128,1024]{1,0:T(8,128)(2,1)S(1)}, u32[]{:S(2)}, u32[]{:S(2)}) collective-permute-start(bf16[128,1024]{1,0:T(8,128)(2,1)S(1)} %get-tuple-element.31), channel_id=1, source_target_pairs={{0,3},{1,0},{2,1},{3,2},{4,7},{5,4},{6,5},{7,6},{8,11},{9,8},{10,9... | collective-permute-start | bytes 786440 | tf_op jit(solution)/shard_map/ppermute | solution.py:178
  17.8 1.5 collective-permute-start.7
  19.4 0.0 collective-permute-done.1.refs_2_
  19.4 1.4 collective-permute-start.4
  20.8 3.0 %collective-permute-done.2.refs_3_ = bf16[128,1024]{1,0:T(8,128)(2,1)S(1)} collective-permute-done((bf16[128,1024]{1,0:T(8,128)(2,1)S(1)}, bf16[128,1024]{1,0:T(8,128)(2,1)S(1)}, u32[]{:S(2)}, u32[]{:S(2)}) %collective-permute-start.2) | collective-permute-done | bytes 262176 | tf_op jit(solution)/shard_map/ppermute | solution.py:178
  23.8 13.6 %collective-permute-start.5 = (bf16[128,1024]{1,0:T(8,128)(2,1)S(1)}, bf16[128,1024]{1,0:T(8,128)(2,1)S(1)}, u32[]{:S(2)}, u32[]{:S(2)}) collective-permute-start(bf16[128,1024]{1,0:T(8,128)(2,1)S(1)} %get-tuple-element.35), channel_id=1, source_target_pairs={{0,2},{1,3},{2,0},{3,1},{4,6},{5,7},{6,4},{7,5},{8,10},{9,11},{10,... | collective-permute-start | bytes 786440 | tf_op jit(solution)/shard_map/ppermute | solution.py:178
  37.4 0.0 collective-permute-start.8
  37.4 0.0 collective-permute-done.3.refs_4_
  37.4 2.0 %collective-permute-start.9 = (bf16[128,1024]{1,0:T(8,128)(2,1)S(1)}, bf16[128,1024]{1,0:T(8,128)(2,1)S(1)}, u32[]{:S(2)}, u32[]{:S(2)}) collective-permute-start(bf16[128,1024]{1,0:T(8,128)(2,1)S(1)} %collective-permute-done.1.refs_2_), channel_id=1, source_target_pairs={{0,8},{1,9},{2,10},{3,11},{4,12},{5,13},{6,14},{7,15},{8,0},{9,1},... | collective-permute-start | bytes 786440 | tf_op jit(solution)/shard_map/ppermute | solution.py:182
  39.4 0.0 collective-permute-done.7.refs_8_
  39.4 0.1 collective-permute-start.10
  39.5 0.0 collective-permute-done.4.refs_5_
  39.5 8.0 %collective-permute-start.6 = (bf16[128,1024]{1,0:T(8,128)(2,1)S(1)}, bf16[128,1024]{1,0:T(8,128)(2,1)S(1)}, u32[]{:S(2)}, u32[]{:S(2)}) collective-permute-start(bf16[128,1024]{1,0:T(8,128)(2,1)S(1)} %get-tuple-element.37), channel_id=1, source_target_pairs={{0,18},{1,19},{2,16},{3,17},{4,22},{5,23},{6,20},{7,21},{8,26},{9,... | collective-permute-start | bytes 786440 | tf_op jit(solution)/shard_map/ppermute | solution.py:178
  47.5 3.5 %collective-permute-done.5.refs_6_ = bf16[128,1024]{1,0:T(8,128)(2,1)S(1)} collective-permute-done((bf16[128,1024]{1,0:T(8,128)(2,1)S(1)}, bf16[128,1024]{1,0:T(8,128)(2,1)S(1)}, u32[]{:S(2)}, u32[]{:S(2)}) %collective-permute-start.5) | collective-permute-done | bytes 262176 | tf_op jit(solution)/shard_map/ppermute | solution.py:178
  51.0 1.4 collective-permute-start.11
  52.3 0.0 collective-permute-done.8.refs_9_
  52.3 0.7 collective-permute-start.12
  53.0 0.1 pad_maximum_fusion
  53.1 0.0 collective-permute-done.9.refs_10_
  53.1 0.1 collective-permute-start.15
  53.2 0.0 collective-permute-done.10.refs_11_
  53.2 1.4 collective-permute-start.13
  54.6 1.7 %collective-permute-done.6.refs_7_ = bf16[128,1024]{1,0:T(8,128)(2,1)S(1)} collective-permute-done((bf16[128,1024]{1,0:T(8,128)(2,1)S(1)}, bf16[128,1024]{1,0:T(8,128)(2,1)S(1)}, u32[]{:S(2)}, u32[]{:S(2)}) %collective-permute-start.6) | collective-permute-done | bytes 262176 | tf_op jit(solution)/shard_map/ppermute | solution.py:178
  56.3 1.5 collective-permute-start.14
  57.8 0.1 pad_maximum_fusion.1
  57.9 2.3 %collective-permute-done.11.refs_12_ = bf16[128,1024]{1,0:T(8,128)(2,1)S(1)} collective-permute-done((bf16[128,1024]{1,0:T(8,128)(2,1)S(1)}, bf16[128,1024]{1,0:T(8,128)(2,1)S(1)}, u32[]{:S(2)}, u32[]{:S(2)}) %collective-permute-start.11) | collective-permute-done | bytes 262176 | tf_op jit(solution)/shard_map/ppermute | solution.py:182
  60.2 0.0 collective-permute-start.16
  60.2 5.6 %collective-permute-done.12.refs_13_ = bf16[128,1024]{1,0:T(8,128)(2,1)S(1)} collective-permute-done((bf16[128,1024]{1,0:T(8,128)(2,1)S(1)}, bf16[128,1024]{1,0:T(8,128)(2,1)S(1)}, u32[]{:S(2)}, u32[]{:S(2)}) %collective-permute-start.12) | collective-permute-done | bytes 262176 | tf_op jit(solution)/shard_map/ppermute | solution.py:182
  65.8 0.1 pad_maximum_fusion.2
  65.9 0.1 collective-permute-start.17
  65.9 5.5 %collective-permute-done.13.refs_14_ = bf16[128,1024]{1,0:T(8,128)(2,1)S(1)} collective-permute-done((bf16[128,1024]{1,0:T(8,128)(2,1)S(1)}, bf16[128,1024]{1,0:T(8,128)(2,1)S(1)}, u32[]{:S(2)}, u32[]{:S(2)}) %collective-permute-start.13) | collective-permute-done | bytes 262176 | tf_op jit(solution)/shard_map/ppermute | solution.py:182
  71.4 4.3 %collective-permute-done.14.refs_15_ = bf16[128,1024]{1,0:T(8,128)(2,1)S(1)} collective-permute-done((bf16[128,1024]{1,0:T(8,128)(2,1)S(1)}, bf16[128,1024]{1,0:T(8,128)(2,1)S(1)}, u32[]{:S(2)}, u32[]{:S(2)}) %collective-permute-start.14) | collective-permute-done | bytes 262176 | tf_op jit(solution)/shard_map/ppermute | solution.py:182
  75.7 0.1 pad_maximum_fusion.3
  75.8 0.1 collective-permute-start.18
  75.9 0.0 collective-permute-done.15.refs_16_
  75.9 0.0 copy-start.2
  75.9 0.0 collective-permute-done.16.refs_17_
  75.9 0.0 collective-permute-done.17.refs_18_
  76.0 2.6 %collective-permute-done.18.refs_19_ = bf16[512,1024]{1,0:T(8,128)(2,1)S(1)} collective-permute-done((bf16[512,1024]{1,0:T(8,128)(2,1)S(1)}, bf16[512,1024]{1,0:T(8,128)(2,1)S(1)}, u32[]{:S(2)}, u32[]{:S(2)}) %collective-permute-start.18) | collective-permute-done | bytes 1048608 | tf_op jit(solution)/shard_map/ppermute | solution.py:186
  78.6 1.0 copy-done.6
  79.5 17.5 %weigh.2 = (bf16[136,1024]{1,0:T(8,128)(2,1)S(1)}, bf16[136,1024]{1,0:T(8,128)(2,1)S(1)}, bf16[136,1024]{1,0:T(8,128)(2,1)S(1)}, bf16[136,1024]{1,0:T(8,128)(2,1...) custom-call(bf16[128,1024]{1,0:T(8,128)(2,1)S(1)} %get-tuple-element.26.refs_0_, ...), custom_call_target="tpu_custom_call" | custom-call | flops 12884901888 | bytes 8388608 | tf_op jit(solution)/shard_map/weigh/pallas_call | solution.py:193
  97.0 2.8 %collective-permute-start.19 = (bf16[136,1024]{1,0:T(8,128)(2,1)S(1)}, bf16[136,1024]{1,0:T(8,128)(2,1)S(1)}, u32[]{:S(2)}, u32[]{:S(2)}) collective-permute-start(bf16[136,1024]{1,0:T(8,128)(2,1)S(1)} %get-tuple-element.39), channel_id=1, source_target_pairs={{0,16},{1,17},{2,18},{3,19},{4,20},{5,21},{6,22},{7,23},{8,24},{9,... | collective-permute-start | bytes 835592 | tf_op jit(solution)/shard_map/ppermute | solution.py:223
  99.8 0.0 collective-permute-start.20
  99.8 1.0 collective-permute-start.21
  100.8 1.1 collective-permute-start.22
  101.9 2.9 %collective-permute-start.23 = (bf16[136,1024]{1,0:T(8,128)(2,1)S(1)}, bf16[136,1024]{1,0:T(8,128)(2,1)S(1)}, u32[]{:S(2)}, u32[]{:S(2)}) collective-permute-start(bf16[136,1024]{1,0:T(8,128)(2,1)S(1)} %get-tuple-element.43), channel_id=1, source_target_pairs={{0,17},{1,18},{2,19},{3,16},{4,21},{5,22},{6,23},{7,20},{8,25},{9,... | collective-permute-start | bytes 835592 | tf_op jit(solution)/shard_map/ppermute | solution.py:223
  104.8 1.2 copy-done.3
  106.0 6.9 %weigh.3 = (bf16[136,1024]{1,0:T(8,128)(2,1)S(1)}, bf16[136,1024]{1,0:T(8,128)(2,1)S(1)}) custom-call(bf16[128,1024]{1,0:T(8,128)(2,1)S(1)} %get-tuple-element.26.refs_0_, bf16[128,1024]{1,0:T(8,128)(2,1)S(1)} %collective-permute-done.refs_1_, bf16[128,1024]{1,0:T(8,128)(2,1)S(1)} %collective-permute-done.1.refs_2_, ...), custom_call_target="tpu_custom_call" | custom-call | flops 4294967296 | bytes 8388608 | tf_op jit(solution)/shard_map/weigh/pallas_call | solution.py:193
  113.0 1.8 %collective-permute-start.24 = (bf16[136,1024]{1,0:T(8,128)(2,1)S(1)}, bf16[136,1024]{1,0:T(8,128)(2,1)S(1)}, u32[]{:S(2)}, u32[]{:S(2)}) collective-permute-start(bf16[136,1024]{1,0:T(8,128)(2,1)S(1)} %get-tuple-element.44), channel_id=1, source_target_pairs={{0,2},{1,3},{2,0},{3,1},{4,6},{5,7},{6,4},{7,5},{8,10},{9,11},{10,... | collective-permute-start | bytes 835592 | tf_op jit(solution)/shard_map/ppermute | solution.py:223
  114.8 0.0 collective-permute-done.20.refs_2_
  114.8 0.6 collective-permute-start.25
  115.5 10.3 %collective-permute-done.21.refs_3_ = bf16[136,1024]{1,0:T(8,128)(2,1)S(1)} collective-permute-done((bf16[136,1024]{1,0:T(8,128)(2,1)S(1)}, bf16[136,1024]{1,0:T(8,128)(2,1)S(1)}, u32[]{:S(2)}, u32[]{:S(2)}) %collective-permute-start.21) | collective-permute-done | bytes 278560 | tf_op jit(solution)/shard_map/ppermute | solution.py:223
  125.7 0.0 collective-permute-done.22.refs_4_
  125.8 0.6 collective-permute-done.23.refs_5_
  126.3 17.3 %collective-permute-done.24.refs_6_ = bf16[136,1024]{1,0:T(8,128)(2,1)S(1)} collective-permute-done((bf16[136,1024]{1,0:T(8,128)(2,1)S(1)}, bf16[136,1024]{1,0:T(8,128)(2,1)S(1)}, u32[]{:S(2)}, u32[]{:S(2)}) %collective-permute-start.24) | collective-permute-done | bytes 278560 | tf_op jit(solution)/shard_map/ppermute | solution.py:223
  143.6 5.7 %collective-permute-done.25.refs_7_ = bf16[136,1024]{1,0:T(8,128)(2,1)S(1)} collective-permute-done((bf16[136,1024]{1,0:T(8,128)(2,1)S(1)}, bf16[136,1024]{1,0:T(8,128)(2,1)S(1)}, u32[]{:S(2)}, u32[]{:S(2)}) %collective-permute-start.25) | collective-permute-done | bytes 278560 | tf_op jit(solution)/shard_map/ppermute | solution.py:223
  149.3 3.9 %unpack.1 = (f32[1,512]{1,0:T(1,128)}, f32[512,1024]{1,0:T(8,128)}) custom-call(s32[1,512]{1,0:T(1,128)S(1)} %get-tuple-element.25.pos_ref, bf16[136,1024]{1,0:T(8,128)(2,1)S(1)} %get-tuple-element.38.refs_0_, bf16[136,1024]{1,0:T(8,128)(2,1)S(1)} %collective-permute-done.19.refs_1_, bf16[136,1024]{1,0:T(8,128)(2,1)S(1)} %collective-permute-done.20.refs_2_, ...), custom_call_target="tpu_custom_call" | custom-call | tf_op jit(solution)/shard_map/unpack/pallas_call | solution.py:224
  (10 shorter events, 0.0 us)
Async XLA Ops:
  0.6 1.6 %copy-start = (f32[512,1024]{1,0:T(8,128)S(1)}, f32[512,1024]{1,0:T(8,128)}, u32[]{:S(2)}) copy-start(f32[512,1024]{1,0:T(8,128)} %emb_ref.1) | copy-start | bytes 6291460
  2.2 0.7 copy-start.1
  4.4 9.3 %collective-permute-start = (bf16[128,1024]{1,0:T(8,128)(2,1)S(1)}, bf16[128,1024]{1,0:T(8,128)(2,1)S(1)}, u32[]{:S(2)}, u32[]{:S(2)}) collective-permute-start(bf16[128,1024]{1,0:T(8,128)(2,1)S(1)} %get-tuple-element.27), channel_id=1, source_target_pairs={{0,16},{1,17},{2,18},{3,19},{4,20},{5,21},{6,22},{7,23},{8,24},{9,... | collective-permute-start | bytes 786440 | tf_op jit(solution)/shard_map/ppermute | solution.py:178
  7.5 11.9 %collective-permute-start.1 = (bf16[128,1024]{1,0:T(8,128)(2,1)S(1)}, bf16[128,1024]{1,0:T(8,128)(2,1)S(1)}, u32[]{:S(2)}, u32[]{:S(2)}) collective-permute-start(bf16[128,1024]{1,0:T(8,128)(2,1)S(1)} %get-tuple-element.28), channel_id=1, source_target_pairs={{0,1},{1,2},{2,3},{3,0},{4,5},{5,6},{6,7},{7,4},{8,9},{9,10},{10,1... | collective-permute-start | bytes 786440 | tf_op jit(solution)/shard_map/ppermute | solution.py:178
  9.0 14.8 %collective-permute-start.2 = (bf16[128,1024]{1,0:T(8,128)(2,1)S(1)}, bf16[128,1024]{1,0:T(8,128)(2,1)S(1)}, u32[]{:S(2)}, u32[]{:S(2)}) collective-permute-start(bf16[128,1024]{1,0:T(8,128)(2,1)S(1)} %get-tuple-element.29), channel_id=1, source_target_pairs={{0,17},{1,18},{2,19},{3,16},{4,21},{5,22},{6,23},{7,20},{8,25},{9,... | collective-permute-start | bytes 786440 | tf_op jit(solution)/shard_map/ppermute | solution.py:178
  13.8 23.6 %collective-permute-start.3 = (bf16[128,1024]{1,0:T(8,128)(2,1)S(1)}, bf16[128,1024]{1,0:T(8,128)(2,1)S(1)}, u32[]{:S(2)}, u32[]{:S(2)}) collective-permute-start(bf16[128,1024]{1,0:T(8,128)(2,1)S(1)} %get-tuple-element.31), channel_id=1, source_target_pairs={{0,3},{1,0},{2,1},{3,2},{4,7},{5,4},{6,5},{7,6},{8,11},{9,8},{10,9... | collective-permute-start | bytes 786440 | tf_op jit(solution)/shard_map/ppermute | solution.py:178
  17.8 21.6 %collective-permute-start.7 = (bf16[128,1024]{1,0:T(8,128)(2,1)S(1)}, bf16[128,1024]{1,0:T(8,128)(2,1)S(1)}, u32[]{:S(2)}, u32[]{:S(2)}) collective-permute-start(bf16[128,1024]{1,0:T(8,128)(2,1)S(1)} %get-tuple-element.26.refs_0_), channel_id=1, source_target_pairs={{0,8},{1,9},{2,10},{3,11},{4,12},{5,13},{6,14},{7,15},{8,0},{9,1},... | collective-permute-start | bytes 786440 | tf_op jit(solution)/shard_map/ppermute | solution.py:182
  19.4 20.1 %collective-permute-start.4 = (bf16[128,1024]{1,0:T(8,128)(2,1)S(1)}, bf16[128,1024]{1,0:T(8,128)(2,1)S(1)}, u32[]{:S(2)}, u32[]{:S(2)}) collective-permute-start(bf16[128,1024]{1,0:T(8,128)(2,1)S(1)} %get-tuple-element.33), channel_id=1, source_target_pairs={{0,19},{1,16},{2,17},{3,18},{4,23},{5,20},{6,21},{7,22},{8,27},{9,... | collective-permute-start | bytes 786440 | tf_op jit(solution)/shard_map/ppermute | solution.py:178
  23.8 27.2 %collective-permute-start.5 = (bf16[128,1024]{1,0:T(8,128)(2,1)S(1)}, bf16[128,1024]{1,0:T(8,128)(2,1)S(1)}, u32[]{:S(2)}, u32[]{:S(2)}) collective-permute-start(bf16[128,1024]{1,0:T(8,128)(2,1)S(1)} %get-tuple-element.35), channel_id=1, source_target_pairs={{0,2},{1,3},{2,0},{3,1},{4,6},{5,7},{6,4},{7,5},{8,10},{9,11},{10,... | collective-permute-start | bytes 786440 | tf_op jit(solution)/shard_map/ppermute | solution.py:178
  37.4 15.0 %collective-permute-start.8 = (bf16[128,1024]{1,0:T(8,128)(2,1)S(1)}, bf16[128,1024]{1,0:T(8,128)(2,1)S(1)}, u32[]{:S(2)}, u32[]{:S(2)}) collective-permute-start(bf16[128,1024]{1,0:T(8,128)(2,1)S(1)} %collective-permute-done.refs_1_), channel_id=1, source_target_pairs={{0,8},{1,9},{2,10},{3,11},{4,12},{5,13},{6,14},{7,15},{8,0},{9,1},... | collective-permute-start | bytes 786440 | tf_op jit(solution)/shard_map/ppermute | solution.py:182
  37.4 15.7 %collective-permute-start.9 = (bf16[128,1024]{1,0:T(8,128)(2,1)S(1)}, bf16[128,1024]{1,0:T(8,128)(2,1)S(1)}, u32[]{:S(2)}, u32[]{:S(2)}) collective-permute-start(bf16[128,1024]{1,0:T(8,128)(2,1)S(1)} %collective-permute-done.1.refs_2_), channel_id=1, source_target_pairs={{0,8},{1,9},{2,10},{3,11},{4,12},{5,13},{6,14},{7,15},{8,0},{9,1},... | collective-permute-start | bytes 786440 | tf_op jit(solution)/shard_map/ppermute | solution.py:182
  39.4 13.7 %collective-permute-start.10 = (bf16[128,1024]{1,0:T(8,128)(2,1)S(1)}, bf16[128,1024]{1,0:T(8,128)(2,1)S(1)}, u32[]{:S(2)}, u32[]{:S(2)}) collective-permute-start(bf16[128,1024]{1,0:T(8,128)(2,1)S(1)} %collective-permute-done.2.refs_3_), channel_id=1, source_target_pairs={{0,8},{1,9},{2,10},{3,11},{4,12},{5,13},{6,14},{7,15},{8,0},{9,1},... | collective-permute-start | bytes 786440 | tf_op jit(solution)/shard_map/ppermute | solution.py:182
  39.5 16.8 %collective-permute-start.6 = (bf16[128,1024]{1,0:T(8,128)(2,1)S(1)}, bf16[128,1024]{1,0:T(8,128)(2,1)S(1)}, u32[]{:S(2)}, u32[]{:S(2)}) collective-permute-start(bf16[128,1024]{1,0:T(8,128)(2,1)S(1)} %get-tuple-element.37), channel_id=1, source_target_pairs={{0,18},{1,19},{2,16},{3,17},{4,22},{5,23},{6,20},{7,21},{8,26},{9,... | collective-permute-start | bytes 786440 | tf_op jit(solution)/shard_map/ppermute | solution.py:178
  51.0 9.2 %collective-permute-start.11 = (bf16[128,1024]{1,0:T(8,128)(2,1)S(1)}, bf16[128,1024]{1,0:T(8,128)(2,1)S(1)}, u32[]{:S(2)}, u32[]{:S(2)}) collective-permute-start(bf16[128,1024]{1,0:T(8,128)(2,1)S(1)} %collective-permute-done.3.refs_4_), channel_id=1, source_target_pairs={{0,8},{1,9},{2,10},{3,11},{4,12},{5,13},{6,14},{7,15},{8,0},{9,1},... | collective-permute-start | bytes 786440 | tf_op jit(solution)/shard_map/ppermute | solution.py:182
  52.3 13.4 %collective-permute-start.12 = (bf16[128,1024]{1,0:T(8,128)(2,1)S(1)}, bf16[128,1024]{1,0:T(8,128)(2,1)S(1)}, u32[]{:S(2)}, u32[]{:S(2)}) collective-permute-start(bf16[128,1024]{1,0:T(8,128)(2,1)S(1)} %collective-permute-done.4.refs_5_), channel_id=1, source_target_pairs={{0,8},{1,9},{2,10},{3,11},{4,12},{5,13},{6,14},{7,15},{8,0},{9,1},... | collective-permute-start | bytes 786440 | tf_op jit(solution)/shard_map/ppermute | solution.py:182
  53.1 22.8 %collective-permute-start.15 = (bf16[512,1024]{1,0:T(8,128)(2,1)S(1)}, bf16[512,1024]{1,0:T(8,128)(2,1)S(1)}, u32[]{:S(2)}, u32[]{:S(2)}) collective-permute-start(bf16[512,1024]{1,0:T(8,128)(2,1)S(1)} %pad_maximum_fusion), channel_id=1, source_target_pairs={{0,4},{1,5},{2,6},{3,7},{4,0},{5,1},{6,2},{7,3},{8,12},{9,13},{10,... | collective-permute-start | bytes 3145736 | tf_op jit(solution)/shard_map/ppermute | solution.py:186
  53.2 18.2 %collective-permute-start.13 = (bf16[128,1024]{1,0:T(8,128)(2,1)S(1)}, bf16[128,1024]{1,0:T(8,128)(2,1)S(1)}, u32[]{:S(2)}, u32[]{:S(2)}) collective-permute-start(bf16[128,1024]{1,0:T(8,128)(2,1)S(1)} %collective-permute-done.5.refs_6_), channel_id=1, source_target_pairs={{0,8},{1,9},{2,10},{3,11},{4,12},{5,13},{6,14},{7,15},{8,0},{9,1},... | collective-permute-start | bytes 786440 | tf_op jit(solution)/shard_map/ppermute | solution.py:182
  56.3 19.4 %collective-permute-start.14 = (bf16[128,1024]{1,0:T(8,128)(2,1)S(1)}, bf16[128,1024]{1,0:T(8,128)(2,1)S(1)}, u32[]{:S(2)}, u32[]{:S(2)}) collective-permute-start(bf16[128,1024]{1,0:T(8,128)(2,1)S(1)} %collective-permute-done.6.refs_7_), channel_id=1, source_target_pairs={{0,8},{1,9},{2,10},{3,11},{4,12},{5,13},{6,14},{7,15},{8,0},{9,1},... | collective-permute-start | bytes 786440 | tf_op jit(solution)/shard_map/ppermute | solution.py:182
  60.2 15.7 %collective-permute-start.16 = (bf16[512,1024]{1,0:T(8,128)(2,1)S(1)}, bf16[512,1024]{1,0:T(8,128)(2,1)S(1)}, u32[]{:S(2)}, u32[]{:S(2)}) collective-permute-start(bf16[512,1024]{1,0:T(8,128)(2,1)S(1)} %pad_maximum_fusion.1), channel_id=1, source_target_pairs={{0,4},{1,5},{2,6},{3,7},{4,0},{5,1},{6,2},{7,3},{8,12},{9,13},{10,... | collective-permute-start | bytes 3145736 | tf_op jit(solution)/shard_map/ppermute | solution.py:186
  65.9 10.1 %collective-permute-start.17 = (bf16[512,1024]{1,0:T(8,128)(2,1)S(1)}, bf16[512,1024]{1,0:T(8,128)(2,1)S(1)}, u32[]{:S(2)}, u32[]{:S(2)}) collective-permute-start(bf16[512,1024]{1,0:T(8,128)(2,1)S(1)} %pad_maximum_fusion.2), channel_id=1, source_target_pairs={{0,4},{1,5},{2,6},{3,7},{4,0},{5,1},{6,2},{7,3},{8,12},{9,13},{10,... | collective-permute-start | bytes 3145736 | tf_op jit(solution)/shard_map/ppermute | solution.py:186
  75.8 2.7 %collective-permute-start.18 = (bf16[512,1024]{1,0:T(8,128)(2,1)S(1)}, bf16[512,1024]{1,0:T(8,128)(2,1)S(1)}, u32[]{:S(2)}, u32[]{:S(2)}) collective-permute-start(bf16[512,1024]{1,0:T(8,128)(2,1)S(1)} %pad_maximum_fusion.3), channel_id=1, source_target_pairs={{0,4},{1,5},{2,6},{3,7},{4,0},{5,1},{6,2},{7,3},{8,12},{9,13},{10,... | collective-permute-start | bytes 3145736 | tf_op jit(solution)/shard_map/ppermute | solution.py:186
  75.9 2.6 %copy-start.2 = (bf16[512,1024]{1,0:T(8,128)(2,1)}, bf16[512,1024]{1,0:T(8,128)(2,1)S(1)}, u32[]{:S(2)}) copy-start(bf16[512,1024]{1,0:T(8,128)(2,1)S(1)} %collective-permute-done.15.refs_16_) | copy-start | bytes 3145732
  75.9 2.6 %copy-start.4 = (bf16[512,1024]{1,0:T(8,128)(2,1)}, bf16[512,1024]{1,0:T(8,128)(2,1)S(1)}, u32[]{:S(2)}) copy-start(bf16[512,1024]{1,0:T(8,128)(2,1)S(1)} %collective-permute-done.16.refs_17_) | copy-start | bytes 3145732
  75.9 2.6 %copy-start.5 = (bf16[512,1024]{1,0:T(8,128)(2,1)}, bf16[512,1024]{1,0:T(8,128)(2,1)S(1)}, u32[]{:S(2)}) copy-start(bf16[512,1024]{1,0:T(8,128)(2,1)S(1)} %collective-permute-done.17.refs_18_) | copy-start | bytes 3145732
  78.5 1.0 copy-start.6
  97.0 15.9 %collective-permute-start.19 = (bf16[136,1024]{1,0:T(8,128)(2,1)S(1)}, bf16[136,1024]{1,0:T(8,128)(2,1)S(1)}, u32[]{:S(2)}, u32[]{:S(2)}) collective-permute-start(bf16[136,1024]{1,0:T(8,128)(2,1)S(1)} %get-tuple-element.39), channel_id=1, source_target_pairs={{0,16},{1,17},{2,18},{3,19},{4,20},{5,21},{6,22},{7,23},{8,24},{9,... | collective-permute-start | bytes 835592 | tf_op jit(solution)/shard_map/ppermute | solution.py:223
  99.8 15.0 %collective-permute-start.20 = (bf16[136,1024]{1,0:T(8,128)(2,1)S(1)}, bf16[136,1024]{1,0:T(8,128)(2,1)S(1)}, u32[]{:S(2)}, u32[]{:S(2)}) collective-permute-start(bf16[136,1024]{1,0:T(8,128)(2,1)S(1)} %get-tuple-element.40), channel_id=1, source_target_pairs={{0,3},{1,0},{2,1},{3,2},{4,7},{5,4},{6,5},{7,6},{8,11},{9,8},{10,9... | collective-permute-start | bytes 835592 | tf_op jit(solution)/shard_map/ppermute | solution.py:223
  99.8 25.9 %collective-permute-start.21 = (bf16[136,1024]{1,0:T(8,128)(2,1)S(1)}, bf16[136,1024]{1,0:T(8,128)(2,1)S(1)}, u32[]{:S(2)}, u32[]{:S(2)}) collective-permute-start(bf16[136,1024]{1,0:T(8,128)(2,1)S(1)} %get-tuple-element.41), channel_id=1, source_target_pairs={{0,19},{1,16},{2,17},{3,18},{4,23},{5,20},{6,21},{7,22},{8,27},{9,... | collective-permute-start | bytes 835592 | tf_op jit(solution)/shard_map/ppermute | solution.py:223
  100.8 25.0 %collective-permute-start.22 = (bf16[136,1024]{1,0:T(8,128)(2,1)S(1)}, bf16[136,1024]{1,0:T(8,128)(2,1)S(1)}, u32[]{:S(2)}, u32[]{:S(2)}) collective-permute-start(bf16[136,1024]{1,0:T(8,128)(2,1)S(1)} %get-tuple-element.42), channel_id=1, source_target_pairs={{0,1},{1,2},{2,3},{3,0},{4,5},{5,6},{6,7},{7,4},{8,9},{9,10},{10,1... | collective-permute-start | bytes 835592 | tf_op jit(solution)/shard_map/ppermute | solution.py:223
  101.9 24.5 %collective-permute-start.23 = (bf16[136,1024]{1,0:T(8,128)(2,1)S(1)}, bf16[136,1024]{1,0:T(8,128)(2,1)S(1)}, u32[]{:S(2)}, u32[]{:S(2)}) collective-permute-start(bf16[136,1024]{1,0:T(8,128)(2,1)S(1)} %get-tuple-element.43), channel_id=1, source_target_pairs={{0,17},{1,18},{2,19},{3,16},{4,21},{5,22},{6,23},{7,20},{8,25},{9,... | collective-permute-start | bytes 835592 | tf_op jit(solution)/shard_map/ppermute | solution.py:223
  104.8 1.2 copy-start.3
  113.0 30.7 %collective-permute-start.24 = (bf16[136,1024]{1,0:T(8,128)(2,1)S(1)}, bf16[136,1024]{1,0:T(8,128)(2,1)S(1)}, u32[]{:S(2)}, u32[]{:S(2)}) collective-permute-start(bf16[136,1024]{1,0:T(8,128)(2,1)S(1)} %get-tuple-element.44), channel_id=1, source_target_pairs={{0,2},{1,3},{2,0},{3,1},{4,6},{5,7},{6,4},{7,5},{8,10},{9,11},{10,... | collective-permute-start | bytes 835592 | tf_op jit(solution)/shard_map/ppermute | solution.py:223
  114.8 34.5 %collective-permute-start.25 = (bf16[136,1024]{1,0:T(8,128)(2,1)S(1)}, bf16[136,1024]{1,0:T(8,128)(2,1)S(1)}, u32[]{:S(2)}, u32[]{:S(2)}) collective-permute-start(bf16[136,1024]{1,0:T(8,128)(2,1)S(1)} %get-tuple-element.45), channel_id=1, source_target_pairs={{0,18},{1,19},{2,16},{3,17},{4,22},{5,23},{6,20},{7,21},{8,26},{9,... | collective-permute-start | bytes 835592 | tf_op jit(solution)/shard_map/ppermute | solution.py:223

commit v2 on v1

v2 whole, which is shorter than its diff:
```python
import functools

import jax
import jax.numpy as jnp
from jax import lax
from jax.experimental import pallas as pl
from jax.experimental.pallas import tpu as pltpu
from jax.sharding import PartitionSpec as P

AXES = ("shard", "grp")
EXTRA = 8
MIB = 1 << 20


def hop_order(ng):
    return sorted(range(ng), key=lambda d: (min(d, ng - d), d))


def pack_kernel(hi_n, ng, slots, emb_ref, ids_ref, pos_ref, *out_refs):
    n, width = emb_ref.shape
    nb = hi_n * ng
    emb = emb_ref[...]
    scale = lax.rsqrt(jnp.mean(emb * emb, axis=1, keepdims=True) + 1e-06)
    units = (emb * scale).astype(jnp.bfloat16)
    hi = lax.axis_index("shard") // ng
    z = lax.axis_index("grp")
    ids = ids_ref[...]
    blk = jnp.zeros((1, n), jnp.int32)
    for k, dz in enumerate(hop_order(ng)):
        for dh in range(hi_n):
            owner = lax.rem(hi + dh, hi_n) * ng + lax.rem(z + dz, ng)
            blk = jnp.where(ids == owner, k * hi_n + dh, blk)
    onehot = lax.broadcasted_iota(jnp.int32, (nb, n), 0) == blk
    upto = lax.broadcasted_iota(jnp.int32, (n, n), 0) <= lax.broadcasted_iota(jnp.int32, (n, n), 1)
    cum = jnp.dot(
        onehot.astype(jnp.bfloat16), upto.astype(jnp.bfloat16), preferred_element_type=jnp.float32
    )
    rank = jnp.sum(jnp.where(onehot, cum, 0.0), axis=0, keepdims=True).astype(jnp.int32) - 1
    pos = blk * slots + rank
    pos_ref[...] = pos
    mark = float(2.0 * width**0.5)
    for k in range(nb):
        pick = lax.broadcasted_iota(jnp.int32, (slots, n), 0) + k * slots == pos
        rows = jnp.dot(pick.astype(jnp.bfloat16), units, preferred_element_type=jnp.float32)
        used = cum[k : k + 1, n - 1 : n].astype(jnp.int32)
        empty = lax.broadcasted_iota(jnp.int32, (slots, width), 0) >= used
        first = lax.broadcasted_iota(jnp.int32, (slots, width), 1) == 0
        out_refs[k][...] = jnp.where(empty & first, mark, rows).astype(jnp.bfloat16)


def weigh_kernel(layout, row_stage, slots, nblocks, carried, last, *refs):
    sizes = [n for _, ns in layout for n in ns]
    ncol, nunit = len(sizes), len(row_stage)
    refs = list(refs)
    row_in, cols = refs[:nunit], refs[nunit : nunit + ncol]
    del refs[: nunit + ncol]
    if carried:
        pull_in, count_in = refs[:2]
        del refs[:2]
    if last:
        outs = refs[:nblocks]
        del refs[:nblocks]
        units, rows, pull, count, sems = refs
    else:
        pull, count, units, rows, sems = refs
    total, width = units.shape
    unit = row_in[0].shape[0]
    nrows = nunit * unit
    starts = [sum(sizes[:i]) for i in range(ncol)]
    copies = [
        pltpu.make_async_copy(row_in[i], rows.at[pl.ds(i * unit, unit)], sems.at[i])
        for i in range(nunit)
    ]
    copies += [
        pltpu.make_async_copy(cols[i], units.at[pl.ds(starts[i], sizes[i])], sems.at[nunit + i])
        for i in range(ncol)
    ]
    for c in copies:
        c.start()
    limit = 1.5 * width**0.5
    probe = lax.broadcasted_iota(jnp.int32, (16, width), 1) == 0
    rows[pl.ds(nrows, 16), :] = probe.astype(jnp.bfloat16)
    for c in copies[:nunit]:
        c.wait()
    waited = 0
    at = 0
    for stage, ns in layout:
        size = sum(ns)
        chunk = min(size, 4 * unit)
        for half in range(size // chunk):
            while waited < ncol and starts[waited] < at + chunk:
                copies[nunit + waited].wait()
                waited += 1
            part = units[pl.ds(at, chunk), :]
            scores = lax.dot_general(
                rows[...], part, (((1,), (1,)), ((), ())), preferred_element_type=jnp.float32
            )
            keep = jnp.broadcast_to(scores[nrows : nrows + 1, :] < limit, (nrows, chunk))
            if half == 0 and any(s == stage for s, _ in row_stage):
                col = lax.broadcasted_iota(jnp.int32, (unit, chunk), 1)
                row = lax.broadcasted_iota(jnp.int32, (unit, chunk), 0)
                off = [
                    col != (row + h * unit if s == stage else -1) for s, h in row_stage
                ]
                keep = keep & jnp.concatenate(off, axis=0)
            weight = jnp.where(keep, jnp.exp(scores[:nrows] * (64.0 / width)), 0.0)
            add_count = jnp.broadcast_to(jnp.sum(weight, axis=1, keepdims=True), count.shape)
            add_pull = jnp.dot(
                weight.astype(jnp.bfloat16), part, preferred_element_type=jnp.float32
            )
            if at:
                count[...] += add_count
                pull[...] += add_pull
            elif carried:
                count[...] = count_in[...] + add_count
                pull[...] = pull_in[...] + add_pull
            else:
                count[...] = add_count
                pull[...] = add_pull
            at += chunk
    if not last:
        return
    valid = rows[pl.ds(0, nrows), 0:128].astype(jnp.float32)[:, 0:1] < limit
    for i in range(nblocks):
        at = i * slots
        ok = valid[at : at + slots]
        cnt = count[pl.ds(at, slots), :]
        near = pull[pl.ds(at, slots), :] / (1.0 + cnt[:, 0:1])
        outs[i][pl.ds(0, slots), :] = jnp.where(ok, near, 0.0).astype(jnp.bfloat16)
        dup = jnp.where(ok, jnp.log1p(cnt), 0.0)
        if slots < 128:
            dup = jnp.concatenate([dup, jnp.zeros((128 - slots, 128), jnp.float32)], axis=0)
        dup = dup.T[0:EXTRA]
        high = dup.astype(jnp.bfloat16).astype(jnp.float32)
        line = lax.broadcasted_iota(jnp.int32, (EXTRA, 128), 0)
        two = jnp.where(line == 0, high, jnp.where(line == 1, dup - high, 0.0))
        outs[i][pl.ds(slots, EXTRA), pl.ds(0, 128)] = two.astype(jnp.bfloat16)


def unpack_kernel(slots, which, carried, pos_ref, *refs):
    refs = list(refs)
    dup_ref, near_ref = refs[-2:]
    blocks = refs[: len(which)]
    n = pos_ref.shape[1]
    pos = pos_ref[...]
    dup = jnp.zeros((EXTRA, n), jnp.float32)
    for i, (k, ref) in enumerate(zip(which, blocks)):
        pick = lax.broadcasted_iota(jnp.int32, (slots, n), 0) + k * slots == pos
        pick = pick.astype(jnp.bfloat16)
        near = lax.dot_general(
            pick,
            ref[pl.ds(0, slots), :],
            (((0,), (0,)), ((), ())),
            preferred_element_type=jnp.float32,
        )
        if i:
            near_ref[...] += near
        elif carried:
            near_ref[...] = refs[len(which) + 1][...] + near
        else:
            near_ref[...] = near
        two = ref[pl.ds(slots, EXTRA), pl.ds(0, 128)][:, :slots]
        dup = dup + jnp.dot(two, pick, preferred_element_type=jnp.float32)
    total = dup[0:1] + dup[1:2]
    dup_ref[...] = refs[len(which)][...] + total if carried else total


def after(value, *deps):
    return lax.optimization_barrier((value,) + deps)[0]


def local(embeddings, cluster):
    n, width = embeddings.shape
    ns, ng = lax.axis_size("shard"), lax.axis_size("grp")
    hi_n = ns // ng
    nb = ns
    slots = 2 * n // ns

    def moved(f):
        return [(s * ng + z, f(s, z)) for s in range(ns) for z in range(ng)]

    def to_owner(dh, dz, sign):
        return moved(
            lambda s, z: ((s // ng + sign * dh) % hi_n * ng + s % ng) * ng + (z + sign * dz) % ng
        )

    def beside(bit):
        return moved(lambda s, z: (s ^ bit) * ng + z)

    hops = [(dh, dz) for dz in hop_order(ng) for dh in range(hi_n)]
    vmem = pl.BlockSpec(memory_space=pltpu.VMEM)
    anyspace = pl.BlockSpec(memory_space=pl.ANY)
    ids = cluster.reshape(1, n)
    pos, *outbox = pl.pallas_call(
        functools.partial(pack_kernel, hi_n, ng, slots),
        out_shape=[jax.ShapeDtypeStruct((1, n), jnp.int32)]
        + [jax.ShapeDtypeStruct((slots, width), jnp.bfloat16)] * nb,
        in_specs=[vmem, vmem],
        out_specs=[vmem] * (nb + 1),
        compiler_params=pltpu.CompilerParams(vmem_limit_bytes=40 * MIB),
        name="pack",
    )(embeddings, ids)

    per = hi_n // 2
    unit = per * slots
    nstage = ng
    inbox = [None] * nb
    own, side, other = {}, {}, {}

    def send(stage, half, *deps):
        got = []
        for k in range(stage * hi_n + half * per, stage * hi_n + (half + 1) * per):
            if k:
                src = after(outbox[k], *deps) if deps else outbox[k]
                inbox[k] = lax.ppermute(src, AXES, to_owner(*hops[k], 1))
            else:
                inbox[k] = outbox[k]
            got.append(inbox[k])
        own[stage, half] = got[0] if per == 1 else jnp.concatenate(got, axis=0)

    def across(stage, half, *deps):
        src = own[stage, half]
        side[stage, half] = lax.ppermute(after(src, *deps) if deps else src, AXES, beside(2))

    def swap(*units):
        both = jnp.concatenate([own[u] for u in units] + [side[u] for u in units], axis=0)
        got = lax.ppermute(both, AXES, beside(1))
        other.setdefault(units[0][0], []).append(got)

    def weigh(row_units, stages, carry=(), last=False, deps=()):
        nblocks = len(row_units) * per
        nrows = len(row_units) * unit
        cols = [(g, [own[g, 0], own[g, 1], side[g, 0], side[g, 1]]) for g in stages]
        cols += [(None, [c]) for g in stages for c in other.get(g, [])]
        layout = [(g, [c.shape[0] for c in cs]) for g, cs in cols]
        total = sum(sum(ns) for _, ns in layout)
        cols = [c for _, cs in cols for c in cs]
        ins = [own[u] for u in row_units] + cols + list(carry)
        if deps:
            ins[0] = after(ins[0], *deps)
        sums = [(nrows, width), (nrows, 128)]
        if last:
            out_shape = [jax.ShapeDtypeStruct((slots + EXTRA, width), jnp.bfloat16)] * nblocks
        else:
            out_shape = [jax.ShapeDtypeStruct(t, jnp.float32) for t in sums]
        return pl.pallas_call(
            functools.partial(
                weigh_kernel, layout, row_units, slots, nblocks, bool(carry), last
            ),
            out_shape=out_shape,
            in_specs=[anyspace] * (len(ins) - len(carry)) + [vmem] * len(carry),
            out_specs=[vmem] * len(out_shape),
            input_output_aliases=(
                {len(ins) - 2: 0, len(ins) - 1: 1} if carry and not last else {}
            ),
            scratch_shapes=[
                pltpu.VMEM((total, width), jnp.bfloat16),
                pltpu.VMEM((nrows + 16, width), jnp.bfloat16),
            ]
            + ([pltpu.VMEM(t, jnp.float32) for t in sums] if last else [])
            + [pltpu.SemaphoreType.DMA((len(ins),))],
            compiler_params=pltpu.CompilerParams(vmem_limit_bytes=48 * MIB),
            cost_estimate=pl.CostEstimate(
                flops=4 * nrows * total * width if last else 0,
                bytes_accessed=2 * total * width if last else 0,
                transcendentals=nrows * total if last else 0,
            ),
            name="weigh",
        )(*ins)

    send(1, 0)
    send(1, 1)
    send(0, 0)
    across(0, 0)
    send(0, 1)
    across(0, 1, side[0, 0])
    send(2, 0, own[0, 1])
    across(1, 0, own[1, 0])
    send(2, 1, own[1, 0])
    across(1, 1, side[0, 1])
    send(3, 0, own[1, 1])
    swap((0, 0), (0, 1))
    across(2, 0, side[1, 0])
    send(3, 1, own[2, 0])
    across(2, 1, side[1, 1])
    swap((1, 0), (1, 1))
    across(3, 0, side[2, 0])
    across(3, 1, side[2, 1])
    swap((2, 0), (2, 1))
    swap((3, 0))
    swap((3, 1))
    parts = [[(1, 0), (1, 1)], [(2, 0), (2, 1)], [(3, 0), (3, 1), (0, 1), (0, 0)]]
    result = [None] * nb
    order, deps = [], ()
    for part in parts:
        outs = weigh(part, list(range(nstage)), (), True, deps)
        deps = outs[:1]
        blocks = [g * hi_n + h * per + i for g, h in part for i in range(per)]
        for k, r in zip(blocks, outs):
            result[k] = r
        order += blocks
    back = [result[0]] + [None] * (nb - 1)
    for b in order:
        if b:
            back[b] = lax.ppermute(result[b], AXES, to_owner(*hops[b], -1))

    def unpack(which, carry=()):
        return pl.pallas_call(
            functools.partial(unpack_kernel, slots, which, bool(carry)),
            out_shape=[
                jax.ShapeDtypeStruct((1, n), jnp.float32),
                jax.ShapeDtypeStruct((n, width), jnp.float32),
            ],
            in_specs=[vmem] * (1 + len(which) + len(carry)),
            out_specs=[vmem, vmem],
            compiler_params=pltpu.CompilerParams(vmem_limit_bytes=40 * MIB),
            name="unpack",
        )(pos, *[back[k] for k in which], *carry)

    late = [b for g, h in parts[2][:3] for b in range(g * hi_n + h * per, g * hi_n + (h + 1) * per)]
    dup, near = unpack(late, unpack([b for b in range(nb) if b not in late]))
    return dup.reshape(n), near


def solution(mesh):
    return jax.shard_map(
        local,
        mesh=mesh,
        in_specs=(P(("shard", "grp"), None), P(("shard", "grp"), None)),
        out_specs=(P(("shard", "grp")), P(("shard", "grp"), None)),
        check_vma=False,
    )
```

time: 153 us -> 135 us (0.88)
  waiting for transfers between devices: 65.6 us -> 47.8 us
  Pallas kernels: 29.8 us -> 34.3 us
  starting transfers between devices: 52.2 us -> 47.8 us
    ppermute x7, waiting for transfers between devices: 33.8 us -> 20.4 us  [local(): back[b] = lax.ppermute(result[b], AXES, to_owner(*hops[b], -1))]
    ppermute x19 -> x20, starting transfers between devices: 42 us -> 36.4 us  [the longest x7 28.2 us: send(): inbox[k] = lax.ppermute(src, AXES, to_owner(*hops[k], 1))]
    pallas_call x3 -> x5, Pallas kernels: 28.3 us -> 32.8 us  [the longest x3 28.8 us: weigh(): pl.pallas_call(functools.partial(weigh_kernel, layout, row_units, slots,...]
    ppermute x19 -> x20, waiting for transfers between devices: 31.8 us -> 27.4 us  [the longest x8 16.8 us: across(): lax.ppermute(after(src, *deps) if deps else src, AXES, beside(2))]
    unnamed x14 -> x12, local copies, waits for them, and re-layouts: 4.48 us -> 4.26 us
  transfers between devices with their start and end apart: 26 -> 27, of which waited for: 13 -> 11; matrix products, arithmetic and copies ran while one was open for 0% -> 0% of each run, Pallas kernels for 5% -> 17%
where the time goes in v2:
time: 135 us
  starting transfers between devices  47.8 us (35%)
  waiting for transfers between devices  47.8 us (35%)
  Pallas kernels  34.3 us (25%)
  local copies, waits for them, and re-layouts  4.26 us (3%)
    pallas_call x3, Pallas kernels, weigh(): pl.pallas_call(functools.partial(weigh_kernel, layout, row_units, slots,...  28.8 us
    ppermute x7, starting transfers between devices, send(): inbox[k] = lax.ppermute(src, AXES, to_owner(*hops[k], 1))  28.2 us
    ppermute x7, waiting for transfers between devices, local(): back[b] = lax.ppermute(result[b], AXES, to_owner(*hops[b], -1))  20.4 us
    ppermute x8, waiting for transfers between devices, across(): lax.ppermute(after(src, *deps) if deps else src, AXES, beside(2))  16.8 us
    ppermute x7, starting transfers between devices, local(): back[b] = lax.ppermute(result[b], AXES, to_owner(*hops[b], -1))  11.4 us
    ppermute x7, waiting for transfers between devices, send(): inbox[k] = lax.ppermute(src, AXES, to_owner(*hops[k], 1))  8.76 us
    ppermute x8, starting transfers between devices, across(): lax.ppermute(after(src, *deps) if deps else src, AXES, beside(2))  7.96 us
    unnamed x12, local copies, waits for them, and re-layouts  4.26 us
  transfers between devices with their start and end apart: 27, of which 11 were waited for; matrix products, arithmetic and copies ran while one was open for 0% of the time, Pallas kernels for 17%

profile of v2, /device:TPU:0, one launch (start us, length us, event | category | flops | bytes accessed | tf_op | source)
XLA Modules:
  0.0 135.3 jit_solution(17774214316381469345)
XLA Ops:
  0.6 1.6 %copy-done = f32[512,1024]{1,0:T(8,128)S(1)} copy-done((f32[512,1024]{1,0:T(8,128)S(1)}, f32[512,1024]{1,0:T(8,128)}, u32[]{:S(2)}) %copy-start) | copy-done | bytes 2097176
  2.2 0.7 copy-done.1
  2.9 1.5 %pack.1 = (s32[1,512]{1,0:T(1,128)S(1)}, bf16[128,1024]{1,0:T(8,128)(2,1)S(1)}, bf16[128,1024]{1,0:T(8,128)(2,1)S(1)}, bf16[128,1024]{1,0:T(8,128)(2,1)S(1)}, bf...) custom-call(f32[512,1024]{1,0:T(8,128)S(1)} %copy-done, ...), custom_call_target="tpu_custom_call" | custom-call | tf_op jit(solution)/shard_map/pack/pallas_call | solution.py:194
  4.4 3.0 %collective-permute-start.2 = (bf16[128,1024]{1,0:T(8,128)(2,1)S(1)}, bf16[128,1024]{1,0:T(8,128)(2,1)S(1)}, u32[]{:S(2)}, u32[]{:S(2)}) collective-permute-start(bf16[128,1024]{1,0:T(8,128)(2,1)S(1)} %get-tuple-element.41), channel_id=1, source_target_pairs={{0,16},{1,17},{2,18},{3,19},{4,20},{5,21},{6,22},{7,23},{8,24},{9,... | collective-permute-start | bytes 786440 | tf_op jit(solution)/shard_map/ppermute | solution.py:215
  7.5 1.5 %collective-permute-start.5 = (bf16[128,1024]{1,0:T(8,128)(2,1)S(1)}, bf16[128,1024]{1,0:T(8,128)(2,1)S(1)}, u32[]{:S(2)}, u32[]{:S(2)}) collective-permute-start(bf16[128,1024]{1,0:T(8,128)(2,1)S(1)} %get-tuple-element.44.refs_2_.refs_3_.refs_4_), channel_id=1, source_target_pairs={{0,8},{1,9},{2,10},{3,11},{4,12},{5,13},{6,14},{7,15},{8,0},{9,1},... | collective-permute-start | bytes 786440 | tf_op jit(solution)/shard_map/ppermute | solution.py:223
  8.9 1.6 %collective-permute-start.4 = (bf16[128,1024]{1,0:T(8,128)(2,1)S(1)}, bf16[128,1024]{1,0:T(8,128)(2,1)S(1)}, u32[]{:S(2)}, u32[]{:S(2)}) collective-permute-start(bf16[128,1024]{1,0:T(8,128)(2,1)S(1)} %get-tuple-element.43), channel_id=1, source_target_pairs={{0,1},{1,2},{2,3},{3,0},{4,5},{5,6},{6,7},{7,4},{8,9},{9,10},{10,1... | collective-permute-start | bytes 786440 | tf_op jit(solution)/shard_map/ppermute | solution.py:215
  10.5 1.5 %collective-permute-start = (bf16[128,1024]{1,0:T(8,128)(2,1)S(1)}, bf16[128,1024]{1,0:T(8,128)(2,1)S(1)}, u32[]{:S(2)}, u32[]{:S(2)}) collective-permute-start(bf16[128,1024]{1,0:T(8,128)(2,1)S(1)} %get-tuple-element.38), channel_id=1, source_target_pairs={{0,17},{1,18},{2,19},{3,16},{4,21},{5,22},{6,23},{7,20},{8,25},{9,... | collective-permute-start | bytes 786440 | tf_op jit(solution)/shard_map/ppermute | solution.py:215
  12.0 1.7 %collective-permute-done.2.refs_3_.refs_2_.refs_5_ = bf16[128,1024]{1,0:T(8,128)(2,1)S(1)} collective-permute-done((bf16[128,1024]{1,0:T(8,128)(2,1)S(1)}, bf16[128,1024]{1,0:T(8,128)(2,1)S(1)}, u32[]{:S(2)}, u32[]{:S(2)}) %collective-permute-start.2) | collective-permute-done | bytes 262176 | tf_op jit(solution)/shard_map/ppermute | solution.py:215
  13.8 1.5 %collective-permute-done.5.refs_4_.refs_6_ = bf16[128,1024]{1,0:T(8,128)(2,1)S(1)} collective-permute-done((bf16[128,1024]{1,0:T(8,128)(2,1)S(1)}, bf16[128,1024]{1,0:T(8,128)(2,1)S(1)}, u32[]{:S(2)}, u32[]{:S(2)}) %collective-permute-start.5) | collective-permute-done | bytes 262176 | tf_op jit(solution)/shard_map/ppermute | solution.py:223
  15.2 1.5 %collective-permute-start.6 = (bf16[128,1024]{1,0:T(8,128)(2,1)S(1)}, bf16[128,1024]{1,0:T(8,128)(2,1)S(1)}, u32[]{:S(2)}, u32[]{:S(2)}) collective-permute-start(bf16[128,1024]{1,0:T(8,128)(2,1)S(1)} %collective-permute-done.2.refs_3_.refs_2_.refs_5_), channel_id=1, source_target_pairs={{0,8},{1,9},{2,10},{3,11},{4,12},{5,13},{6,14},{7,15},{8,0},{9,1},... | collective-permute-start | bytes 786440 | tf_op jit(solution)/shard_map/ppermute | solution.py:223
  16.7 3.6 %collective-permute-start.3 = (bf16[128,1024]{1,0:T(8,128)(2,1)S(1)}, bf16[128,1024]{1,0:T(8,128)(2,1)S(1)}, u32[]{:S(2)}, u32[]{:S(2)}) collective-permute-start(bf16[128,1024]{1,0:T(8,128)(2,1)S(1)} %get-tuple-element.42), channel_id=1, source_target_pairs={{0,3},{1,0},{2,1},{3,2},{4,7},{5,4},{6,5},{7,6},{8,11},{9,8},{10,9... | collective-permute-start | bytes 786440 | tf_op jit(solution)/shard_map/ppermute | solution.py:215
  20.3 0.0 collective-permute-done.4.refs_0_.refs_6_.refs_8_
  20.3 0.5 collective-permute-start.7
  20.8 1.4 %collective-permute-start.9 = (bf16[128,1024]{1,0:T(8,128)(2,1)S(1)}, bf16[128,1024]{1,0:T(8,128)(2,1)S(1)}, u32[]{:S(2)}, u32[]{:S(2)}) collective-permute-start(bf16[128,1024]{1,0:T(8,128)(2,1)S(1)} %get-tuple-element.49), channel_id=1, source_target_pairs={{0,19},{1,16},{2,17},{3,18},{4,23},{5,20},{6,21},{7,22},{8,27},{9,... | collective-permute-start | bytes 786440 | tf_op jit(solution)/shard_map/ppermute | solution.py:215
  22.2 3.3 %collective-permute-done.refs_1_.refs_7_.refs_9_ = bf16[128,1024]{1,0:T(8,128)(2,1)S(1)} collective-permute-done((bf16[128,1024]{1,0:T(8,128)(2,1)S(1)}, bf16[128,1024]{1,0:T(8,128)(2,1)S(1)}, u32[]{:S(2)}, u32[]{:S(2)}) %collective-permute-start) | collective-permute-done | bytes 262176 | tf_op jit(solution)/shard_map/ppermute | solution.py:215
  25.6 0.0 collective-permute-done.6.refs_5_.refs_7_
  25.6 0.3 collective-permute-start.8
  25.9 16.1 %collective-permute-start.1 = (bf16[128,1024]{1,0:T(8,128)(2,1)S(1)}, bf16[128,1024]{1,0:T(8,128)(2,1)S(1)}, u32[]{:S(2)}, u32[]{:S(2)}) collective-permute-start(bf16[128,1024]{1,0:T(8,128)(2,1)S(1)} %get-tuple-element.39), channel_id=1, source_target_pairs={{0,2},{1,3},{2,0},{3,1},{4,6},{5,7},{6,4},{7,5},{8,10},{9,11},{10,... | collective-permute-start | bytes 786440 | tf_op jit(solution)/shard_map/ppermute | solution.py:215
  42.0 0.0 collective-permute-done.3.refs_10_.refs_0_.refs_12_
  42.0 1.0 collective-permute-start.12
  42.9 0.0 collective-permute-done.7.refs_8_.refs_10_
  42.9 1.5 %collective-permute-start.10 = (bf16[128,1024]{1,0:T(8,128)(2,1)S(1)}, bf16[128,1024]{1,0:T(8,128)(2,1)S(1)}, u32[]{:S(2)}, u32[]{:S(2)}) collective-permute-start(bf16[128,1024]{1,0:T(8,128)(2,1)S(1)} %collective-permute-done.3.refs_10_.refs_0_.refs_12_), channel_id=1, source_target_pairs={{0,8},{1,9},{2,10},{3,11},{4,12},{5,13},{6,14},{7,15},{8,0},{9,1},... | collective-permute-start | bytes 786440 | tf_op jit(solution)/shard_map/ppermute | solution.py:223
  44.4 0.0 collective-permute-done.9.refs_11_.refs_1_.refs_13_
  44.4 0.0 collective-permute-done.8.refs_9_.refs_11_
  44.4 0.5 collective-permute-start.11
  45.0 0.1 pad_maximum_fusion
  45.0 0.1 collective-permute-start.15
  45.1 0.1 pad_maximum_fusion.1
  45.2 4.1 %collective-permute-done.10.refs_12_.refs_14_ = bf16[128,1024]{1,0:T(8,128)(2,1)S(1)} collective-permute-done((bf16[128,1024]{1,0:T(8,128)(2,1)S(1)}, bf16[128,1024]{1,0:T(8,128)(2,1)S(1)}, u32[]{:S(2)}, u32[]{:S(2)}) %collective-permute-start.10) | collective-permute-done | bytes 262176 | tf_op jit(solution)/shard_map/ppermute | solution.py:223
  49.3 0.0 collective-permute-start.16
  49.3 2.8 %collective-permute-done.11.refs_13_.refs_15_ = bf16[128,1024]{1,0:T(8,128)(2,1)S(1)} collective-permute-done((bf16[128,1024]{1,0:T(8,128)(2,1)S(1)}, bf16[128,1024]{1,0:T(8,128)(2,1)S(1)}, u32[]{:S(2)}, u32[]{:S(2)}) %collective-permute-start.11) | collective-permute-done | bytes 262176 | tf_op jit(solution)/shard_map/ppermute | solution.py:223
  52.1 0.1 pad_maximum_fusion.2
  52.2 0.1 collective-permute-start.17
  52.3 1.6 %collective-permute-start.13 = (bf16[128,1024]{1,0:T(8,128)(2,1)S(1)}, bf16[128,1024]{1,0:T(8,128)(2,1)S(1)}, u32[]{:S(2)}, u32[]{:S(2)}) collective-permute-start(bf16[128,1024]{1,0:T(8,128)(2,1)S(1)} %collective-permute-done.1.refs_14_.refs_0_.refs_16_), channel_id=1, source_target_pairs={{0,8},{1,9},{2,10},{3,11},{4,12},{5,13},{6,14},{7,15},{8,0},{9,1},... | collective-permute-start | bytes 786440 | tf_op jit(solution)/shard_map/ppermute | solution.py:223
  53.8 3.7 %collective-permute-done.12.refs_15_.refs_1_.refs_17_ = bf16[128,1024]{1,0:T(8,128)(2,1)S(1)} collective-permute-done((bf16[128,1024]{1,0:T(8,128)(2,1)S(1)}, bf16[128,1024]{1,0:T(8,128)(2,1)S(1)}, u32[]{:S(2)}, u32[]{:S(2)}) %collective-permute-start.12) | collective-permute-done | bytes 262176 | tf_op jit(solution)/shard_map/ppermute | solution.py:215
  57.5 0.6 collective-permute-start.14
  58.1 3.4 %collective-permute-done.13.refs_16_.refs_18_ = bf16[128,1024]{1,0:T(8,128)(2,1)S(1)} collective-permute-done((bf16[128,1024]{1,0:T(8,128)(2,1)S(1)}, bf16[128,1024]{1,0:T(8,128)(2,1)S(1)}, u32[]{:S(2)}, u32[]{:S(2)}) %collective-permute-start.13) | collective-permute-done | bytes 262176 | tf_op jit(solution)/shard_map/ppermute | solution.py:223
  61.5 0.1 collective-permute-start.18
  61.6 5.0 %collective-permute-done.14.refs_17_.refs_19_ = bf16[128,1024]{1,0:T(8,128)(2,1)S(1)} collective-permute-done((bf16[128,1024]{1,0:T(8,128)(2,1)S(1)}, bf16[128,1024]{1,0:T(8,128)(2,1)S(1)}, u32[]{:S(2)}, u32[]{:S(2)}) %collective-permute-start.14) | collective-permute-done | bytes 262176 | tf_op jit(solution)/shard_map/ppermute | solution.py:223
  66.6 0.1 collective-permute-start.19
  66.7 0.0 collective-permute-done.15.refs_18_.refs_20_
  66.7 0.0 copy-start.3
  66.7 1.9 %collective-permute-done.19.refs_22_.refs_24_ = bf16[256,1024]{1,0:T(8,128)(2,1)S(1)} collective-permute-done((bf16[256,1024]{1,0:T(8,128)(2,1)S(1)}, bf16[256,1024]{1,0:T(8,128)(2,1)S(1)}, u32[]{:S(2)}, u32[]{:S(2)}) %collective-permute-start.19) | collective-permute-done | bytes 524320 | tf_op jit(solution)/shard_map/ppermute | solution.py:227
  68.6 1.0 copy-done.4
  69.6 1.0 copy-done.5
  70.6 7.6 %weigh.3 = (bf16[136,1024]{1,0:T(8,128)(2,1)S(1)}, bf16[136,1024]{1,0:T(8,128)(2,1)S(1)}) custom-call(bf16[128,1024]{1,0:T(8,128)(2,1)S(1)} %collective-permute-done.4.refs_0_.refs_6_.refs_8_, bf16[128,1024]{1,0:T(8,128)(2,1)S(1)} %collective-permute-done.refs_1_.refs_7_.refs_9_, bf16[128,1024]{1,0:T(8,128)(2,1)S(1)} %get-tuple-element.44.refs_2_.refs_3_.refs_4_, ...), custom_call_target="tpu_custom_call" | custom-call | flops 4294967296 | bytes 8388608 | tf_op jit(solution)/shard_map/weigh/pallas_call | solution.py:246
  78.2 1.1 collective-permute-start.23
  79.3 3.5 %collective-permute-start.24 = (bf16[136,1024]{1,0:T(8,128)(2,1)S(1)}, bf16[136,1024]{1,0:T(8,128)(2,1)S(1)}, u32[]{:S(2)}, u32[]{:S(2)}) collective-permute-start(bf16[136,1024]{1,0:T(8,128)(2,1)S(1)} %get-tuple-element.64), channel_id=1, source_target_pairs={{0,19},{1,16},{2,17},{3,18},{4,23},{5,20},{6,21},{7,22},{8,27},{9,... | collective-permute-start | bytes 835592 | tf_op jit(solution)/shard_map/ppermute | solution.py:305
  82.7 7.6 %weigh.4 = (bf16[136,1024]{1,0:T(8,128)(2,1)S(1)}, bf16[136,1024]{1,0:T(8,128)(2,1)S(1)}) custom-call(bf16[128,1024]{1,0:T(8,128)(2,1)S(1)} %collective-permute-done.3.refs_10_.refs_0_.refs_12_, bf16[128,1024]{1,0:T(8,128)(2,1)S(1)} %collective-permute-done.9.refs_11_.refs_1_.refs_13_, bf16[128,1024]{1,0:T(8,128)(2,1)S(1)} %get-tuple-element.44.refs_2_.refs_3_.refs_4_, ...), custom_call_target="tpu_custom_call" | custom-call | flops 4294967296 | bytes 8388608 | tf_op jit(solution)/shard_map/weigh/pallas_call | solution.py:246
  90.4 0.1 collective-permute-start.25
  90.4 0.4 collective-permute-start.26
  90.9 13.6 %weigh.5 = (bf16[136,1024]{1,0:T(8,128)(2,1)S(1)}, bf16[136,1024]{1,0:T(8,128)(2,1)S(1)}, bf16[136,1024]{1,0:T(8,128)(2,1)S(1)}, bf16[136,1024]{1,0:T(8,128)(2,1)S(1)}) custom-call(bf16[128,1024]{1,0:T(8,128)(2,1)S(1)} %collective-permute-done.1.refs_14_.refs_0_.refs_16_, bf16[128,1024]{1,0:T(8,128)(2,1)S(1)} %collective-permute-done.12.refs_15_.refs_1_.refs_17_, ...), custom_call_target="tpu_custom_call" | custom-call | flops 8589934592 | bytes 8388608 | tf_op jit(solution)/shard_map/weigh/pallas_call | solution.py:246
  104.5 4.8 %collective-permute-start.20 = (bf16[136,1024]{1,0:T(8,128)(2,1)S(1)}, bf16[136,1024]{1,0:T(8,128)(2,1)S(1)}, u32[]{:S(2)}, u32[]{:S(2)}) collective-permute-start(bf16[136,1024]{1,0:T(8,128)(2,1)S(1)} %get-tuple-element.60), channel_id=1, source_target_pairs={{0,2},{1,3},{2,0},{3,1},{4,6},{5,7},{6,4},{7,5},{8,10},{9,11},{10,... | collective-permute-start | bytes 835592 | tf_op jit(solution)/shard_map/ppermute | solution.py:305
  109.3 0.0 collective-permute-done.24.refs_2_
  109.3 0.2 collective-permute-start.21
  109.4 0.0 collective-permute-done.23.refs_1_
  109.4 1.4 %collective-permute-start.22 = (bf16[136,1024]{1,0:T(8,128)(2,1)S(1)}, bf16[136,1024]{1,0:T(8,128)(2,1)S(1)}, u32[]{:S(2)}, u32[]{:S(2)}) collective-permute-start(bf16[136,1024]{1,0:T(8,128)(2,1)S(1)} %get-tuple-element.62), channel_id=1, source_target_pairs={{0,16},{1,17},{2,18},{3,19},{4,20},{5,21},{6,22},{7,23},{8,24},{9,... | collective-permute-start | bytes 835592 | tf_op jit(solution)/shard_map/ppermute | solution.py:305
  110.8 0.0 collective-permute-done.26.refs_4_
  110.8 0.0 collective-permute-done.25.refs_3_
  110.8 1.7 %unpack.2 = (f32[1,512]{1,0:T(1,128)S(1)}, f32[512,1024]{1,0:T(8,128)S(1)}) custom-call(s32[1,512]{1,0:T(1,128)S(1)} %get-tuple-element.36.pos_ref, bf16[136,1024]{1,0:T(8,128)(2,1)S(1)} %get-tuple-element.63.refs_0_, bf16[136,1024]{1,0:T(8,128)(2,1)S(1)} %collective-permute-done.23.refs_1_, bf16[136,1024]{1,0:T(8,128)(2,1)S(1)} %collective-permute-done.24.refs_2_, ...), custom_call_target="tpu_custom_call" | custom-call | tf_op jit(solution)/shard_map/unpack/pallas_call | solution.py:308
  112.5 14.4 %collective-permute-done.20.refs_0_ = bf16[136,1024]{1,0:T(8,128)(2,1)S(1)} collective-permute-done((bf16[136,1024]{1,0:T(8,128)(2,1)S(1)}, bf16[136,1024]{1,0:T(8,128)(2,1)S(1)}, u32[]{:S(2)}, u32[]{:S(2)}) %collective-permute-start.20) | collective-permute-done | bytes 278560 | tf_op jit(solution)/shard_map/ppermute | solution.py:305
  126.9 6.0 %collective-permute-done.21.refs_1_ = bf16[136,1024]{1,0:T(8,128)(2,1)S(1)} collective-permute-done((bf16[136,1024]{1,0:T(8,128)(2,1)S(1)}, bf16[136,1024]{1,0:T(8,128)(2,1)S(1)}, u32[]{:S(2)}, u32[]{:S(2)}) %collective-permute-start.21) | collective-permute-done | bytes 278560 | tf_op jit(solution)/shard_map/ppermute | solution.py:305
  132.9 0.0 collective-permute-done.22.refs_2_
  132.9 2.4 %unpack.3 = (f32[1,512]{1,0:T(1,128)}, f32[512,1024]{1,0:T(8,128)}) custom-call(s32[1,512]{1,0:T(1,128)S(1)} %get-tuple-element.36.pos_ref, bf16[136,1024]{1,0:T(8,128)(2,1)S(1)} %collective-permute-done.20.refs_0_, bf16[136,1024]{1,0:T(8,128)(2,1)S(1)} %collective-permute-done.21.refs_1_, bf16[136,1024]{1,0:T(8,128)(2,1)S(1)} %collective-permute-done.22.refs_2_, ...), custom_call_target="tpu_custom_call" | custom-call | tf_op jit(solution)/shard_map/unpack/pallas_call | solution.py:308
  (13 shorter events, 0.1 us)
Async XLA Ops:
  0.6 1.6 %copy-start = (f32[512,1024]{1,0:T(8,128)S(1)}, f32[512,1024]{1,0:T(8,128)}, u32[]{:S(2)}) copy-start(f32[512,1024]{1,0:T(8,128)} %emb_ref.1) | copy-start | bytes 6291460
  2.2 0.7 copy-start.1
  4.4 9.3 %collective-permute-start.2 = (bf16[128,1024]{1,0:T(8,128)(2,1)S(1)}, bf16[128,1024]{1,0:T(8,128)(2,1)S(1)}, u32[]{:S(2)}, u32[]{:S(2)}) collective-permute-start(bf16[128,1024]{1,0:T(8,128)(2,1)S(1)} %get-tuple-element.41), channel_id=1, source_target_pairs={{0,16},{1,17},{2,18},{3,19},{4,20},{5,21},{6,22},{7,23},{8,24},{9,... | collective-permute-start | bytes 786440 | tf_op jit(solution)/shard_map/ppermute | solution.py:215
  7.5 7.8 %collective-permute-start.5 = (bf16[128,1024]{1,0:T(8,128)(2,1)S(1)}, bf16[128,1024]{1,0:T(8,128)(2,1)S(1)}, u32[]{:S(2)}, u32[]{:S(2)}) collective-permute-start(bf16[128,1024]{1,0:T(8,128)(2,1)S(1)} %get-tuple-element.44.refs_2_.refs_3_.refs_4_), channel_id=1, source_target_pairs={{0,8},{1,9},{2,10},{3,11},{4,12},{5,13},{6,14},{7,15},{8,0},{9,1},... | collective-permute-start | bytes 786440 | tf_op jit(solution)/shard_map/ppermute | solution.py:223
  8.9 11.4 %collective-permute-start.4 = (bf16[128,1024]{1,0:T(8,128)(2,1)S(1)}, bf16[128,1024]{1,0:T(8,128)(2,1)S(1)}, u32[]{:S(2)}, u32[]{:S(2)}) collective-permute-start(bf16[128,1024]{1,0:T(8,128)(2,1)S(1)} %get-tuple-element.43), channel_id=1, source_target_pairs={{0,1},{1,2},{2,3},{3,0},{4,5},{5,6},{6,7},{7,4},{8,9},{9,10},{10,1... | collective-permute-start | bytes 786440 | tf_op jit(solution)/shard_map/ppermute | solution.py:215
  10.5 15.1 %collective-permute-start = (bf16[128,1024]{1,0:T(8,128)(2,1)S(1)}, bf16[128,1024]{1,0:T(8,128)(2,1)S(1)}, u32[]{:S(2)}, u32[]{:S(2)}) collective-permute-start(bf16[128,1024]{1,0:T(8,128)(2,1)S(1)} %get-tuple-element.38), channel_id=1, source_target_pairs={{0,17},{1,18},{2,19},{3,16},{4,21},{5,22},{6,23},{7,20},{8,25},{9,... | collective-permute-start | bytes 786440 | tf_op jit(solution)/shard_map/ppermute | solution.py:215
  15.2 10.4 %collective-permute-start.6 = (bf16[128,1024]{1,0:T(8,128)(2,1)S(1)}, bf16[128,1024]{1,0:T(8,128)(2,1)S(1)}, u32[]{:S(2)}, u32[]{:S(2)}) collective-permute-start(bf16[128,1024]{1,0:T(8,128)(2,1)S(1)} %collective-permute-done.2.refs_3_.refs_2_.refs_5_), channel_id=1, source_target_pairs={{0,8},{1,9},{2,10},{3,11},{4,12},{5,13},{6,14},{7,15},{8,0},{9,1},... | collective-permute-start | bytes 786440 | tf_op jit(solution)/shard_map/ppermute | solution.py:223
  16.7 25.3 %collective-permute-start.3 = (bf16[128,1024]{1,0:T(8,128)(2,1)S(1)}, bf16[128,1024]{1,0:T(8,128)(2,1)S(1)}, u32[]{:S(2)}, u32[]{:S(2)}) collective-permute-start(bf16[128,1024]{1,0:T(8,128)(2,1)S(1)} %get-tuple-element.42), channel_id=1, source_target_pairs={{0,3},{1,0},{2,1},{3,2},{4,7},{5,4},{6,5},{7,6},{8,11},{9,8},{10,9... | collective-permute-start | bytes 786440 | tf_op jit(solution)/shard_map/ppermute | solution.py:215
  20.3 22.6 %collective-permute-start.7 = (bf16[128,1024]{1,0:T(8,128)(2,1)S(1)}, bf16[128,1024]{1,0:T(8,128)(2,1)S(1)}, u32[]{:S(2)}, u32[]{:S(2)}) collective-permute-start(bf16[128,1024]{1,0:T(8,128)(2,1)S(1)} %collective-permute-done.4.refs_0_.refs_6_.refs_8_), channel_id=1, source_target_pairs={{0,8},{1,9},{2,10},{3,11},{4,12},{5,13},{6,14},{7,15},{8,0},{9,1},... | collective-permute-start | bytes 786440 | tf_op jit(solution)/shard_map/ppermute | solution.py:223
  20.8 23.6 %collective-permute-start.9 = (bf16[128,1024]{1,0:T(8,128)(2,1)S(1)}, bf16[128,1024]{1,0:T(8,128)(2,1)S(1)}, u32[]{:S(2)}, u32[]{:S(2)}) collective-permute-start(bf16[128,1024]{1,0:T(8,128)(2,1)S(1)} %get-tuple-element.49), channel_id=1, source_target_pairs={{0,19},{1,16},{2,17},{3,18},{4,23},{5,20},{6,21},{7,22},{8,27},{9,... | collective-permute-start | bytes 786440 | tf_op jit(solution)/shard_map/ppermute | solution.py:215
  25.6 18.8 %collective-permute-start.8 = (bf16[128,1024]{1,0:T(8,128)(2,1)S(1)}, bf16[128,1024]{1,0:T(8,128)(2,1)S(1)}, u32[]{:S(2)}, u32[]{:S(2)}) collective-permute-start(bf16[128,1024]{1,0:T(8,128)(2,1)S(1)} %collective-permute-done.refs_1_.refs_7_.refs_9_), channel_id=1, source_target_pairs={{0,8},{1,9},{2,10},{3,11},{4,12},{5,13},{6,14},{7,15},{8,0},{9,1},... | collective-permute-start | bytes 786440 | tf_op jit(solution)/shard_map/ppermute | solution.py:223
  25.9 26.4 %collective-permute-start.1 = (bf16[128,1024]{1,0:T(8,128)(2,1)S(1)}, bf16[128,1024]{1,0:T(8,128)(2,1)S(1)}, u32[]{:S(2)}, u32[]{:S(2)}) collective-permute-start(bf16[128,1024]{1,0:T(8,128)(2,1)S(1)} %get-tuple-element.39), channel_id=1, source_target_pairs={{0,2},{1,3},{2,0},{3,1},{4,6},{5,7},{6,4},{7,5},{8,10},{9,11},{10,... | collective-permute-start | bytes 786440 | tf_op jit(solution)/shard_map/ppermute | solution.py:215
  42.0 15.6 %collective-permute-start.12 = (bf16[128,1024]{1,0:T(8,128)(2,1)S(1)}, bf16[128,1024]{1,0:T(8,128)(2,1)S(1)}, u32[]{:S(2)}, u32[]{:S(2)}) collective-permute-start(bf16[128,1024]{1,0:T(8,128)(2,1)S(1)} %get-tuple-element.53), channel_id=1, source_target_pairs={{0,18},{1,19},{2,16},{3,17},{4,22},{5,23},{6,20},{7,21},{8,26},{9,... | collective-permute-start | bytes 786440 | tf_op jit(solution)/shard_map/ppermute | solution.py:215
  42.9 6.4 %collective-permute-start.10 = (bf16[128,1024]{1,0:T(8,128)(2,1)S(1)}, bf16[128,1024]{1,0:T(8,128)(2,1)S(1)}, u32[]{:S(2)}, u32[]{:S(2)}) collective-permute-start(bf16[128,1024]{1,0:T(8,128)(2,1)S(1)} %collective-permute-done.3.refs_10_.refs_0_.refs_12_), channel_id=1, source_target_pairs={{0,8},{1,9},{2,10},{3,11},{4,12},{5,13},{6,14},{7,15},{8,0},{9,1},... | collective-permute-start | bytes 786440 | tf_op jit(solution)/shard_map/ppermute | solution.py:223
  44.4 7.7 %collective-permute-start.11 = (bf16[128,1024]{1,0:T(8,128)(2,1)S(1)}, bf16[128,1024]{1,0:T(8,128)(2,1)S(1)}, u32[]{:S(2)}, u32[]{:S(2)}) collective-permute-start(bf16[128,1024]{1,0:T(8,128)(2,1)S(1)} %collective-permute-done.9.refs_11_.refs_1_.refs_13_), channel_id=1, source_target_pairs={{0,8},{1,9},{2,10},{3,11},{4,12},{5,13},{6,14},{7,15},{8,0},{9,1},... | collective-permute-start | bytes 786440 | tf_op jit(solution)/shard_map/ppermute | solution.py:223
  45.0 21.7 %collective-permute-start.15 = (bf16[512,1024]{1,0:T(8,128)(2,1)S(1)}, bf16[512,1024]{1,0:T(8,128)(2,1)S(1)}, u32[]{:S(2)}, u32[]{:S(2)}) collective-permute-start(bf16[512,1024]{1,0:T(8,128)(2,1)S(1)} %pad_maximum_fusion), channel_id=1, source_target_pairs={{0,4},{1,5},{2,6},{3,7},{4,0},{5,1},{6,2},{7,3},{8,12},{9,13},{10,... | collective-permute-start | bytes 3145736 | tf_op jit(solution)/shard_map/ppermute | solution.py:227
  49.3 19.3 %collective-permute-start.16 = (bf16[512,1024]{1,0:T(8,128)(2,1)S(1)}, bf16[512,1024]{1,0:T(8,128)(2,1)S(1)}, u32[]{:S(2)}, u32[]{:S(2)}) collective-permute-start(bf16[512,1024]{1,0:T(8,128)(2,1)S(1)} %pad_maximum_fusion.1), channel_id=1, source_target_pairs={{0,4},{1,5},{2,6},{3,7},{4,0},{5,1},{6,2},{7,3},{8,12},{9,13},{10,... | collective-permute-start | bytes 3145736 | tf_op jit(solution)/shard_map/ppermute | solution.py:227
  52.2 16.4 %collective-permute-start.17 = (bf16[512,1024]{1,0:T(8,128)(2,1)S(1)}, bf16[512,1024]{1,0:T(8,128)(2,1)S(1)}, u32[]{:S(2)}, u32[]{:S(2)}) collective-permute-start(bf16[512,1024]{1,0:T(8,128)(2,1)S(1)} %pad_maximum_fusion.2), channel_id=1, source_target_pairs={{0,4},{1,5},{2,6},{3,7},{4,0},{5,1},{6,2},{7,3},{8,12},{9,13},{10,... | collective-permute-start | bytes 3145736 | tf_op jit(solution)/shard_map/ppermute | solution.py:227
  52.3 9.2 %collective-permute-start.13 = (bf16[128,1024]{1,0:T(8,128)(2,1)S(1)}, bf16[128,1024]{1,0:T(8,128)(2,1)S(1)}, u32[]{:S(2)}, u32[]{:S(2)}) collective-permute-start(bf16[128,1024]{1,0:T(8,128)(2,1)S(1)} %collective-permute-done.1.refs_14_.refs_0_.refs_16_), channel_id=1, source_target_pairs={{0,8},{1,9},{2,10},{3,11},{4,12},{5,13},{6,14},{7,15},{8,0},{9,1},... | collective-permute-start | bytes 786440 | tf_op jit(solution)/shard_map/ppermute | solution.py:223
  57.5 9.1 %collective-permute-start.14 = (bf16[128,1024]{1,0:T(8,128)(2,1)S(1)}, bf16[128,1024]{1,0:T(8,128)(2,1)S(1)}, u32[]{:S(2)}, u32[]{:S(2)}) collective-permute-start(bf16[128,1024]{1,0:T(8,128)(2,1)S(1)} %collective-permute-done.12.refs_15_.refs_1_.refs_17_), channel_id=1, source_target_pairs={{0,8},{1,9},{2,10},{3,11},{4,12},{5,13},{6,14},{7,15},{8,0},{9,1},... | collective-permute-start | bytes 786440 | tf_op jit(solution)/shard_map/ppermute | solution.py:223
  61.5 5.2 %collective-permute-start.18 = (bf16[256,1024]{1,0:T(8,128)(2,1)S(1)}, bf16[256,1024]{1,0:T(8,128)(2,1)S(1)}, u32[]{:S(2)}, u32[]{:S(2)}) collective-permute-start(bf16[256,1024]{1,0:T(8,128)(2,1)S(1)} %pad_maximum_fusion.3), channel_id=1, source_target_pairs={{0,4},{1,5},{2,6},{3,7},{4,0},{5,1},{6,2},{7,3},{8,12},{9,13},{10,... | collective-permute-start | bytes 1572872 | tf_op jit(solution)/shard_map/ppermute | solution.py:227
  66.6 2.0 %collective-permute-start.19 = (bf16[256,1024]{1,0:T(8,128)(2,1)S(1)}, bf16[256,1024]{1,0:T(8,128)(2,1)S(1)}, u32[]{:S(2)}, u32[]{:S(2)}) collective-permute-start(bf16[256,1024]{1,0:T(8,128)(2,1)S(1)} %pad_maximum_fusion.4), channel_id=1, source_target_pairs={{0,4},{1,5},{2,6},{3,7},{4,0},{5,1},{6,2},{7,3},{8,12},{9,13},{10,... | collective-permute-start | bytes 1572872 | tf_op jit(solution)/shard_map/ppermute | solution.py:227
  66.7 1.9 %copy-start.3 = (bf16[512,1024]{1,0:T(8,128)(2,1)}, bf16[512,1024]{1,0:T(8,128)(2,1)S(1)}, u32[]{:S(2)}) copy-start(bf16[512,1024]{1,0:T(8,128)(2,1)S(1)} %collective-permute-done.15.refs_18_.refs_20_) | copy-start | bytes 3145732
  68.6 14.1 %copy-start.2 = (bf16[256,1024]{1,0:T(8,128)(2,1)}, bf16[256,1024]{1,0:T(8,128)(2,1)S(1)}, u32[]{:S(2)}) copy-start(bf16[256,1024]{1,0:T(8,128)(2,1)S(1)} %collective-permute-done.19.refs_22_.refs_24_) | copy-start | bytes 1572868
  68.6 1.0 copy-start.4
  69.6 1.0 copy-start.5
  78.2 31.3 %collective-permute-start.23 = (bf16[136,1024]{1,0:T(8,128)(2,1)S(1)}, bf16[136,1024]{1,0:T(8,128)(2,1)S(1)}, u32[]{:S(2)}, u32[]{:S(2)}) collective-permute-start(bf16[136,1024]{1,0:T(8,128)(2,1)S(1)} %get-tuple-element.56), channel_id=1, source_target_pairs={{0,3},{1,0},{2,1},{3,2},{4,7},{5,4},{6,5},{7,6},{8,11},{9,8},{10,9... | collective-permute-start | bytes 835592 | tf_op jit(solution)/shard_map/ppermute | solution.py:305
  79.3 30.0 %collective-permute-start.24 = (bf16[136,1024]{1,0:T(8,128)(2,1)S(1)}, bf16[136,1024]{1,0:T(8,128)(2,1)S(1)}, u32[]{:S(2)}, u32[]{:S(2)}) collective-permute-start(bf16[136,1024]{1,0:T(8,128)(2,1)S(1)} %get-tuple-element.64), channel_id=1, source_target_pairs={{0,19},{1,16},{2,17},{3,18},{4,23},{5,20},{6,21},{7,22},{8,27},{9,... | collective-permute-start | bytes 835592 | tf_op jit(solution)/shard_map/ppermute | solution.py:305
  90.4 20.4 %collective-permute-start.25 = (bf16[136,1024]{1,0:T(8,128)(2,1)S(1)}, bf16[136,1024]{1,0:T(8,128)(2,1)S(1)}, u32[]{:S(2)}, u32[]{:S(2)}) collective-permute-start(bf16[136,1024]{1,0:T(8,128)(2,1)S(1)} %get-tuple-element.58), channel_id=1, source_target_pairs={{0,1},{1,2},{2,3},{3,0},{4,5},{5,6},{6,7},{7,4},{8,9},{9,10},{10,1... | collective-permute-start | bytes 835592 | tf_op jit(solution)/shard_map/ppermute | solution.py:305
  90.4 20.4 %collective-permute-start.26 = (bf16[136,1024]{1,0:T(8,128)(2,1)S(1)}, bf16[136,1024]{1,0:T(8,128)(2,1)S(1)}, u32[]{:S(2)}, u32[]{:S(2)}) collective-permute-start(bf16[136,1024]{1,0:T(8,128)(2,1)S(1)} %get-tuple-element.65), channel_id=1, source_target_pairs={{0,17},{1,18},{2,19},{3,16},{4,21},{5,22},{6,23},{7,20},{8,25},{9,... | collective-permute-start | bytes 835592 | tf_op jit(solution)/shard_map/ppermute | solution.py:305
  104.5 22.5 %collective-permute-start.20 = (bf16[136,1024]{1,0:T(8,128)(2,1)S(1)}, bf16[136,1024]{1,0:T(8,128)(2,1)S(1)}, u32[]{:S(2)}, u32[]{:S(2)}) collective-permute-start(bf16[136,1024]{1,0:T(8,128)(2,1)S(1)} %get-tuple-element.60), channel_id=1, source_target_pairs={{0,2},{1,3},{2,0},{3,1},{4,6},{5,7},{6,4},{7,5},{8,10},{9,11},{10,... | collective-permute-start | bytes 835592 | tf_op jit(solution)/shard_map/ppermute | solution.py:305
  109.3 23.6 %collective-permute-start.21 = (bf16[136,1024]{1,0:T(8,128)(2,1)S(1)}, bf16[136,1024]{1,0:T(8,128)(2,1)S(1)}, u32[]{:S(2)}, u32[]{:S(2)}) collective-permute-start(bf16[136,1024]{1,0:T(8,128)(2,1)S(1)} %get-tuple-element.61), channel_id=1, source_target_pairs={{0,18},{1,19},{2,16},{3,17},{4,22},{5,23},{6,20},{7,21},{8,26},{9,... | collective-permute-start | bytes 835592 | tf_op jit(solution)/shard_map/ppermute | solution.py:305
  109.4 23.4 %collective-permute-start.22 = (bf16[136,1024]{1,0:T(8,128)(2,1)S(1)}, bf16[136,1024]{1,0:T(8,128)(2,1)S(1)}, u32[]{:S(2)}, u32[]{:S(2)}) collective-permute-start(bf16[136,1024]{1,0:T(8,128)(2,1)S(1)} %get-tuple-element.62), channel_id=1, source_target_pairs={{0,16},{1,17},{2,18},{3,19},{4,20},{5,21},{6,22},{7,23},{8,24},{9,... | collective-permute-start | bytes 835592 | tf_op jit(solution)/shard_map/ppermute | solution.py:305

commit v3 on v0

v3 whole, which is shorter than its diff:
```python
import functools

import jax
import jax.numpy as jnp
from jax import lax
from jax.experimental import pallas as pl
from jax.experimental.pallas import tpu as pltpu
from jax.sharding import PartitionSpec as P

AXES = ("shard", "grp")
MIB = 1 << 20


def hop_order(ng):
    return sorted(range(ng), key=lambda d: (min(d, ng - d), d))


def write_blocks(first, slots, pos, used, units, out_refs):
    n, width = units.shape
    mark = float(2.0 * width**0.5)
    for i, ref in enumerate(out_refs):
        k = first + i
        pick = lax.broadcasted_iota(jnp.int32, (slots, n), 0) + k * slots == pos
        rows = jnp.dot(pick.astype(jnp.bfloat16), units, preferred_element_type=jnp.float32)
        empty = lax.broadcasted_iota(jnp.int32, (slots, width), 0) >= used[k : k + 1, 0:1]
        column = lax.broadcasted_iota(jnp.int32, (slots, width), 1)
        ref[...] = jnp.where(empty & (column == 0), mark, rows).astype(jnp.bfloat16)


def pack_kernel(hi_n, ng, slots, first, emb_ref, ids_ref, pos_ref, used_ref, units_ref, *out_refs):
    n, width = emb_ref.shape
    nb = hi_n * ng
    hi = lax.axis_index("shard") // ng
    z = lax.axis_index("grp")
    ids = ids_ref[...]
    blk = jnp.zeros((1, n), jnp.int32)
    for k, dz in enumerate(hop_order(ng)):
        for dh in range(hi_n):
            owner = lax.rem(hi + dh, hi_n) * ng + lax.rem(z + dz, ng)
            blk = jnp.where(ids == owner, k * hi_n + dh, blk)
    onehot = lax.broadcasted_iota(jnp.int32, (nb, n), 0) == blk
    upto = lax.broadcasted_iota(jnp.int32, (n, n), 0) <= lax.broadcasted_iota(jnp.int32, (n, n), 1)
    cum = jnp.dot(
        onehot.astype(jnp.bfloat16), upto.astype(jnp.bfloat16), preferred_element_type=jnp.float32
    )
    rank = jnp.sum(jnp.where(onehot, cum, 0.0), axis=0, keepdims=True).astype(jnp.int32) - 1
    pos = blk * slots + rank
    used = cum[:, n - 1 : n].astype(jnp.int32)
    pos_ref[...] = pos
    used_ref[...] = jnp.broadcast_to(used, used_ref.shape)
    emb = emb_ref[...]
    scale = lax.rsqrt(jnp.mean(emb * emb, axis=1, keepdims=True) + 1e-06)
    units = (emb * scale).astype(jnp.bfloat16)
    units_ref[...] = units
    write_blocks(first, slots, pos, used, units, out_refs)


def pack_rest_kernel(slots, skip, pos_ref, used_ref, units_ref, *out_refs):
    units, pos, used = units_ref[...], pos_ref[...], used_ref[...]
    start, stop = skip
    write_blocks(0, slots, pos, used, units, out_refs[:start])
    write_blocks(stop, slots, pos, used, units, out_refs[start:])


def weigh_kernel(layout, row_stage, unit, slots, ng, hops, summed, carried, last, *refs):
    refs = list(refs)

    def take(count):
        got = refs[:count]
        del refs[:count]
        return got

    row_in = take(sum(c for _, _, c in row_stage))
    cols = take(sum(c for _, c in layout))
    pull_in, count_in = take(2) if summed else (None, None)
    dups_in = take(1) if carried else None
    if last:
        outs = take(len(hops))
        dups, pull, count = refs
    else:
        pull, count = refs
    width = row_in[0].shape[1]
    nrows = len(row_stage) * unit
    limit = 1.5 * width**0.5
    probe = lax.broadcasted_iota(jnp.int32, (16, width), 1) == 0
    rows = jnp.concatenate([r[...] for r in row_in] + [probe.astype(jnp.bfloat16)], axis=0)
    for at, (stage, narr) in enumerate(layout):
        part = jnp.concatenate([c[...] for c in cols[:narr]], axis=0)
        del cols[:narr]
        chunk = part.shape[0]
        scores = lax.dot_general(
            rows, part, (((1,), (1,)), ((), ())), preferred_element_type=jnp.float32
        )
        keep = jnp.broadcast_to(scores[nrows : nrows + 1, :] < limit, (nrows, chunk))
        if any(s == stage for s, _, _ in row_stage):
            col = lax.broadcasted_iota(jnp.int32, (unit, chunk), 1)
            row = lax.broadcasted_iota(jnp.int32, (unit, chunk), 0)
            off = [col != (row + h * unit if s == stage else -1) for s, h, _ in row_stage]
            keep = keep & jnp.concatenate(off, axis=0)
        weight = jnp.where(keep, jnp.exp(scores[:nrows] * (64.0 / width)), 0.0)
        add_count = jnp.broadcast_to(jnp.sum(weight, axis=1, keepdims=True), count.shape)
        add_pull = jnp.dot(weight.astype(jnp.bfloat16), part, preferred_element_type=jnp.float32)
        if at:
            count[...] += add_count
            pull[...] += add_pull
        elif summed:
            count[...] = count_in[...] + add_count
            pull[...] = pull_in[...] + add_pull
        else:
            count[...] = add_count
            pull[...] = add_pull
    if not last:
        return
    dups[...] = dups_in[0][...] if carried else jnp.zeros(dups.shape, jnp.float32)
    hi_n = dups.shape[0] // ng
    hi, z = lax.axis_index("shard") // ng, lax.axis_index("grp")
    valid = rows[:nrows, 0:128].astype(jnp.float32)[:, 0:1] < limit
    for i in range(len(hops)):
        at = i * slots
        ok = valid[at : at + slots]
        cnt = count[pl.ds(at, slots), :]
        near = pull[pl.ds(at, slots), :] / (1.0 + cnt[:, 0:1])
        outs[i][...] = jnp.where(ok, near, 0.0).astype(jnp.bfloat16)
        dup = jnp.where(ok, jnp.log1p(cnt), 0.0)
        if slots < 128:
            dup = jnp.concatenate([dup, jnp.zeros((128 - slots, 128), jnp.float32)], axis=0)
        dh, dz = hops[i]
        home = lax.rem(hi + hi_n - dh, hi_n) * ng + lax.rem(z + ng - dz, ng)
        dups[pl.ds(home, 1), :] = dup.T[0:1]


def unpack_kernel(slots, which, last, hi_n, ng, pos_ref, *refs):
    refs = list(refs)
    nwhich = len(which)
    pos = pos_ref[...]
    n = pos.shape[1]

    def pick(k):
        at = lax.broadcasted_iota(jnp.int32, (slots, n), 0) + k * slots
        return (at == pos).astype(jnp.bfloat16)

    picks = jnp.concatenate([pick(k) for k in which], axis=0)
    rows = jnp.concatenate([r[...] for r in refs[:nwhich]], axis=0)
    if not last:
        dups, dup_ref, near_ref = refs[nwhich:]
        hi, z = lax.axis_index("shard") // ng, lax.axis_index("grp")
        line = lax.broadcasted_iota(jnp.int32, (8, 128), 0)
        dup = jnp.zeros((8, n), jnp.float32)
        for k, (dh, dz) in enumerate((dh, dz) for dz in hop_order(ng) for dh in range(hi_n)):
            owner = lax.rem(hi + dh, hi_n) * ng + lax.rem(z + dz, ng)
            row = jnp.broadcast_to(dups[pl.ds(owner, 1), :], (8, 128))
            high = row.astype(jnp.bfloat16).astype(jnp.float32)
            two = jnp.where(line == 0, high, jnp.where(line == 1, row - high, 0.0))
            two = two.astype(jnp.bfloat16)[:, :slots]
            dup = dup + jnp.dot(two, pick(k), preferred_element_type=jnp.float32)
        dup_ref[...] = dup[0:1] + dup[1:2]
        near_ref[...] = lax.dot_general(
            picks, rows, (((0,), (0,)), ((), ())), preferred_element_type=jnp.float32
        )
        return
    near_in, near_ref, near, sems = refs[nwhich:]
    step = n // 4
    copies = []
    for i in range(4):
        at = pl.ds(i * step, step)
        near[at, :] = near_in[at, :] + lax.dot_general(
            picks[:, i * step : (i + 1) * step],
            rows,
            (((0,), (0,)), ((), ())),
            preferred_element_type=jnp.float32,
        )
        copies.append(pltpu.make_async_copy(near.at[at], near_ref.at[at], sems.at[i]))
        copies[-1].start()
    for c in copies:
        c.wait()


def after(value, *deps):
    return lax.optimization_barrier((value,) + deps)[0]


def local(embeddings, cluster):
    n, width = embeddings.shape
    ns, ng = lax.axis_size("shard"), lax.axis_size("grp")
    hi_n = ns // ng
    nb = ns
    slots = 2 * n // ns

    def moved(f):
        return [(s * ng + z, f(s, z)) for s in range(ns) for z in range(ng)]

    def to_owner(dh, dz, sign):
        return moved(
            lambda s, z: ((s // ng + sign * dh) % hi_n * ng + s % ng) * ng + (z + sign * dz) % ng
        )

    def beside(bit):
        return moved(lambda s, z: (s ^ bit) * ng + z)

    hops = [(dh, dz) for dz in hop_order(ng) for dh in range(hi_n)]
    vmem = pl.BlockSpec(memory_space=pltpu.VMEM)
    hbm = pl.BlockSpec(memory_space=pltpu.HBM)
    ids = cluster.reshape(1, n)
    block = jax.ShapeDtypeStruct((slots, width), jnp.bfloat16)
    small = pltpu.CompilerParams(vmem_limit_bytes=16 * MIB)
    pos, used, units, *outbox = pl.pallas_call(
        functools.partial(pack_kernel, hi_n, ng, slots, hi_n),
        out_shape=[
            jax.ShapeDtypeStruct((1, n), jnp.int32),
            jax.ShapeDtypeStruct((nb, 128), jnp.int32),
            jax.ShapeDtypeStruct((n, width), jnp.bfloat16),
        ]
        + [block] * hi_n,
        in_specs=[vmem, vmem],
        out_specs=[vmem] * (hi_n + 3),
        compiler_params=small,
        name="pack",
    )(embeddings, ids)
    rest = pl.pallas_call(
        functools.partial(pack_rest_kernel, slots, (hi_n, 2 * hi_n)),
        out_shape=[block] * (nb - hi_n),
        in_specs=[vmem] * 3,
        out_specs=[vmem] * (nb - hi_n),
        compiler_params=small,
        name="pack_rest",
    )(pos, used, units)
    outbox = [*rest[:hi_n], *outbox, *rest[hi_n:]]

    per = hi_n // 2
    unit = per * slots
    nstage = ng
    own, side, other = {}, {}, {}

    def send(stage, half, *deps, cut=1):
        ks = blocks_of((stage, half))
        whole = [outbox[k] for k in ks]
        if cut > 1 and per == 1:
            pieces = [(ks[0], whole[0][i * unit // cut : (i + 1) * unit // cut]) for i in range(cut)]
        else:
            pieces = list(zip(ks, whole))
        got = []
        for k, src in pieces:
            if k:
                src = lax.ppermute(after(src, *deps) if deps else src, AXES, to_owner(*hops[k], 1))
            got.append(src)
        each = len(got) // cut
        own[stage, half] = [
            got[i] if each == 1 else jnp.concatenate(got[i : i + each], axis=0)
            for i in range(0, len(got), each)
        ]

    def across(stage, half, *deps):
        side[stage, half] = [
            lax.ppermute(after(src, *deps) if deps else src, AXES, beside(2))
            for src in own[stage, half]
        ]

    def swap(*units, deps=()):
        both = jnp.concatenate([a for t in (own, side) for u in units for a in t[u]], axis=0)
        got = lax.ppermute(after(both, *deps) if deps else both, AXES, beside(1))
        other.setdefault(units[0][0], []).append(got)

    def blocks_of(unit):
        start = unit[0] * hi_n + unit[1] * per
        return range(start, start + per)

    def weigh(row_units, stages, sums=(), dups=(), last=True, deps=()):
        nrows = len(row_units) * unit
        layout, cols = [], []
        for g in stages:
            cs = own[g, 0] + own[g, 1] + side[g, 0] + side[g, 1]
            layout.append((g, len(cs)))
            cols += cs
        for g in stages:
            layout.append((None, len(other[g])))
            cols += other[g]
        total = sum(c.shape[0] for c in cols)
        row_in = [a for u in row_units for a in own[u]]
        if deps:
            row_in[0] = after(row_in[0], *deps)
        row_stage = [(g, h, len(own[g, h])) for g, h in row_units]
        ks = [k for u in row_units for k in blocks_of(u)]
        acc = [(nrows, width), (nrows, 128)]
        ins = row_in + cols + list(sums) + list(dups)
        if last:
            out_shape = [block] * len(ks) + [jax.ShapeDtypeStruct((nb, 128), jnp.float32)]
        else:
            out_shape = [jax.ShapeDtypeStruct(t, jnp.float32) for t in acc]
        return pl.pallas_call(
            functools.partial(
                weigh_kernel,
                layout,
                row_stage,
                unit,
                slots,
                ng,
                [hops[k] for k in ks],
                bool(sums),
                bool(dups),
                last,
            ),
            out_shape=out_shape,
            in_specs=[vmem] * len(ins),
            out_specs=[vmem] * len(out_shape),
            scratch_shapes=[pltpu.VMEM(t, jnp.float32) for t in acc] if last else [],
            compiler_params=pltpu.CompilerParams(vmem_limit_bytes=32 * MIB),
            cost_estimate=pl.CostEstimate(
                flops=4 * nrows * total * width,
                bytes_accessed=2 * total * width,
                transcendentals=nrows * total,
            ),
            name="weigh",
        )(*ins)

    send(0, 0)
    send(1, 0)
    send(1, 1)
    send(2, 0)
    send(0, 1)
    across(0, 0, *own[1, 0])
    across(0, 1)
    across(1, 0)
    across(1, 1, *side[0, 0])
    send(2, 1, *own[1, 0])
    send(3, 0, *own[1, 1])
    send(3, 1, *own[2, 0])
    across(2, 0, *side[1, 0], *side[0, 1])
    across(2, 1, *side[1, 1])
    across(3, 0, *side[2, 0])
    across(3, 1, *side[2, 1])
    swap((0, 0), (0, 1))
    swap((1, 0), (1, 1))
    swap((2, 0), (2, 1))
    swap((3, 0))
    parts = [[(1, 0), (1, 1)], [(2, 0), (2, 1)], [(3, 0), (3, 1), (0, 1), (0, 0)]]
    stages = list(range(nstage))
    swap((3, 1))
    early, sums = [], ()
    result = [None] * nb
    order, dups, deps = [], (), ()
    for part in parts:
        todo = [g for g in stages if g not in early]
        *outs, dup = weigh(part, todo, sums, dups, deps=deps)
        early, sums, dups, deps = [], (), (dup,), outs[:1]
        blocks = [k for u in part for k in blocks_of(u)]
        for k, r in zip(blocks, outs):
            result[k] = r
        order += blocks
    back = [result[0]] + [None] * (nb - 1)
    for b in order:
        if b:
            back[b] = lax.ppermute(result[b], AXES, to_owner(*hops[b], -1))

    same = [
        [((h * ng + lo) * ng) + z for h in range(hi_n) for z in range(ng)] for lo in range(ng)
    ]
    dups = lax.all_to_all(*dups, AXES, 0, 0, tiled=True, axis_index_groups=same)

    def unpack(which, also, last):
        near = jax.ShapeDtypeStruct((n, width), jnp.float32)
        scratch = [pltpu.VMEM((n, width), jnp.float32), pltpu.SemaphoreType.DMA((4,))]
        return pl.pallas_call(
            functools.partial(unpack_kernel, slots, which, last, hi_n, ng),
            out_shape=[near] if last else [jax.ShapeDtypeStruct((1, n), jnp.float32), near],
            in_specs=[vmem] * (2 + len(which)),
            out_specs=[hbm] if last else [vmem, vmem],
            scratch_shapes=scratch if last else [],
            compiler_params=pltpu.CompilerParams(vmem_limit_bytes=16 * MIB),
            name="unpack",
        )(pos, *[back[k] for k in which], also)

    late = [k for u in parts[2][:3] for k in blocks_of(u)]
    dup, near = unpack([b for b in range(nb) if b not in late], dups, False)
    (near,) = unpack(late, near, True)
    return dup.reshape(n), near


def solution(mesh):
    return jax.shard_map(
        local,
        mesh=mesh,
        in_specs=(P(("shard", "grp"), None), P(("shard", "grp"), None)),
        out_specs=(P(("shard", "grp")), P(("shard", "grp"), None)),
        check_vma=False,
    )
```

time: 339 us -> 127 us (0.37)
  waiting for transfers between devices: 151 us -> 35.6 us
  local copies, waits for them, and re-layouts: 71.8 us -> 2.27 us
  matrix products: 34.6 us -> 0 us
  starting transfers between devices: 11.6 us -> 46.1 us
  blocking collectives: 48.2 us -> 15.2 us
  Pallas kernels: 0 us -> 26.5 us
  between operations: 14.1 us -> 0.96 us
  other arithmetic: 7.54 us -> 0.28 us
    all_gather x1 -> x0, waiting for transfers between devices: 102 us -> none  [local(): piece_unit = lax.all_gather(own_unit, 'grp', axis=0, tiled=True)]
    scatter x2 -> x0, local copies, waits for them, and re-layouts: 55.6 us -> none  [the longest x1 33 us: local(): jnp.zeros((nclus, slots, width), jnp.bfloat16).at[ids, rank].set(units)]
    all_to_all x3 -> x0, waiting for transfers between devices: 49 us -> none  [the longest x1 44.5 us: local(): lax.all_to_all(near_rows.reshape(nclus, slots, width), 'shard', split_axi...]
    ppermute x0 -> x27, starting transfers between devices: none -> 46.1 us  [the longest x7 19.6 us: local(): back[b] = lax.ppermute(result[b], AXES, to_owner(*hops[b], -1))]
    ppermute x0 -> x27, waiting for transfers between devices: none -> 35.6 us  [the longest x8 21 us: across(): lax.ppermute(after(src, *deps) if deps else src, AXES, beside(2))]
    dot_general x2 -> x0, matrix products: 34.6 us -> none  [the longest x1 18.1 us: row_terms(): jnp.dot(rows_unit, cols_unit.T, preferred_element_type=jnp.float32)]
    pallas_call x0 -> x7, Pallas kernels: none -> 26.5 us  [the longest x3 22 us: weigh(): pl.pallas_call(functools.partial(weigh_kernel, layout, row_stage, unit, s...]
    all_gather x1 -> x0, blocking collectives: 16.5 us -> none  [local(): piece_flag = lax.all_gather(own_flag, 'grp', axis=0, tiled=True)]
  transfers between devices with their start and end apart: 4 -> 27, of which waited for: 3 -> 12; matrix products, arithmetic and copies ran while one was open for 13% -> 0% of each run, Pallas kernels for 0% -> 14%
where the time goes in v3:
time: 127 us
  starting transfers between devices  46.1 us (36%)
  waiting for transfers between devices  35.6 us (28%)
  Pallas kernels  26.5 us (21%)
  blocking collectives  15.2 us (12%)
  local copies, waits for them, and re-layouts  2.27 us (2%)
    pallas_call x3, Pallas kernels, weigh(): pl.pallas_call(functools.partial(weigh_kernel, layout, row_stage, unit, s...  22 us
    ppermute x8, waiting for transfers between devices, across(): lax.ppermute(after(src, *deps) if deps else src, AXES, beside(2))  21 us
    ppermute x7, starting transfers between devices, local(): back[b] = lax.ppermute(result[b], AXES, to_owner(*hops[b], -1))  19.6 us
    ppermute x7, starting transfers between devices, send(): lax.ppermute(after(src, *deps) if deps else src, AXES, to_owner(*hops[k],...  15.6 us
    all_to_all x1, blocking collectives, local(): dups = lax.all_to_all(*dups, AXES, 0, 0, tiled=True, axis_index_groups=same)  15.2 us
    ppermute x7, waiting for transfers between devices, send(): lax.ppermute(after(src, *deps) if deps else src, AXES, to_owner(*hops[k],...  12.7 us
    ppermute x8, starting transfers between devices, across(): lax.ppermute(after(src, *deps) if deps else src, AXES, beside(2))  10.6 us
    pallas_call x2, Pallas kernels, unpack(): pl.pallas_call(functools.partial(unpack_kernel, slots, which, last, hi_n,...  2.84 us
  transfers between devices with their start and end apart: 27, of which 12 were waited for; matrix products, arithmetic and copies ran while one was open for 0% of the time, Pallas kernels for 14%

profile of v3, /device:TPU:0, one launch (start us, length us, event | category | flops | bytes accessed | tf_op | source)
XLA Modules:
  0.0 127.0 jit_solution(8575316743144694474)
XLA Ops:
  0.6 1.6 %copy-done = f32[512,1024]{1,0:T(8,128)S(1)} copy-done((f32[512,1024]{1,0:T(8,128)S(1)}, f32[512,1024]{1,0:T(8,128)}, u32[]{:S(2)}) %copy-start) | copy-done | bytes 2097176
  2.2 0.7 copy-done.1
  2.9 0.7 pack.1
  3.6 3.1 %collective-permute-start.3 = (bf16[128,1024]{1,0:T(8,128)(2,1)S(1)}, bf16[128,1024]{1,0:T(8,128)(2,1)S(1)}, u32[]{:S(2)}, u32[]{:S(2)}) collective-permute-start(bf16[128,1024]{1,0:T(8,128)(2,1)S(1)} %get-tuple-element.44), channel_id=1, source_target_pairs={{0,1},{1,2},{2,3},{3,0},{4,5},{5,6},{6,7},{7,4},{8,9},{9,10},{10,1... | collective-permute-start | bytes 786440 | tf_op jit(solution)/shard_map/ppermute | solution.py:244
  6.7 2.5 %collective-permute-start = (bf16[128,1024]{1,0:T(8,128)(2,1)S(1)}, bf16[128,1024]{1,0:T(8,128)(2,1)S(1)}, u32[]{:S(2)}, u32[]{:S(2)}) collective-permute-start(bf16[128,1024]{1,0:T(8,128)(2,1)S(1)} %get-tuple-element.41), channel_id=1, source_target_pairs={{0,17},{1,18},{2,19},{3,16},{4,21},{5,22},{6,23},{7,20},{8,25},{9,... | collective-permute-start | bytes 786440 | tf_op jit(solution)/shard_map/ppermute | solution.py:244
  9.2 1.0 pack_rest.1
  10.3 0.6 collective-permute-start.4
  10.8 5.0 %collective-permute-done.3.refs_0_.refs_6_.refs_8_ = bf16[128,1024]{1,0:T(8,128)(2,1)S(1)} collective-permute-done((bf16[128,1024]{1,0:T(8,128)(2,1)S(1)}, bf16[128,1024]{1,0:T(8,128)(2,1)S(1)}, u32[]{:S(2)}, u32[]{:S(2)}) %collective-permute-start.3) | collective-permute-done | bytes 262176 | tf_op jit(solution)/shard_map/ppermute | solution.py:244
  15.8 1.7 %collective-permute-start.5 = (bf16[128,1024]{1,0:T(8,128)(2,1)S(1)}, bf16[128,1024]{1,0:T(8,128)(2,1)S(1)}, u32[]{:S(2)}, u32[]{:S(2)}) collective-permute-start(bf16[128,1024]{1,0:T(8,128)(2,1)S(1)} %get-tuple-element.47.refs_2_.refs_3_.refs_4_), channel_id=1, source_target_pairs={{0,8},{1,9},{2,10},{3,11},{4,12},{5,13},{6,14},{7,15},{8,0},{9,1},... | collective-permute-start | bytes 786440 | tf_op jit(solution)/shard_map/ppermute | solution.py:254
  17.6 1.8 %collective-permute-start.2 = (bf16[128,1024]{1,0:T(8,128)(2,1)S(1)}, bf16[128,1024]{1,0:T(8,128)(2,1)S(1)}, u32[]{:S(2)}, u32[]{:S(2)}) collective-permute-start(bf16[128,1024]{1,0:T(8,128)(2,1)S(1)} %get-tuple-element.43), channel_id=1, source_target_pairs={{0,3},{1,0},{2,1},{3,2},{4,7},{5,4},{6,5},{7,6},{8,11},{9,8},{10,9... | collective-permute-start | bytes 786440 | tf_op jit(solution)/shard_map/ppermute | solution.py:244
  19.4 0.5 collective-permute-start.7
  19.9 3.5 %collective-permute-done.4.refs_3_.refs_2_.refs_5_ = bf16[128,1024]{1,0:T(8,128)(2,1)S(1)} collective-permute-done((bf16[128,1024]{1,0:T(8,128)(2,1)S(1)}, bf16[128,1024]{1,0:T(8,128)(2,1)S(1)}, u32[]{:S(2)}, u32[]{:S(2)}) %collective-permute-start.4) | collective-permute-done | bytes 262176 | tf_op jit(solution)/shard_map/ppermute | solution.py:244
  23.4 1.5 %collective-permute-start.6 = (bf16[128,1024]{1,0:T(8,128)(2,1)S(1)}, bf16[128,1024]{1,0:T(8,128)(2,1)S(1)}, u32[]{:S(2)}, u32[]{:S(2)}) collective-permute-start(bf16[128,1024]{1,0:T(8,128)(2,1)S(1)} %collective-permute-done.4.refs_3_.refs_2_.refs_5_), channel_id=1, source_target_pairs={{0,8},{1,9},{2,10},{3,11},{4,12},{5,13},{6,14},{7,15},{8,0},{9,1},... | collective-permute-start | bytes 786440 | tf_op jit(solution)/shard_map/ppermute | solution.py:254
  24.9 0.0 collective-permute-done.refs_1_.refs_7_.refs_9_
  24.9 4.0 %collective-permute-start.9 = (bf16[128,1024]{1,0:T(8,128)(2,1)S(1)}, bf16[128,1024]{1,0:T(8,128)(2,1)S(1)}, u32[]{:S(2)}, u32[]{:S(2)}) collective-permute-start(bf16[128,1024]{1,0:T(8,128)(2,1)S(1)} %get-tuple-element.50), channel_id=1, source_target_pairs={{0,19},{1,16},{2,17},{3,18},{4,23},{5,20},{6,21},{7,22},{8,27},{9,... | collective-permute-start | bytes 786440 | tf_op jit(solution)/shard_map/ppermute | solution.py:244
  28.9 0.0 collective-permute-done.5.refs_4_.refs_6_
  28.9 1.5 %collective-permute-start.8 = (bf16[128,1024]{1,0:T(8,128)(2,1)S(1)}, bf16[128,1024]{1,0:T(8,128)(2,1)S(1)}, u32[]{:S(2)}, u32[]{:S(2)}) collective-permute-start(bf16[128,1024]{1,0:T(8,128)(2,1)S(1)} %collective-permute-done.refs_1_.refs_7_.refs_9_), channel_id=1, source_target_pairs={{0,8},{1,9},{2,10},{3,11},{4,12},{5,13},{6,14},{7,15},{8,0},{9,1},... | collective-permute-start | bytes 786440 | tf_op jit(solution)/shard_map/ppermute | solution.py:254
  30.4 0.0 collective-permute-done.2.refs_10_.refs_0_.refs_12_
  30.4 0.0 collective-permute-start.1
  30.4 0.3 collective-permute-done.7.refs_8_.refs_10_
  30.7 3.6 %collective-permute-start.12 = (bf16[128,1024]{1,0:T(8,128)(2,1)S(1)}, bf16[128,1024]{1,0:T(8,128)(2,1)S(1)}, u32[]{:S(2)}, u32[]{:S(2)}) collective-permute-start(bf16[128,1024]{1,0:T(8,128)(2,1)S(1)} %get-tuple-element.54), channel_id=1, source_target_pairs={{0,18},{1,19},{2,16},{3,17},{4,22},{5,23},{6,20},{7,21},{8,26},{9,... | collective-permute-start | bytes 786440 | tf_op jit(solution)/shard_map/ppermute | solution.py:244
  34.3 2.0 %collective-permute-done.6.refs_5_.refs_7_ = bf16[128,1024]{1,0:T(8,128)(2,1)S(1)} collective-permute-done((bf16[128,1024]{1,0:T(8,128)(2,1)S(1)}, bf16[128,1024]{1,0:T(8,128)(2,1)S(1)}, u32[]{:S(2)}, u32[]{:S(2)}) %collective-permute-start.6) | collective-permute-done | bytes 262176 | tf_op jit(solution)/shard_map/ppermute | solution.py:254
  36.3 1.7 %collective-permute-start.10 = (bf16[128,1024]{1,0:T(8,128)(2,1)S(1)}, bf16[128,1024]{1,0:T(8,128)(2,1)S(1)}, u32[]{:S(2)}, u32[]{:S(2)}) collective-permute-start(bf16[128,1024]{1,0:T(8,128)(2,1)S(1)} %collective-permute-done.2.refs_10_.refs_0_.refs_12_), channel_id=1, source_target_pairs={{0,8},{1,9},{2,10},{3,11},{4,12},{5,13},{6,14},{7,15},{8,0},{9,1},... | collective-permute-start | bytes 786440 | tf_op jit(solution)/shard_map/ppermute | solution.py:254
  38.1 0.0 collective-permute-done.9.refs_11_.refs_1_.refs_13_
  38.1 3.9 %collective-permute-done.8.refs_9_.refs_11_ = bf16[128,1024]{1,0:T(8,128)(2,1)S(1)} collective-permute-done((bf16[128,1024]{1,0:T(8,128)(2,1)S(1)}, bf16[128,1024]{1,0:T(8,128)(2,1)S(1)}, u32[]{:S(2)}, u32[]{:S(2)}) %collective-permute-start.8) | collective-permute-done | bytes 262176 | tf_op jit(solution)/shard_map/ppermute | solution.py:254
  41.9 1.7 %collective-permute-start.11 = (bf16[128,1024]{1,0:T(8,128)(2,1)S(1)}, bf16[128,1024]{1,0:T(8,128)(2,1)S(1)}, u32[]{:S(2)}, u32[]{:S(2)}) collective-permute-start(bf16[128,1024]{1,0:T(8,128)(2,1)S(1)} %collective-permute-done.9.refs_11_.refs_1_.refs_13_), channel_id=1, source_target_pairs={{0,8},{1,9},{2,10},{3,11},{4,12},{5,13},{6,14},{7,15},{8,0},{9,1},... | collective-permute-start | bytes 786440 | tf_op jit(solution)/shard_map/ppermute | solution.py:254
  43.7 0.1 pad_maximum_fusion
  43.7 0.1 collective-permute-start.15
  43.8 0.1 pad_maximum_fusion.1
  43.9 3.6 %collective-permute-done.10.refs_12_.refs_14_ = bf16[128,1024]{1,0:T(8,128)(2,1)S(1)} collective-permute-done((bf16[128,1024]{1,0:T(8,128)(2,1)S(1)}, bf16[128,1024]{1,0:T(8,128)(2,1)S(1)}, u32[]{:S(2)}, u32[]{:S(2)}) %collective-permute-start.10) | collective-permute-done | bytes 262176 | tf_op jit(solution)/shard_map/ppermute | solution.py:254
  47.5 0.0 collective-permute-start.16
  47.6 3.0 %collective-permute-done.11.refs_13_.refs_15_ = bf16[128,1024]{1,0:T(8,128)(2,1)S(1)} collective-permute-done((bf16[128,1024]{1,0:T(8,128)(2,1)S(1)}, bf16[128,1024]{1,0:T(8,128)(2,1)S(1)}, u32[]{:S(2)}, u32[]{:S(2)}) %collective-permute-start.11) | collective-permute-done | bytes 262176 | tf_op jit(solution)/shard_map/ppermute | solution.py:254
  50.6 0.1 pad_maximum_fusion.2
  50.7 0.1 collective-permute-start.17
  50.7 1.3 %collective-permute-done.1.refs_14_.refs_0_.refs_16_ = bf16[128,1024]{1,0:T(8,128)(2,1)S(1)} collective-permute-done((bf16[128,1024]{1,0:T(8,128)(2,1)S(1)}, bf16[128,1024]{1,0:T(8,128)(2,1)S(1)}, u32[]{:S(2)}, u32[]{:S(2)}) %collective-permute-start.1) | collective-permute-done | bytes 262176 | tf_op jit(solution)/shard_map/ppermute | solution.py:244
  52.0 1.1 collective-permute-start.13
  53.2 2.9 %collective-permute-done.12.refs_15_.refs_1_.refs_17_ = bf16[128,1024]{1,0:T(8,128)(2,1)S(1)} collective-permute-done((bf16[128,1024]{1,0:T(8,128)(2,1)S(1)}, bf16[128,1024]{1,0:T(8,128)(2,1)S(1)}, u32[]{:S(2)}, u32[]{:S(2)}) %collective-permute-start.12) | collective-permute-done | bytes 262176 | tf_op jit(solution)/shard_map/ppermute | solution.py:244
  56.1 0.7 collective-permute-start.14
  56.8 4.5 %collective-permute-done.13.refs_16_.refs_18_ = bf16[128,1024]{1,0:T(8,128)(2,1)S(1)} collective-permute-done((bf16[128,1024]{1,0:T(8,128)(2,1)S(1)}, bf16[128,1024]{1,0:T(8,128)(2,1)S(1)}, u32[]{:S(2)}, u32[]{:S(2)}) %collective-permute-start.13) | collective-permute-done | bytes 262176 | tf_op jit(solution)/shard_map/ppermute | solution.py:254
  61.3 0.1 collective-permute-start.18
  61.4 3.7 %collective-permute-done.14.refs_17_.refs_19_ = bf16[128,1024]{1,0:T(8,128)(2,1)S(1)} collective-permute-done((bf16[128,1024]{1,0:T(8,128)(2,1)S(1)}, bf16[128,1024]{1,0:T(8,128)(2,1)S(1)}, u32[]{:S(2)}, u32[]{:S(2)}) %collective-permute-start.14) | collective-permute-done | bytes 262176 | tf_op jit(solution)/shard_map/ppermute | solution.py:254
  65.1 0.1 collective-permute-start.19
  65.2 0.0 collective-permute-done.18.refs_21_.refs_23_
  65.2 0.0 collective-permute-done.15.refs_18_.refs_20_
  65.2 1.9 %collective-permute-done.19.refs_22_.refs_24_ = bf16[256,1024]{1,0:T(8,128)(2,1)S(1)} collective-permute-done((bf16[256,1024]{1,0:T(8,128)(2,1)S(1)}, bf16[256,1024]{1,0:T(8,128)(2,1)S(1)}, u32[]{:S(2)}, u32[]{:S(2)}) %collective-permute-start.19) | collective-permute-done | bytes 524320 | tf_op jit(solution)/shard_map/ppermute | solution.py:260
  67.1 0.0 collective-permute-done.16.refs_19_.refs_21_
  67.1 0.0 collective-permute-done.17.refs_20_.refs_22_
  67.1 5.8 %weigh.3 = (bf16[128,1024]{1,0:T(8,128)(2,1)S(1)}, bf16[128,1024]{1,0:T(8,128)(2,1)S(1)}, f32[8,128]{1,0:T(8,128)S(1)}) custom-call(bf16[128,1024]{1,0:T(8,128)(2,1)S(1)} %collective-permute-done.3.refs_0_.refs_6_.refs_8_, bf16[128,1024]{1,0:T(8,128)(2,1)S(1)} %collective-permute-done.refs_1_.refs_7_.refs_9_, ...), custom_call_target="tpu_custom_call" | custom-call | flops 4294967296 | bytes 8388608 | tf_op jit(solution)/shard_map/weigh/pallas_call | solution.py:289
  72.9 1.5 %collective-permute-start.20 = (bf16[128,1024]{1,0:T(8,128)(2,1)S(1)}, bf16[128,1024]{1,0:T(8,128)(2,1)S(1)}, u32[]{:S(2)}, u32[]{:S(2)}) collective-permute-start(bf16[128,1024]{1,0:T(8,128)(2,1)S(1)} %get-tuple-element.57), channel_id=1, source_target_pairs={{0,3},{1,0},{2,1},{3,2},{4,7},{5,4},{6,5},{7,6},{8,11},{9,8},{10,9... | collective-permute-start | bytes 786440 | tf_op jit(solution)/shard_map/ppermute | solution.py:352
  74.4 2.7 %collective-permute-start.21 = (bf16[128,1024]{1,0:T(8,128)(2,1)S(1)}, bf16[128,1024]{1,0:T(8,128)(2,1)S(1)}, u32[]{:S(2)}, u32[]{:S(2)}) collective-permute-start(bf16[128,1024]{1,0:T(8,128)(2,1)S(1)} %get-tuple-element.64), channel_id=1, source_target_pairs={{0,19},{1,16},{2,17},{3,18},{4,23},{5,20},{6,21},{7,22},{8,27},{9,... | collective-permute-start | bytes 786440 | tf_op jit(solution)/shard_map/ppermute | solution.py:352
  77.1 5.8 %weigh.4 = (bf16[128,1024]{1,0:T(8,128)(2,1)S(1)}, bf16[128,1024]{1,0:T(8,128)(2,1)S(1)}, f32[8,128]{1,0:T(8,128)S(1)}) custom-call(bf16[128,1024]{1,0:T(8,128)(2,1)S(1)} %collective-permute-done.2.refs_10_.refs_0_.refs_12_, bf16[128,1024]{1,0:T(8,128)(2,1)S(1)} %collective-permute-done.9.refs_11_.refs_1_.refs_13_, ...), custom_call_target="tpu_custom_call" | custom-call | flops 4294967296 | bytes 8388608 | tf_op jit(solution)/shard_map/weigh/pallas_call | solution.py:289
  83.0 0.4 collective-permute-start.22
  83.3 2.4 %collective-permute-start.23 = (bf16[128,1024]{1,0:T(8,128)(2,1)S(1)}, bf16[128,1024]{1,0:T(8,128)(2,1)S(1)}, u32[]{:S(2)}, u32[]{:S(2)}) collective-permute-start(bf16[128,1024]{1,0:T(8,128)(2,1)S(1)} %get-tuple-element.65), channel_id=1, source_target_pairs={{0,17},{1,18},{2,19},{3,16},{4,21},{5,22},{6,23},{7,20},{8,25},{9,... | collective-permute-start | bytes 786440 | tf_op jit(solution)/shard_map/ppermute | solution.py:352
  85.7 10.3 %weigh.5 = (bf16[128,1024]{1,0:T(8,128)(2,1)S(1)}, bf16[128,1024]{1,0:T(8,128)(2,1)S(1)}, bf16[128,1024]{1,0:T(8,128)(2,1)S(1)}, bf16[128,1024]{1,0:T(8,128)(2,1)S(1)}, f32[8,128]{1,0:T(8,128)S(1)}) custom-call(bf16[128,1024]{1,0:T(8,128)(2,1)S(1)} %collective-permute-done.1.refs_14_.refs_0_.refs_16_, ...), custom_call_target="tpu_custom_call" | custom-call | flops 8589934592 | bytes 8388608 | tf_op jit(solution)/shard_map/weigh/pallas_call | solution.py:289
  96.0 1.8 %collective-permute-start.24 = (bf16[128,1024]{1,0:T(8,128)(2,1)S(1)}, bf16[128,1024]{1,0:T(8,128)(2,1)S(1)}, u32[]{:S(2)}, u32[]{:S(2)}) collective-permute-start(bf16[128,1024]{1,0:T(8,128)(2,1)S(1)} %get-tuple-element.68), channel_id=1, source_target_pairs={{0,2},{1,3},{2,0},{3,1},{4,6},{5,7},{6,4},{7,5},{8,10},{9,11},{10,... | collective-permute-start | bytes 786440 | tf_op jit(solution)/shard_map/ppermute | solution.py:352
  97.8 0.0 collective-permute-done.21.refs_2_
  97.8 9.5 %collective-permute-start.25 = (bf16[128,1024]{1,0:T(8,128)(2,1)S(1)}, bf16[128,1024]{1,0:T(8,128)(2,1)S(1)}, u32[]{:S(2)}, u32[]{:S(2)}) collective-permute-start(bf16[128,1024]{1,0:T(8,128)(2,1)S(1)} %get-tuple-element.69), channel_id=1, source_target_pairs={{0,18},{1,19},{2,16},{3,17},{4,22},{5,23},{6,20},{7,21},{8,26},{9,... | collective-permute-start | bytes 786440 | tf_op jit(solution)/shard_map/ppermute | solution.py:352
  107.3 0.0 collective-permute-done.20.refs_1_
  107.3 1.4 %collective-permute-start.26 = (bf16[128,1024]{1,0:T(8,128)(2,1)S(1)}, bf16[128,1024]{1,0:T(8,128)(2,1)S(1)}, u32[]{:S(2)}, u32[]{:S(2)}) collective-permute-start(bf16[128,1024]{1,0:T(8,128)(2,1)S(1)} %get-tuple-element.70), channel_id=1, source_target_pairs={{0,16},{1,17},{2,18},{3,19},{4,20},{5,21},{6,22},{7,23},{8,24},{9,... | collective-permute-start | bytes 786440 | tf_op jit(solution)/shard_map/ppermute | solution.py:352
  108.7 15.2 %all_to_all.11 = f32[8,1,128]{2,1,0:T(1,128)S(1)} all-to-all(f32[8,1,128]{2,1,0:T(1,128)S(1)} %bitcast.7), channel_id=1, replica_groups={{0,1,2,3,16,17,18,19},{4,5,6,7,20,21,22,23},{8,9,10,11,24,25,26,27},{12..., dimensions={0} | all-to-all | bytes 8192 | tf_op jit(solution)/shard_map/all_to_all | solution.py:357
  123.9 0.0 collective-permute-done.23.refs_4_
  124.0 1.2 unpack.2
  125.1 0.0 collective-permute-done.24.refs_0_
  125.1 1.7 %unpack.3 = f32[512,1024]{1,0:T(8,128)} custom-call(s32[1,512]{1,0:T(1,128)S(1)} %get-tuple-element.37.pos_ref, bf16[128,1024]{1,0:T(8,128)(2,1)S(1)} %collective-permute-done.24.refs_0_, bf16[128,1024]{1,0:T(8,128)(2,1)S(1)} %collective-permute-done.25.refs_1_, bf16[128,1024]{1,0:T(8,128)(2,1)S(1)} %collective-permute-done.26.refs_2_, ...), custom_call_target="tpu_custom_call" | custom-call | tf_op jit(solution)/shard_map/unpack/pallas_call | solution.py:362
  (7 shorter events, 0.1 us)
Async XLA Ops:
  0.6 1.6 %copy-start = (f32[512,1024]{1,0:T(8,128)S(1)}, f32[512,1024]{1,0:T(8,128)}, u32[]{:S(2)}) copy-start(f32[512,1024]{1,0:T(8,128)} %emb_ref.1) | copy-start | bytes 6291460
  2.2 0.7 copy-start.1
  3.6 12.2 %collective-permute-start.3 = (bf16[128,1024]{1,0:T(8,128)(2,1)S(1)}, bf16[128,1024]{1,0:T(8,128)(2,1)S(1)}, u32[]{:S(2)}, u32[]{:S(2)}) collective-permute-start(bf16[128,1024]{1,0:T(8,128)(2,1)S(1)} %get-tuple-element.44), channel_id=1, source_target_pairs={{0,1},{1,2},{2,3},{3,0},{4,5},{5,6},{6,7},{7,4},{8,9},{9,10},{10,1... | collective-permute-start | bytes 786440 | tf_op jit(solution)/shard_map/ppermute | solution.py:244
  6.7 18.2 %collective-permute-start = (bf16[128,1024]{1,0:T(8,128)(2,1)S(1)}, bf16[128,1024]{1,0:T(8,128)(2,1)S(1)}, u32[]{:S(2)}, u32[]{:S(2)}) collective-permute-start(bf16[128,1024]{1,0:T(8,128)(2,1)S(1)} %get-tuple-element.41), channel_id=1, source_target_pairs={{0,17},{1,18},{2,19},{3,16},{4,21},{5,22},{6,23},{7,20},{8,25},{9,... | collective-permute-start | bytes 786440 | tf_op jit(solution)/shard_map/ppermute | solution.py:244
  10.3 13.2 %collective-permute-start.4 = (bf16[128,1024]{1,0:T(8,128)(2,1)S(1)}, bf16[128,1024]{1,0:T(8,128)(2,1)S(1)}, u32[]{:S(2)}, u32[]{:S(2)}) collective-permute-start(bf16[128,1024]{1,0:T(8,128)(2,1)S(1)} %get-tuple-element.46), channel_id=1, source_target_pairs={{0,16},{1,17},{2,18},{3,19},{4,20},{5,21},{6,22},{7,23},{8,24},{9,... | collective-permute-start | bytes 786440 | tf_op jit(solution)/shard_map/ppermute | solution.py:244
  15.8 13.1 %collective-permute-start.5 = (bf16[128,1024]{1,0:T(8,128)(2,1)S(1)}, bf16[128,1024]{1,0:T(8,128)(2,1)S(1)}, u32[]{:S(2)}, u32[]{:S(2)}) collective-permute-start(bf16[128,1024]{1,0:T(8,128)(2,1)S(1)} %get-tuple-element.47.refs_2_.refs_3_.refs_4_), channel_id=1, source_target_pairs={{0,8},{1,9},{2,10},{3,11},{4,12},{5,13},{6,14},{7,15},{8,0},{9,1},... | collective-permute-start | bytes 786440 | tf_op jit(solution)/shard_map/ppermute | solution.py:254
  17.6 12.9 %collective-permute-start.2 = (bf16[128,1024]{1,0:T(8,128)(2,1)S(1)}, bf16[128,1024]{1,0:T(8,128)(2,1)S(1)}, u32[]{:S(2)}, u32[]{:S(2)}) collective-permute-start(bf16[128,1024]{1,0:T(8,128)(2,1)S(1)} %get-tuple-element.43), channel_id=1, source_target_pairs={{0,3},{1,0},{2,1},{3,2},{4,7},{5,4},{6,5},{7,6},{8,11},{9,8},{10,9... | collective-permute-start | bytes 786440 | tf_op jit(solution)/shard_map/ppermute | solution.py:244
  19.4 11.3 %collective-permute-start.7 = (bf16[128,1024]{1,0:T(8,128)(2,1)S(1)}, bf16[128,1024]{1,0:T(8,128)(2,1)S(1)}, u32[]{:S(2)}, u32[]{:S(2)}) collective-permute-start(bf16[128,1024]{1,0:T(8,128)(2,1)S(1)} %collective-permute-done.3.refs_0_.refs_6_.refs_8_), channel_id=1, source_target_pairs={{0,8},{1,9},{2,10},{3,11},{4,12},{5,13},{6,14},{7,15},{8,0},{9,1},... | collective-permute-start | bytes 786440 | tf_op jit(solution)/shard_map/ppermute | solution.py:254
  23.4 12.9 %collective-permute-start.6 = (bf16[128,1024]{1,0:T(8,128)(2,1)S(1)}, bf16[128,1024]{1,0:T(8,128)(2,1)S(1)}, u32[]{:S(2)}, u32[]{:S(2)}) collective-permute-start(bf16[128,1024]{1,0:T(8,128)(2,1)S(1)} %collective-permute-done.4.refs_3_.refs_2_.refs_5_), channel_id=1, source_target_pairs={{0,8},{1,9},{2,10},{3,11},{4,12},{5,13},{6,14},{7,15},{8,0},{9,1},... | collective-permute-start | bytes 786440 | tf_op jit(solution)/shard_map/ppermute | solution.py:254
  24.9 13.1 %collective-permute-start.9 = (bf16[128,1024]{1,0:T(8,128)(2,1)S(1)}, bf16[128,1024]{1,0:T(8,128)(2,1)S(1)}, u32[]{:S(2)}, u32[]{:S(2)}) collective-permute-start(bf16[128,1024]{1,0:T(8,128)(2,1)S(1)} %get-tuple-element.50), channel_id=1, source_target_pairs={{0,19},{1,16},{2,17},{3,18},{4,23},{5,20},{6,21},{7,22},{8,27},{9,... | collective-permute-start | bytes 786440 | tf_op jit(solution)/shard_map/ppermute | solution.py:244
  28.9 13.0 %collective-permute-start.8 = (bf16[128,1024]{1,0:T(8,128)(2,1)S(1)}, bf16[128,1024]{1,0:T(8,128)(2,1)S(1)}, u32[]{:S(2)}, u32[]{:S(2)}) collective-permute-start(bf16[128,1024]{1,0:T(8,128)(2,1)S(1)} %collective-permute-done.refs_1_.refs_7_.refs_9_), channel_id=1, source_target_pairs={{0,8},{1,9},{2,10},{3,11},{4,12},{5,13},{6,14},{7,15},{8,0},{9,1},... | collective-permute-start | bytes 786440 | tf_op jit(solution)/shard_map/ppermute | solution.py:254
  30.4 21.6 %collective-permute-start.1 = (bf16[128,1024]{1,0:T(8,128)(2,1)S(1)}, bf16[128,1024]{1,0:T(8,128)(2,1)S(1)}, u32[]{:S(2)}, u32[]{:S(2)}) collective-permute-start(bf16[128,1024]{1,0:T(8,128)(2,1)S(1)} %get-tuple-element.42), channel_id=1, source_target_pairs={{0,2},{1,3},{2,0},{3,1},{4,6},{5,7},{6,4},{7,5},{8,10},{9,11},{10,... | collective-permute-start | bytes 786440 | tf_op jit(solution)/shard_map/ppermute | solution.py:244
  30.7 25.4 %collective-permute-start.12 = (bf16[128,1024]{1,0:T(8,128)(2,1)S(1)}, bf16[128,1024]{1,0:T(8,128)(2,1)S(1)}, u32[]{:S(2)}, u32[]{:S(2)}) collective-permute-start(bf16[128,1024]{1,0:T(8,128)(2,1)S(1)} %get-tuple-element.54), channel_id=1, source_target_pairs={{0,18},{1,19},{2,16},{3,17},{4,22},{5,23},{6,20},{7,21},{8,26},{9,... | collective-permute-start | bytes 786440 | tf_op jit(solution)/shard_map/ppermute | solution.py:244
  36.3 11.2 %collective-permute-start.10 = (bf16[128,1024]{1,0:T(8,128)(2,1)S(1)}, bf16[128,1024]{1,0:T(8,128)(2,1)S(1)}, u32[]{:S(2)}, u32[]{:S(2)}) collective-permute-start(bf16[128,1024]{1,0:T(8,128)(2,1)S(1)} %collective-permute-done.2.refs_10_.refs_0_.refs_12_), channel_id=1, source_target_pairs={{0,8},{1,9},{2,10},{3,11},{4,12},{5,13},{6,14},{7,15},{8,0},{9,1},... | collective-permute-start | bytes 786440 | tf_op jit(solution)/shard_map/ppermute | solution.py:254
  41.9 8.7 %collective-permute-start.11 = (bf16[128,1024]{1,0:T(8,128)(2,1)S(1)}, bf16[128,1024]{1,0:T(8,128)(2,1)S(1)}, u32[]{:S(2)}, u32[]{:S(2)}) collective-permute-start(bf16[128,1024]{1,0:T(8,128)(2,1)S(1)} %collective-permute-done.9.refs_11_.refs_1_.refs_13_), channel_id=1, source_target_pairs={{0,8},{1,9},{2,10},{3,11},{4,12},{5,13},{6,14},{7,15},{8,0},{9,1},... | collective-permute-start | bytes 786440 | tf_op jit(solution)/shard_map/ppermute | solution.py:254
  43.7 21.5 %collective-permute-start.15 = (bf16[512,1024]{1,0:T(8,128)(2,1)S(1)}, bf16[512,1024]{1,0:T(8,128)(2,1)S(1)}, u32[]{:S(2)}, u32[]{:S(2)}) collective-permute-start(bf16[512,1024]{1,0:T(8,128)(2,1)S(1)} %pad_maximum_fusion), channel_id=1, source_target_pairs={{0,4},{1,5},{2,6},{3,7},{4,0},{5,1},{6,2},{7,3},{8,12},{9,13},{10,... | collective-permute-start | bytes 3145736 | tf_op jit(solution)/shard_map/ppermute | solution.py:260
  47.5 19.5 %collective-permute-start.16 = (bf16[512,1024]{1,0:T(8,128)(2,1)S(1)}, bf16[512,1024]{1,0:T(8,128)(2,1)S(1)}, u32[]{:S(2)}, u32[]{:S(2)}) collective-permute-start(bf16[512,1024]{1,0:T(8,128)(2,1)S(1)} %pad_maximum_fusion.1), channel_id=1, source_target_pairs={{0,4},{1,5},{2,6},{3,7},{4,0},{5,1},{6,2},{7,3},{8,12},{9,13},{10,... | collective-permute-start | bytes 3145736 | tf_op jit(solution)/shard_map/ppermute | solution.py:260
  50.7 16.4 %collective-permute-start.17 = (bf16[512,1024]{1,0:T(8,128)(2,1)S(1)}, bf16[512,1024]{1,0:T(8,128)(2,1)S(1)}, u32[]{:S(2)}, u32[]{:S(2)}) collective-permute-start(bf16[512,1024]{1,0:T(8,128)(2,1)S(1)} %pad_maximum_fusion.2), channel_id=1, source_target_pairs={{0,4},{1,5},{2,6},{3,7},{4,0},{5,1},{6,2},{7,3},{8,12},{9,13},{10,... | collective-permute-start | bytes 3145736 | tf_op jit(solution)/shard_map/ppermute | solution.py:260
  52.0 9.2 %collective-permute-start.13 = (bf16[128,1024]{1,0:T(8,128)(2,1)S(1)}, bf16[128,1024]{1,0:T(8,128)(2,1)S(1)}, u32[]{:S(2)}, u32[]{:S(2)}) collective-permute-start(bf16[128,1024]{1,0:T(8,128)(2,1)S(1)} %collective-permute-done.1.refs_14_.refs_0_.refs_16_), channel_id=1, source_target_pairs={{0,8},{1,9},{2,10},{3,11},{4,12},{5,13},{6,14},{7,15},{8,0},{9,1},... | collective-permute-start | bytes 786440 | tf_op jit(solution)/shard_map/ppermute | solution.py:254
  56.1 9.0 %collective-permute-start.14 = (bf16[128,1024]{1,0:T(8,128)(2,1)S(1)}, bf16[128,1024]{1,0:T(8,128)(2,1)S(1)}, u32[]{:S(2)}, u32[]{:S(2)}) collective-permute-start(bf16[128,1024]{1,0:T(8,128)(2,1)S(1)} %collective-permute-done.12.refs_15_.refs_1_.refs_17_), channel_id=1, source_target_pairs={{0,8},{1,9},{2,10},{3,11},{4,12},{5,13},{6,14},{7,15},{8,0},{9,1},... | collective-permute-start | bytes 786440 | tf_op jit(solution)/shard_map/ppermute | solution.py:254
  61.3 3.9 %collective-permute-start.18 = (bf16[256,1024]{1,0:T(8,128)(2,1)S(1)}, bf16[256,1024]{1,0:T(8,128)(2,1)S(1)}, u32[]{:S(2)}, u32[]{:S(2)}) collective-permute-start(bf16[256,1024]{1,0:T(8,128)(2,1)S(1)} %pad_maximum_fusion.3), channel_id=1, source_target_pairs={{0,4},{1,5},{2,6},{3,7},{4,0},{5,1},{6,2},{7,3},{8,12},{9,13},{10,... | collective-permute-start | bytes 1572872 | tf_op jit(solution)/shard_map/ppermute | solution.py:260
  65.1 2.0 %collective-permute-start.19 = (bf16[256,1024]{1,0:T(8,128)(2,1)S(1)}, bf16[256,1024]{1,0:T(8,128)(2,1)S(1)}, u32[]{:S(2)}, u32[]{:S(2)}) collective-permute-start(bf16[256,1024]{1,0:T(8,128)(2,1)S(1)} %pad_maximum_fusion.4), channel_id=1, source_target_pairs={{0,4},{1,5},{2,6},{3,7},{4,0},{5,1},{6,2},{7,3},{8,12},{9,13},{10,... | collective-permute-start | bytes 1572872 | tf_op jit(solution)/shard_map/ppermute | solution.py:260
  72.9 34.4 %collective-permute-start.20 = (bf16[128,1024]{1,0:T(8,128)(2,1)S(1)}, bf16[128,1024]{1,0:T(8,128)(2,1)S(1)}, u32[]{:S(2)}, u32[]{:S(2)}) collective-permute-start(bf16[128,1024]{1,0:T(8,128)(2,1)S(1)} %get-tuple-element.57), channel_id=1, source_target_pairs={{0,3},{1,0},{2,1},{3,2},{4,7},{5,4},{6,5},{7,6},{8,11},{9,8},{10,9... | collective-permute-start | bytes 786440 | tf_op jit(solution)/shard_map/ppermute | solution.py:352
  74.4 23.4 %collective-permute-start.21 = (bf16[128,1024]{1,0:T(8,128)(2,1)S(1)}, bf16[128,1024]{1,0:T(8,128)(2,1)S(1)}, u32[]{:S(2)}, u32[]{:S(2)}) collective-permute-start(bf16[128,1024]{1,0:T(8,128)(2,1)S(1)} %get-tuple-element.64), channel_id=1, source_target_pairs={{0,19},{1,16},{2,17},{3,18},{4,23},{5,20},{6,21},{7,22},{8,27},{9,... | collective-permute-start | bytes 786440 | tf_op jit(solution)/shard_map/ppermute | solution.py:352
  83.0 41.0 %collective-permute-start.22 = (bf16[128,1024]{1,0:T(8,128)(2,1)S(1)}, bf16[128,1024]{1,0:T(8,128)(2,1)S(1)}, u32[]{:S(2)}, u32[]{:S(2)}) collective-permute-start(bf16[128,1024]{1,0:T(8,128)(2,1)S(1)} %get-tuple-element.60), channel_id=1, source_target_pairs={{0,1},{1,2},{2,3},{3,0},{4,5},{5,6},{6,7},{7,4},{8,9},{9,10},{10,1... | collective-permute-start | bytes 786440 | tf_op jit(solution)/shard_map/ppermute | solution.py:352
  83.3 40.6 %collective-permute-start.23 = (bf16[128,1024]{1,0:T(8,128)(2,1)S(1)}, bf16[128,1024]{1,0:T(8,128)(2,1)S(1)}, u32[]{:S(2)}, u32[]{:S(2)}) collective-permute-start(bf16[128,1024]{1,0:T(8,128)(2,1)S(1)} %get-tuple-element.65), channel_id=1, source_target_pairs={{0,17},{1,18},{2,19},{3,16},{4,21},{5,22},{6,23},{7,20},{8,25},{9,... | collective-permute-start | bytes 786440 | tf_op jit(solution)/shard_map/ppermute | solution.py:352
  96.0 29.1 %collective-permute-start.24 = (bf16[128,1024]{1,0:T(8,128)(2,1)S(1)}, bf16[128,1024]{1,0:T(8,128)(2,1)S(1)}, u32[]{:S(2)}, u32[]{:S(2)}) collective-permute-start(bf16[128,1024]{1,0:T(8,128)(2,1)S(1)} %get-tuple-element.68), channel_id=1, source_target_pairs={{0,2},{1,3},{2,0},{3,1},{4,6},{5,7},{6,4},{7,5},{8,10},{9,11},{10,... | collective-permute-start | bytes 786440 | tf_op jit(solution)/shard_map/ppermute | solution.py:352
  97.8 27.3 %collective-permute-start.25 = (bf16[128,1024]{1,0:T(8,128)(2,1)S(1)}, bf16[128,1024]{1,0:T(8,128)(2,1)S(1)}, u32[]{:S(2)}, u32[]{:S(2)}) collective-permute-start(bf16[128,1024]{1,0:T(8,128)(2,1)S(1)} %get-tuple-element.69), channel_id=1, source_target_pairs={{0,18},{1,19},{2,16},{3,17},{4,22},{5,23},{6,20},{7,21},{8,26},{9,... | collective-permute-start | bytes 786440 | tf_op jit(solution)/shard_map/ppermute | solution.py:352
  107.3 17.8 %collective-permute-start.26 = (bf16[128,1024]{1,0:T(8,128)(2,1)S(1)}, bf16[128,1024]{1,0:T(8,128)(2,1)S(1)}, u32[]{:S(2)}, u32[]{:S(2)}) collective-permute-start(bf16[128,1024]{1,0:T(8,128)(2,1)S(1)} %get-tuple-element.70), channel_id=1, source_target_pairs={{0,16},{1,17},{2,18},{3,19},{4,20},{5,21},{6,22},{7,23},{8,24},{9,... | collective-permute-start | bytes 786440 | tf_op jit(solution)/shard_map/ppermute | solution.py:352

commit v4 on v3

--- a/solution.py
+++ b/solution.py
@@ -142,23 +142,12 @@
     picks = jnp.concatenate([pick(k) for k in which], axis=0)
     rows = jnp.concatenate([r[...] for r in refs[:nwhich]], axis=0)
     if not last:
-        dups, dup_ref, near_ref = refs[nwhich:]
-        hi, z = lax.axis_index("shard") // ng, lax.axis_index("grp")
-        line = lax.broadcasted_iota(jnp.int32, (8, 128), 0)
-        dup = jnp.zeros((8, n), jnp.float32)
-        for k, (dh, dz) in enumerate((dh, dz) for dz in hop_order(ng) for dh in range(hi_n)):
-            owner = lax.rem(hi + dh, hi_n) * ng + lax.rem(z + dz, ng)
-            row = jnp.broadcast_to(dups[pl.ds(owner, 1), :], (8, 128))
-            high = row.astype(jnp.bfloat16).astype(jnp.float32)
-            two = jnp.where(line == 0, high, jnp.where(line == 1, row - high, 0.0))
-            two = two.astype(jnp.bfloat16)[:, :slots]
-            dup = dup + jnp.dot(two, pick(k), preferred_element_type=jnp.float32)
-        dup_ref[...] = dup[0:1] + dup[1:2]
+        (near_ref,) = refs[nwhich:]
         near_ref[...] = lax.dot_general(
             picks, rows, (((0,), (0,)), ((), ())), preferred_element_type=jnp.float32
         )
         return
-    near_in, near_ref, near, sems = refs[nwhich:]
+    near_in, dups, near_ref, dup_ref, near, sems = refs[nwhich:]
     step = n // 4
     copies = []
     for i in range(4):
@@ -171,6 +160,17 @@
         )
         copies.append(pltpu.make_async_copy(near.at[at], near_ref.at[at], sems.at[i]))
         copies[-1].start()
+    hi, z = lax.axis_index("shard") // ng, lax.axis_index("grp")
+    line = lax.broadcasted_iota(jnp.int32, (8, 128), 0)
+    dup = jnp.zeros((8, n), jnp.float32)
+    for k, (dh, dz) in enumerate((dh, dz) for dz in hop_order(ng) for dh in range(hi_n)):
+        owner = lax.rem(hi + dh, hi_n) * ng + lax.rem(z + dz, ng)
+        row = jnp.broadcast_to(dups[pl.ds(owner, 1), :], (8, 128))
+        high = row.astype(jnp.bfloat16).astype(jnp.float32)
+        two = jnp.where(line == 0, high, jnp.where(line == 1, row - high, 0.0))
+        two = two.astype(jnp.bfloat16)[:, :slots]
+        dup = dup + jnp.dot(two, pick(k), preferred_element_type=jnp.float32)
+    dup_ref[...] = dup[0:1] + dup[1:2]
     for c in copies:
         c.wait()
 
@@ -259,6 +259,11 @@
         both = jnp.concatenate([a for t in (own, side) for u in units for a in t[u]], axis=0)
         got = lax.ppermute(after(both, *deps) if deps else both, AXES, beside(1))
         other.setdefault(units[0][0], []).append(got)
+
+    def pieces(g):
+        other[g] = [
+            lax.ppermute(a, AXES, beside(1)) for t in (own, side) for h in range(2) for a in t[g, h]
+        ]
 
     def blocks_of(unit):
         start = unit[0] * hi_n + unit[1] * per
@@ -305,9 +310,9 @@
             scratch_shapes=[pltpu.VMEM(t, jnp.float32) for t in acc] if last else [],
             compiler_params=pltpu.CompilerParams(vmem_limit_bytes=32 * MIB),
             cost_estimate=pl.CostEstimate(
-                flops=4 * nrows * total * width,
-                bytes_accessed=2 * total * width,
-                transcendentals=nrows * total,
+                flops=4 * nrows * total * width if last else 0,
+                bytes_accessed=2 * total * width if last else 0,
+                transcendentals=nrows * total if last else 0,
             ),
             name="weigh",
         )(*ins)
@@ -328,14 +333,15 @@
     across(2, 1, *side[1, 1])
     across(3, 0, *side[2, 0])
     across(3, 1, *side[2, 1])
-    swap((0, 0), (0, 1))
-    swap((1, 0), (1, 1))
+    pieces(0)
+    pieces(1)
     swap((2, 0), (2, 1))
     swap((3, 0))
     parts = [[(1, 0), (1, 1)], [(2, 0), (2, 1)], [(3, 0), (3, 1), (0, 1), (0, 0)]]
     stages = list(range(nstage))
-    swap((3, 1))
-    early, sums = [], ()
+    early = [0, 1]
+    sums = weigh(parts[0], early, last=False, deps=side[3, 0])
+    swap((3, 1), deps=sums[1:])
     result = [None] * nb
     order, dups, deps = [], (), ()
     for part in parts:
@@ -354,24 +360,24 @@
     same = [
         [((h * ng + lo) * ng) + z for h in range(hi_n) for z in range(ng)] for lo in range(ng)
     ]
-    dups = lax.all_to_all(*dups, AXES, 0, 0, tiled=True, axis_index_groups=same)
 
     def unpack(which, also, last):
         near = jax.ShapeDtypeStruct((n, width), jnp.float32)
         scratch = [pltpu.VMEM((n, width), jnp.float32), pltpu.SemaphoreType.DMA((4,))]
         return pl.pallas_call(
             functools.partial(unpack_kernel, slots, which, last, hi_n, ng),
-            out_shape=[near] if last else [jax.ShapeDtypeStruct((1, n), jnp.float32), near],
-            in_specs=[vmem] * (2 + len(which)),
-            out_specs=[hbm] if last else [vmem, vmem],
+            out_shape=[near, jax.ShapeDtypeStruct((1, n), jnp.float32)] if last else [near],
+            in_specs=[vmem] * (1 + len(which) + len(also)),
+            out_specs=[hbm, vmem] if last else [vmem],
             scratch_shapes=scratch if last else [],
-            compiler_params=pltpu.CompilerParams(vmem_limit_bytes=16 * MIB),
+            compiler_params=small,
             name="unpack",
-        )(pos, *[back[k] for k in which], also)
+        )(pos, *[back[k] for k in which], *also)
 
     late = [k for u in parts[2][:3] for k in blocks_of(u)]
-    dup, near = unpack([b for b in range(nb) if b not in late], dups, False)
-    (near,) = unpack(late, near, True)
+    (near,) = unpack([b for b in range(nb) if b not in late], (), False)
+    dups = lax.all_to_all(after(*dups, near), AXES, 0, 0, tiled=True, axis_index_groups=same)
+    near, dup = unpack(late, (near, dups), True)
     return dup.reshape(n), near
 
 

time: 127 us -> 123 us (0.969)
  waiting for transfers between devices: 35.6 us -> 51.5 us
  blocking collectives: 15.2 us -> 0 us
  starting transfers between devices: 46.1 us -> 39.6 us
  Pallas kernels: 26.5 us -> 27.9 us
    ppermute x7, waiting for transfers between devices: 0.02 us -> 17.9 us  [local(): back[b] = lax.ppermute(result[b], AXES, to_owner(*hops[b], -1))]
    all_to_all x1 -> x0, blocking collectives: 15.2 us -> none  [local(): dups = lax.all_to_all(*dups, AXES, 0, 0, tiled=True, axis_index_groups=same)]
    ppermute x7, starting transfers between devices: 19.6 us -> 7.41 us  [local(): back[b] = lax.ppermute(result[b], AXES, to_owner(*hops[b], -1))]
    all_to_all x0 -> x1, starting transfers between devices: none -> 5.28 us  [local(): lax.all_to_all(after(*dups, near), AXES, 0, 0, tiled=True, axis_index_gro...]
    ppermute x8, waiting for transfers between devices: 21 us -> 16.5 us  [across(): lax.ppermute(after(src, *deps) if deps else src, AXES, beside(2))]
    ppermute x7, starting transfers between devices: 15.6 us -> 13.4 us  [send(): lax.ppermute(after(src, *deps) if deps else src, AXES, to_owner(*hops[k],...]
    ppermute x0 -> x8, starting transfers between devices: none -> 2.11 us  [pieces(): lax.ppermute(a, AXES, beside(1))]
    ppermute x0 -> x8, waiting for transfers between devices: none -> 1.34 us  [pieces(): lax.ppermute(a, AXES, beside(1))]
  transfers between devices with their start and end apart: 27 -> 34, of which waited for: 12 -> 18; matrix products, arithmetic and copies ran while one was open for 0% -> 0% of each run, Pallas kernels for 14% -> 18%
where the time goes in v4:
time: 123 us; the launch traced here: 122 us
  waiting for transfers between devices  51.5 us (42%)
  starting transfers between devices  39.6 us (32%)
  Pallas kernels  27.9 us (23%)
  local copies, waits for them, and re-layouts  2.27 us (2%)
    pallas_call x4, Pallas kernels, weigh(): pl.pallas_call(functools.partial(weigh_kernel, layout, row_stage, unit, s...  22.9 us
    ppermute x7, waiting for transfers between devices, local(): back[b] = lax.ppermute(result[b], AXES, to_owner(*hops[b], -1))  17.9 us
    ppermute x8, waiting for transfers between devices, across(): lax.ppermute(after(src, *deps) if deps else src, AXES, beside(2))  16.5 us
    ppermute x7, waiting for transfers between devices, send(): lax.ppermute(after(src, *deps) if deps else src, AXES, to_owner(*hops[k],...  13.8 us
    ppermute x7, starting transfers between devices, send(): lax.ppermute(after(src, *deps) if deps else src, AXES, to_owner(*hops[k],...  13.4 us
    ppermute x8, starting transfers between devices, across(): lax.ppermute(after(src, *deps) if deps else src, AXES, beside(2))  11.2 us
    ppermute x7, starting transfers between devices, local(): back[b] = lax.ppermute(result[b], AXES, to_owner(*hops[b], -1))  7.41 us
    all_to_all x1, starting transfers between devices, local(): lax.all_to_all(after(*dups, near), AXES, 0, 0, tiled=True, axis_index_gro...  5.28 us
  transfers between devices with their start and end apart: 34, of which 18 were waited for; matrix products, arithmetic and copies ran while one was open for 0% of the time, Pallas kernels for 18%

profile of v4, /device:TPU:0, one launch (start us, length us, event | category | flops | bytes accessed | tf_op | source)
XLA Modules:
  0.0 122.4 jit_solution(7024582010449503374)
XLA Ops:
  0.6 1.6 %copy-done = f32[512,1024]{1,0:T(8,128)S(1)} copy-done((f32[512,1024]{1,0:T(8,128)S(1)}, f32[512,1024]{1,0:T(8,128)}, u32[]{:S(2)}) %copy-start) | copy-done | bytes 2097176
  2.2 0.7 copy-done.1
  2.9 0.7 pack.1
  3.6 3.1 %collective-permute-start.3 = (bf16[128,1024]{1,0:T(8,128)(2,1)S(1)}, bf16[128,1024]{1,0:T(8,128)(2,1)S(1)}, u32[]{:S(2)}, u32[]{:S(2)}) collective-permute-start(bf16[128,1024]{1,0:T(8,128)(2,1)S(1)} %get-tuple-element.49), channel_id=1, source_target_pairs={{0,1},{1,2},{2,3},{3,0},{4,5},{5,6},{6,7},{7,4},{8,9},{9,10},{10,1... | collective-permute-start | bytes 786440 | tf_op jit(solution)/shard_map/ppermute | solution.py:244
  6.7 2.5 %collective-permute-start = (bf16[128,1024]{1,0:T(8,128)(2,1)S(1)}, bf16[128,1024]{1,0:T(8,128)(2,1)S(1)}, u32[]{:S(2)}, u32[]{:S(2)}) collective-permute-start(bf16[128,1024]{1,0:T(8,128)(2,1)S(1)} %get-tuple-element.46), channel_id=1, source_target_pairs={{0,17},{1,18},{2,19},{3,16},{4,21},{5,22},{6,23},{7,20},{8,25},{9,... | collective-permute-start | bytes 786440 | tf_op jit(solution)/shard_map/ppermute | solution.py:244
  9.2 1.0 pack_rest.1
  10.3 0.6 collective-permute-start.6
  10.8 5.0 %collective-permute-done.3.refs_0_.refs_6_.refs_8_ = bf16[128,1024]{1,0:T(8,128)(2,1)S(1)} collective-permute-done((bf16[128,1024]{1,0:T(8,128)(2,1)S(1)}, bf16[128,1024]{1,0:T(8,128)(2,1)S(1)}, u32[]{:S(2)}, u32[]{:S(2)}) %collective-permute-start.3) | collective-permute-done | bytes 262176 | tf_op jit(solution)/shard_map/ppermute | solution.py:244
  15.8 1.7 %collective-permute-start.9 = (bf16[128,1024]{1,0:T(8,128)(2,1)S(1)}, bf16[128,1024]{1,0:T(8,128)(2,1)S(1)}, u32[]{:S(2)}, u32[]{:S(2)}) collective-permute-start(bf16[128,1024]{1,0:T(8,128)(2,1)S(1)} %get-tuple-element.55.refs_2_.refs_3_.refs_4_), channel_id=1, source_target_pairs={{0,8},{1,9},{2,10},{3,11},{4,12},{5,13},{6,14},{7,15},{8,0},{9,1},... | collective-permute-start | bytes 786440 | tf_op jit(solution)/shard_map/ppermute | solution.py:254
  17.6 1.8 %collective-permute-start.2 = (bf16[128,1024]{1,0:T(8,128)(2,1)S(1)}, bf16[128,1024]{1,0:T(8,128)(2,1)S(1)}, u32[]{:S(2)}, u32[]{:S(2)}) collective-permute-start(bf16[128,1024]{1,0:T(8,128)(2,1)S(1)} %get-tuple-element.48), channel_id=1, source_target_pairs={{0,3},{1,0},{2,1},{3,2},{4,7},{5,4},{6,5},{7,6},{8,11},{9,8},{10,9... | collective-permute-start | bytes 786440 | tf_op jit(solution)/shard_map/ppermute | solution.py:244
  19.4 0.5 collective-permute-start.5
  19.9 3.5 %collective-permute-done.6.refs_3_.refs_2_.refs_5_ = bf16[128,1024]{1,0:T(8,128)(2,1)S(1)} collective-permute-done((bf16[128,1024]{1,0:T(8,128)(2,1)S(1)}, bf16[128,1024]{1,0:T(8,128)(2,1)S(1)}, u32[]{:S(2)}, u32[]{:S(2)}) %collective-permute-start.6) | collective-permute-done | bytes 262176 | tf_op jit(solution)/shard_map/ppermute | solution.py:244
  23.4 1.5 %collective-permute-start.7 = (bf16[128,1024]{1,0:T(8,128)(2,1)S(1)}, bf16[128,1024]{1,0:T(8,128)(2,1)S(1)}, u32[]{:S(2)}, u32[]{:S(2)}) collective-permute-start(bf16[128,1024]{1,0:T(8,128)(2,1)S(1)} %collective-permute-done.6.refs_3_.refs_2_.refs_5_), channel_id=1, source_target_pairs={{0,8},{1,9},{2,10},{3,11},{4,12},{5,13},{6,14},{7,15},{8,0},{9,1},... | collective-permute-start | bytes 786440 | tf_op jit(solution)/shard_map/ppermute | solution.py:254
  24.9 4.0 %collective-permute-start.4 = (bf16[128,1024]{1,0:T(8,128)(2,1)S(1)}, bf16[128,1024]{1,0:T(8,128)(2,1)S(1)}, u32[]{:S(2)}, u32[]{:S(2)}) collective-permute-start(bf16[128,1024]{1,0:T(8,128)(2,1)S(1)} %get-tuple-element.51), channel_id=1, source_target_pairs={{0,19},{1,16},{2,17},{3,18},{4,23},{5,20},{6,21},{7,22},{8,27},{9,... | collective-permute-start | bytes 786440 | tf_op jit(solution)/shard_map/ppermute | solution.py:244
  28.9 1.5 %collective-permute-start.10 = (bf16[128,1024]{1,0:T(8,128)(2,1)S(1)}, bf16[128,1024]{1,0:T(8,128)(2,1)S(1)}, u32[]{:S(2)}, u32[]{:S(2)}) collective-permute-start(bf16[128,1024]{1,0:T(8,128)(2,1)S(1)} %collective-permute-done.refs_1_.refs_7_.refs_9_), channel_id=1, source_target_pairs={{0,8},{1,9},{2,10},{3,11},{4,12},{5,13},{6,14},{7,15},{8,0},{9,1},... | collective-permute-start | bytes 786440 | tf_op jit(solution)/shard_map/ppermute | solution.py:254
  30.4 0.0 collective-permute-done.2.refs_2_.refs_0_.refs_10_.refs_12_
  30.4 0.0 collective-permute-start.1
  30.4 0.3 collective-permute-done.5.refs_8_.refs_10_
  30.7 5.6 %collective-permute-done.7.refs_5_.refs_7_ = bf16[128,1024]{1,0:T(8,128)(2,1)S(1)} collective-permute-done((bf16[128,1024]{1,0:T(8,128)(2,1)S(1)}, bf16[128,1024]{1,0:T(8,128)(2,1)S(1)}, u32[]{:S(2)}, u32[]{:S(2)}) %collective-permute-start.7) | collective-permute-done | bytes 262176 | tf_op jit(solution)/shard_map/ppermute | solution.py:254
  36.3 1.7 %collective-permute-start.8 = (bf16[128,1024]{1,0:T(8,128)(2,1)S(1)}, bf16[128,1024]{1,0:T(8,128)(2,1)S(1)}, u32[]{:S(2)}, u32[]{:S(2)}) collective-permute-start(bf16[128,1024]{1,0:T(8,128)(2,1)S(1)} %collective-permute-done.2.refs_2_.refs_0_.refs_10_.refs_12_), channel_id=1, source_target_pairs={{0,8},{1,9},{2,10},{3,11},{4,12},{5,13},{6,14},{7,15},{8,0},{9,1},... | collective-permute-start | bytes 786440 | tf_op jit(solution)/shard_map/ppermute | solution.py:254
  38.1 0.0 collective-permute-start.17
  38.1 0.0 collective-permute-done.4.refs_3_.refs_1_.refs_11_.refs_13_
  38.1 0.5 collective-permute-start.22
  38.6 3.4 %collective-permute-done.10.refs_9_.refs_11_ = bf16[128,1024]{1,0:T(8,128)(2,1)S(1)} collective-permute-done((bf16[128,1024]{1,0:T(8,128)(2,1)S(1)}, bf16[128,1024]{1,0:T(8,128)(2,1)S(1)}, u32[]{:S(2)}, u32[]{:S(2)}) %collective-permute-start.10) | collective-permute-done | bytes 262176 | tf_op jit(solution)/shard_map/ppermute | solution.py:254
  41.9 1.7 %collective-permute-start.11 = (bf16[128,1024]{1,0:T(8,128)(2,1)S(1)}, bf16[128,1024]{1,0:T(8,128)(2,1)S(1)}, u32[]{:S(2)}, u32[]{:S(2)}) collective-permute-start(bf16[128,1024]{1,0:T(8,128)(2,1)S(1)} %collective-permute-done.4.refs_3_.refs_1_.refs_11_.refs_13_), channel_id=1, source_target_pairs={{0,8},{1,9},{2,10},{3,11},{4,12},{5,13},{6,14},{7,15},{8,0},{9,1},... | collective-permute-start | bytes 786440 | tf_op jit(solution)/shard_map/ppermute | solution.py:254
  43.7 0.2 collective-permute-done.1.refs_6_.refs_14_.refs_0_.refs_16_
  43.9 1.4 %collective-permute-start.12 = (bf16[128,1024]{1,0:T(8,128)(2,1)S(1)}, bf16[128,1024]{1,0:T(8,128)(2,1)S(1)}, u32[]{:S(2)}, u32[]{:S(2)}) collective-permute-start(bf16[128,1024]{1,0:T(8,128)(2,1)S(1)} %get-tuple-element.59), channel_id=1, source_target_pairs={{0,18},{1,19},{2,16},{3,17},{4,22},{5,23},{6,20},{7,21},{8,26},{9,... | collective-permute-start | bytes 786440 | tf_op jit(solution)/shard_map/ppermute | solution.py:244
  45.2 2.3 %collective-permute-done.8.refs_4_.refs_12_.refs_14_ = bf16[128,1024]{1,0:T(8,128)(2,1)S(1)} collective-permute-done((bf16[128,1024]{1,0:T(8,128)(2,1)S(1)}, bf16[128,1024]{1,0:T(8,128)(2,1)S(1)}, u32[]{:S(2)}, u32[]{:S(2)}) %collective-permute-start.8) | collective-permute-done | bytes 262176 | tf_op jit(solution)/shard_map/ppermute | solution.py:254
  47.6 0.5 collective-permute-start.18
  48.1 0.1 collective-permute-start.23
  48.1 2.5 %collective-permute-done.11.refs_5_.refs_13_.refs_15_ = bf16[128,1024]{1,0:T(8,128)(2,1)S(1)} collective-permute-done((bf16[128,1024]{1,0:T(8,128)(2,1)S(1)}, bf16[128,1024]{1,0:T(8,128)(2,1)S(1)}, u32[]{:S(2)}, u32[]{:S(2)}) %collective-permute-start.11) | collective-permute-done | bytes 262176 | tf_op jit(solution)/shard_map/ppermute | solution.py:254
  50.6 1.2 %collective-permute-start.13 = (bf16[128,1024]{1,0:T(8,128)(2,1)S(1)}, bf16[128,1024]{1,0:T(8,128)(2,1)S(1)}, u32[]{:S(2)}, u32[]{:S(2)}) collective-permute-start(bf16[128,1024]{1,0:T(8,128)(2,1)S(1)} %collective-permute-done.1.refs_6_.refs_14_.refs_0_.refs_16_), channel_id=1, source_target_pairs={{0,8},{1,9},{2,10},{3,11},{4,12},{5,13},{6,14},{7,15},{8,0},{9,1},... | collective-permute-start | bytes 786440 | tf_op jit(solution)/shard_map/ppermute | solution.py:254
  51.8 0.1 pad_maximum_fusion
  51.9 5.1 %collective-permute-done.12.refs_7_.refs_15_.refs_1_.refs_17_ = bf16[128,1024]{1,0:T(8,128)(2,1)S(1)} collective-permute-done((bf16[128,1024]{1,0:T(8,128)(2,1)S(1)}, bf16[128,1024]{1,0:T(8,128)(2,1)S(1)}, u32[]{:S(2)}, u32[]{:S(2)}) %collective-permute-start.12) | collective-permute-done | bytes 262176 | tf_op jit(solution)/shard_map/ppermute | solution.py:244
  57.0 0.0 collective-permute-start.15
  57.0 0.5 collective-permute-start.19
  57.6 0.1 collective-permute-start.20
  57.6 0.0 collective-permute-done.23.refs_16_.refs_24_.refs_26_
  57.6 0.4 collective-permute-start.24
  58.1 1.2 %collective-permute-start.14 = (bf16[128,1024]{1,0:T(8,128)(2,1)S(1)}, bf16[128,1024]{1,0:T(8,128)(2,1)S(1)}, u32[]{:S(2)}, u32[]{:S(2)}) collective-permute-start(bf16[128,1024]{1,0:T(8,128)(2,1)S(1)} %collective-permute-done.12.refs_7_.refs_15_.refs_1_.refs_17_), channel_id=1, source_target_pairs={{0,8},{1,9},{2,10},{3,11},{4,12},{5,13},{6,14},{7,15},{8,0},{9,1},... | collective-permute-start | bytes 786440 | tf_op jit(solution)/shard_map/ppermute | solution.py:254
  59.4 0.7 collective-permute-done.19.refs_12_.refs_20_.refs_22_
  60.1 0.1 collective-permute-start.16
  60.2 0.2 collective-permute-done.20.refs_13_.refs_21_.refs_23_
  60.4 0.4 collective-permute-done.24.refs_17_.refs_25_.refs_27_
  60.8 3.0 %weigh.4 = (f32[256,1024]{1,0:T(8,128)S(1)}, f32[256,128]{1,0:T(8,128)S(1)}) custom-call(bf16[128,1024]{1,0:T(8,128)(2,1)S(1)} %collective-permute-done.3.refs_0_.refs_6_.refs_8_, bf16[128,1024]{1,0:T(8,128)(2,1)S(1)} %collective-permute-done.refs_1_.refs_7_.refs_9_, bf16[128,1024]{1,0:T(8,128)(2,1)S(1)} %get-tuple-element.55.refs_2_.refs_3_.refs_4_, ...), custom_call_target="tpu_custom_call" | custom-call | tf_op jit(solution)/shard_map/weigh/pallas_call | solution.py:294
  63.9 2.5 %collective-permute-done.14.refs_9_.refs_17_.refs_19_ = bf16[128,1024]{1,0:T(8,128)(2,1)S(1)} collective-permute-done((bf16[128,1024]{1,0:T(8,128)(2,1)S(1)}, bf16[128,1024]{1,0:T(8,128)(2,1)S(1)}, u32[]{:S(2)}, u32[]{:S(2)}) %collective-permute-start.14) | collective-permute-done | bytes 262176 | tf_op jit(solution)/shard_map/ppermute | solution.py:254
  66.4 0.1 collective-permute-start.25
  66.5 1.9 %collective-permute-done.25.refs_12_.refs_28_.refs_30_ = bf16[256,1024]{1,0:T(8,128)(2,1)S(1)} collective-permute-done((bf16[256,1024]{1,0:T(8,128)(2,1)S(1)}, bf16[256,1024]{1,0:T(8,128)(2,1)S(1)}, u32[]{:S(2)}, u32[]{:S(2)}) %collective-permute-start.25) | collective-permute-done | bytes 524320 | tf_op jit(solution)/shard_map/ppermute | solution.py:260
  68.4 3.1 %weigh.5 = (bf16[128,1024]{1,0:T(8,128)(2,1)S(1)}, bf16[128,1024]{1,0:T(8,128)(2,1)S(1)}, f32[8,128]{1,0:T(8,128)S(1)}) custom-call(bf16[128,1024]{1,0:T(8,128)(2,1)S(1)} %collective-permute-done.3.refs_0_.refs_6_.refs_8_, bf16[128,1024]{1,0:T(8,128)(2,1)S(1)} %collective-permute-done.refs_1_.refs_7_.refs_9_, ...), custom_call_target="tpu_custom_call" | custom-call | flops 2147483648 | bytes 4194304 | tf_op jit(solution)/shard_map/weigh/pallas_call | solution.py:294
  71.4 1.4 %collective-permute-start.29 = (bf16[128,1024]{1,0:T(8,128)(2,1)S(1)}, bf16[128,1024]{1,0:T(8,128)(2,1)S(1)}, u32[]{:S(2)}, u32[]{:S(2)}) collective-permute-start(bf16[128,1024]{1,0:T(8,128)(2,1)S(1)} %get-tuple-element.66), channel_id=1, source_target_pairs={{0,3},{1,0},{2,1},{3,2},{4,7},{5,4},{6,5},{7,6},{8,11},{9,8},{10,9... | collective-permute-start | bytes 786440 | tf_op jit(solution)/shard_map/ppermute | solution.py:358
  72.9 1.2 collective-permute-start.30
  74.1 5.8 %weigh.6 = (bf16[128,1024]{1,0:T(8,128)(2,1)S(1)}, bf16[128,1024]{1,0:T(8,128)(2,1)S(1)}, f32[8,128]{1,0:T(8,128)S(1)}) custom-call(bf16[128,1024]{1,0:T(8,128)(2,1)S(1)} %collective-permute-done.2.refs_2_.refs_0_.refs_10_.refs_12_, bf16[128,1024]{1,0:T(8,128)(2,1)S(1)} %collective-permute-done.4.refs_3_.refs_1_.refs_11_.refs_13_, ...), custom_call_target="tpu_custom_call" | custom-call | flops 4294967296 | bytes 8388608 | tf_op jit(solution)/shard_map/weigh/pallas_call | solution.py:294
  79.9 1.8 %collective-permute-start.31 = (bf16[128,1024]{1,0:T(8,128)(2,1)S(1)}, bf16[128,1024]{1,0:T(8,128)(2,1)S(1)}, u32[]{:S(2)}, u32[]{:S(2)}) collective-permute-start(bf16[128,1024]{1,0:T(8,128)(2,1)S(1)} %get-tuple-element.69), channel_id=1, source_target_pairs={{0,1},{1,2},{2,3},{3,0},{4,5},{5,6},{6,7},{7,4},{8,9},{9,10},{10,1... | collective-permute-start | bytes 786440 | tf_op jit(solution)/shard_map/ppermute | solution.py:358
  81.8 0.6 collective-permute-start.32
  82.4 11.0 %weigh.7 = (bf16[128,1024]{1,0:T(8,128)(2,1)}, bf16[128,1024]{1,0:T(8,128)(2,1)S(1)}, bf16[128,1024]{1,0:T(8,128)(2,1)S(1)}, bf16[128,1024]{1,0:T(8,128)(2,1)S(1)}, f32[8,128]{1,0:T(8,128)}) custom-call(bf16[128,1024]{1,0:T(8,128)(2,1)S(1)} %collective-permute-done.1.refs_6_.refs_14_.refs_0_.refs_16_, ...), custom_call_target="tpu_custom_call" | custom-call | flops 8589934592 | bytes 8388608 | tf_op jit(solution)/shard_map/weigh/pallas_call | solution.py:294
  93.4 1.9 %collective-permute-start.26 = (bf16[128,1024]{1,0:T(8,128)(2,1)}, bf16[128,1024]{1,0:T(8,128)(2,1)S(1)}, u32[]{:S(2)}, u32[]{:S(2)}) collective-permute-start(bf16[128,1024]{1,0:T(8,128)(2,1)} %get-tuple-element.72), channel_id=1, source_target_pairs={{0,2},{1,3},{2,0},{3,1},{4,6},{5,7},{6,4},{7,5},{8,10},{9,11},{10,... | collective-permute-start | bytes 786440 | tf_op jit(solution)/shard_map/ppermute | solution.py:358
  95.3 2.7 %collective-permute-done.30.refs_2_ = bf16[128,1024]{1,0:T(8,128)(2,1)S(1)} collective-permute-done((bf16[128,1024]{1,0:T(8,128)(2,1)S(1)}, bf16[128,1024]{1,0:T(8,128)(2,1)S(1)}, u32[]{:S(2)}, u32[]{:S(2)}) %collective-permute-start.30) | collective-permute-done | bytes 262176 | tf_op jit(solution)/shard_map/ppermute | solution.py:358
  98.0 0.4 collective-permute-start.28
  98.4 1.0 unpack.2.refs_3_
  99.4 5.3 %all-to-all-start = ((f32[8,1,128]{2,1,0:T(1,128)}), f32[8,1,128]{2,1,0:T(1,128)S(1)}, u32[]{:S(2)}, u32[]{:S(2)}) async-start(f32[8,1,128]{2,1,0:T(1,128)} %bitcast.2), calls=%async_computation | async-start | bytes 8192 | tf_op jit(solution)/shard_map/all_to_all | solution.py:379
  104.7 8.8 %collective-permute-done.26.refs_0_ = bf16[128,1024]{1,0:T(8,128)(2,1)S(1)} collective-permute-done((bf16[128,1024]{1,0:T(8,128)(2,1)}, bf16[128,1024]{1,0:T(8,128)(2,1)S(1)}, u32[]{:S(2)}, u32[]{:S(2)}) %collective-permute-start.26) | collective-permute-done | bytes 262176 | tf_op jit(solution)/shard_map/ppermute | solution.py:358
  113.5 6.4 %collective-permute-done.27.refs_1_ = bf16[128,1024]{1,0:T(8,128)(2,1)S(1)} collective-permute-done((bf16[128,1024]{1,0:T(8,128)(2,1)S(1)}, bf16[128,1024]{1,0:T(8,128)(2,1)S(1)}, u32[]{:S(2)}, u32[]{:S(2)}) %collective-permute-start.27) | collective-permute-done | bytes 262176 | tf_op jit(solution)/shard_map/ppermute | solution.py:358
  119.9 0.1 all-to-all-done
  120.0 2.3 %unpack.3 = (f32[512,1024]{1,0:T(8,128)}, f32[1,512]{1,0:T(1,128)}) custom-call(s32[1,512]{1,0:T(1,128)S(1)} %get-tuple-element.42.pos_ref, bf16[128,1024]{1,0:T(8,128)(2,1)S(1)} %collective-permute-done.26.refs_0_, bf16[128,1024]{1,0:T(8,128)(2,1)S(1)} %collective-permute-done.27.refs_1_, bf16[128,1024]{1,0:T(8,128)(2,1)S(1)} %collective-permute-done.28.refs_2_, ...), custom_call_target="tpu_custom_call" | custom-call | tf_op jit(solution)/shard_map/unpack/pallas_call | solution.py:367
  (19 shorter events, 0.1 us)
Async XLA Ops:
  0.6 1.6 %copy-start = (f32[512,1024]{1,0:T(8,128)S(1)}, f32[512,1024]{1,0:T(8,128)}, u32[]{:S(2)}) copy-start(f32[512,1024]{1,0:T(8,128)} %emb_ref.1) | copy-start | bytes 6291460
  2.2 0.7 copy-start.1
  3.6 12.2 %collective-permute-start.3 = (bf16[128,1024]{1,0:T(8,128)(2,1)S(1)}, bf16[128,1024]{1,0:T(8,128)(2,1)S(1)}, u32[]{:S(2)}, u32[]{:S(2)}) collective-permute-start(bf16[128,1024]{1,0:T(8,128)(2,1)S(1)} %get-tuple-element.49), channel_id=1, source_target_pairs={{0,1},{1,2},{2,3},{3,0},{4,5},{5,6},{6,7},{7,4},{8,9},{9,10},{10,1... | collective-permute-start | bytes 786440 | tf_op jit(solution)/shard_map/ppermute | solution.py:244
  6.7 18.2 %collective-permute-start = (bf16[128,1024]{1,0:T(8,128)(2,1)S(1)}, bf16[128,1024]{1,0:T(8,128)(2,1)S(1)}, u32[]{:S(2)}, u32[]{:S(2)}) collective-permute-start(bf16[128,1024]{1,0:T(8,128)(2,1)S(1)} %get-tuple-element.46), channel_id=1, source_target_pairs={{0,17},{1,18},{2,19},{3,16},{4,21},{5,22},{6,23},{7,20},{8,25},{9,... | collective-permute-start | bytes 786440 | tf_op jit(solution)/shard_map/ppermute | solution.py:244
  10.3 13.2 %collective-permute-start.6 = (bf16[128,1024]{1,0:T(8,128)(2,1)S(1)}, bf16[128,1024]{1,0:T(8,128)(2,1)S(1)}, u32[]{:S(2)}, u32[]{:S(2)}) collective-permute-start(bf16[128,1024]{1,0:T(8,128)(2,1)S(1)} %get-tuple-element.52), channel_id=1, source_target_pairs={{0,16},{1,17},{2,18},{3,19},{4,20},{5,21},{6,22},{7,23},{8,24},{9,... | collective-permute-start | bytes 786440 | tf_op jit(solution)/shard_map/ppermute | solution.py:244
  15.8 13.1 %collective-permute-start.9 = (bf16[128,1024]{1,0:T(8,128)(2,1)S(1)}, bf16[128,1024]{1,0:T(8,128)(2,1)S(1)}, u32[]{:S(2)}, u32[]{:S(2)}) collective-permute-start(bf16[128,1024]{1,0:T(8,128)(2,1)S(1)} %get-tuple-element.55.refs_2_.refs_3_.refs_4_), channel_id=1, source_target_pairs={{0,8},{1,9},{2,10},{3,11},{4,12},{5,13},{6,14},{7,15},{8,0},{9,1},... | collective-permute-start | bytes 786440 | tf_op jit(solution)/shard_map/ppermute | solution.py:254
  17.6 12.9 %collective-permute-start.2 = (bf16[128,1024]{1,0:T(8,128)(2,1)S(1)}, bf16[128,1024]{1,0:T(8,128)(2,1)S(1)}, u32[]{:S(2)}, u32[]{:S(2)}) collective-permute-start(bf16[128,1024]{1,0:T(8,128)(2,1)S(1)} %get-tuple-element.48), channel_id=1, source_target_pairs={{0,3},{1,0},{2,1},{3,2},{4,7},{5,4},{6,5},{7,6},{8,11},{9,8},{10,9... | collective-permute-start | bytes 786440 | tf_op jit(solution)/shard_map/ppermute | solution.py:244
  19.4 11.3 %collective-permute-start.5 = (bf16[128,1024]{1,0:T(8,128)(2,1)S(1)}, bf16[128,1024]{1,0:T(8,128)(2,1)S(1)}, u32[]{:S(2)}, u32[]{:S(2)}) collective-permute-start(bf16[128,1024]{1,0:T(8,128)(2,1)S(1)} %collective-permute-done.3.refs_0_.refs_6_.refs_8_), channel_id=1, source_target_pairs={{0,8},{1,9},{2,10},{3,11},{4,12},{5,13},{6,14},{7,15},{8,0},{9,1},... | collective-permute-start | bytes 786440 | tf_op jit(solution)/shard_map/ppermute | solution.py:254
  23.4 12.9 %collective-permute-start.7 = (bf16[128,1024]{1,0:T(8,128)(2,1)S(1)}, bf16[128,1024]{1,0:T(8,128)(2,1)S(1)}, u32[]{:S(2)}, u32[]{:S(2)}) collective-permute-start(bf16[128,1024]{1,0:T(8,128)(2,1)S(1)} %collective-permute-done.6.refs_3_.refs_2_.refs_5_), channel_id=1, source_target_pairs={{0,8},{1,9},{2,10},{3,11},{4,12},{5,13},{6,14},{7,15},{8,0},{9,1},... | collective-permute-start | bytes 786440 | tf_op jit(solution)/shard_map/ppermute | solution.py:254
  24.9 13.1 %collective-permute-start.4 = (bf16[128,1024]{1,0:T(8,128)(2,1)S(1)}, bf16[128,1024]{1,0:T(8,128)(2,1)S(1)}, u32[]{:S(2)}, u32[]{:S(2)}) collective-permute-start(bf16[128,1024]{1,0:T(8,128)(2,1)S(1)} %get-tuple-element.51), channel_id=1, source_target_pairs={{0,19},{1,16},{2,17},{3,18},{4,23},{5,20},{6,21},{7,22},{8,27},{9,... | collective-permute-start | bytes 786440 | tf_op jit(solution)/shard_map/ppermute | solution.py:244
  28.9 13.0 %collective-permute-start.10 = (bf16[128,1024]{1,0:T(8,128)(2,1)S(1)}, bf16[128,1024]{1,0:T(8,128)(2,1)S(1)}, u32[]{:S(2)}, u32[]{:S(2)}) collective-permute-start(bf16[128,1024]{1,0:T(8,128)(2,1)S(1)} %collective-permute-done.refs_1_.refs_7_.refs_9_), channel_id=1, source_target_pairs={{0,8},{1,9},{2,10},{3,11},{4,12},{5,13},{6,14},{7,15},{8,0},{9,1},... | collective-permute-start | bytes 786440 | tf_op jit(solution)/shard_map/ppermute | solution.py:254
  30.4 13.4 %collective-permute-start.1 = (bf16[128,1024]{1,0:T(8,128)(2,1)S(1)}, bf16[128,1024]{1,0:T(8,128)(2,1)S(1)}, u32[]{:S(2)}, u32[]{:S(2)}) collective-permute-start(bf16[128,1024]{1,0:T(8,128)(2,1)S(1)} %get-tuple-element.47), channel_id=1, source_target_pairs={{0,2},{1,3},{2,0},{3,1},{4,6},{5,7},{6,4},{7,5},{8,10},{9,11},{10,... | collective-permute-start | bytes 786440 | tf_op jit(solution)/shard_map/ppermute | solution.py:244
  36.3 11.2 %collective-permute-start.8 = (bf16[128,1024]{1,0:T(8,128)(2,1)S(1)}, bf16[128,1024]{1,0:T(8,128)(2,1)S(1)}, u32[]{:S(2)}, u32[]{:S(2)}) collective-permute-start(bf16[128,1024]{1,0:T(8,128)(2,1)S(1)} %collective-permute-done.2.refs_2_.refs_0_.refs_10_.refs_12_), channel_id=1, source_target_pairs={{0,8},{1,9},{2,10},{3,11},{4,12},{5,13},{6,14},{7,15},{8,0},{9,1},... | collective-permute-start | bytes 786440 | tf_op jit(solution)/shard_map/ppermute | solution.py:254
  38.1 9.5 %collective-permute-start.17 = (bf16[128,1024]{1,0:T(8,128)(2,1)S(1)}, bf16[128,1024]{1,0:T(8,128)(2,1)S(1)}, u32[]{:S(2)}, u32[]{:S(2)}) collective-permute-start(bf16[128,1024]{1,0:T(8,128)(2,1)S(1)} %get-tuple-element.55.refs_2_.refs_3_.refs_4_), channel_id=1, source_target_pairs={{0,4},{1,5},{2,6},{3,7},{4,0},{5,1},{6,2},{7,3},{8,12},{9,13},{10,... | collective-permute-start | bytes 786440 | tf_op jit(solution)/shard_map/ppermute | solution.py:265
  38.1 10.0 %collective-permute-start.22 = (bf16[128,1024]{1,0:T(8,128)(2,1)S(1)}, bf16[128,1024]{1,0:T(8,128)(2,1)S(1)}, u32[]{:S(2)}, u32[]{:S(2)}) collective-permute-start(bf16[128,1024]{1,0:T(8,128)(2,1)S(1)} %collective-permute-done.refs_1_.refs_7_.refs_9_), channel_id=1, source_target_pairs={{0,4},{1,5},{2,6},{3,7},{4,0},{5,1},{6,2},{7,3},{8,12},{9,13},{10,... | collective-permute-start | bytes 786440 | tf_op jit(solution)/shard_map/ppermute | solution.py:265
  41.9 8.7 %collective-permute-start.11 = (bf16[128,1024]{1,0:T(8,128)(2,1)S(1)}, bf16[128,1024]{1,0:T(8,128)(2,1)S(1)}, u32[]{:S(2)}, u32[]{:S(2)}) collective-permute-start(bf16[128,1024]{1,0:T(8,128)(2,1)S(1)} %collective-permute-done.4.refs_3_.refs_1_.refs_11_.refs_13_), channel_id=1, source_target_pairs={{0,8},{1,9},{2,10},{3,11},{4,12},{5,13},{6,14},{7,15},{8,0},{9,1},... | collective-permute-start | bytes 786440 | tf_op jit(solution)/shard_map/ppermute | solution.py:254
  43.9 13.2 %collective-permute-start.12 = (bf16[128,1024]{1,0:T(8,128)(2,1)S(1)}, bf16[128,1024]{1,0:T(8,128)(2,1)S(1)}, u32[]{:S(2)}, u32[]{:S(2)}) collective-permute-start(bf16[128,1024]{1,0:T(8,128)(2,1)S(1)} %get-tuple-element.59), channel_id=1, source_target_pairs={{0,18},{1,19},{2,16},{3,17},{4,22},{5,23},{6,20},{7,21},{8,26},{9,... | collective-permute-start | bytes 786440 | tf_op jit(solution)/shard_map/ppermute | solution.py:244
  47.5 9.5 %collective-permute-start.21 = (bf16[128,1024]{1,0:T(8,128)(2,1)S(1)}, bf16[128,1024]{1,0:T(8,128)(2,1)S(1)}, u32[]{:S(2)}, u32[]{:S(2)}) collective-permute-start(bf16[128,1024]{1,0:T(8,128)(2,1)S(1)} %collective-permute-done.3.refs_0_.refs_6_.refs_8_), channel_id=1, source_target_pairs={{0,4},{1,5},{2,6},{3,7},{4,0},{5,1},{6,2},{7,3},{8,12},{9,13},{10,... | collective-permute-start | bytes 786440 | tf_op jit(solution)/shard_map/ppermute | solution.py:265
  47.6 10.0 %collective-permute-start.18 = (bf16[128,1024]{1,0:T(8,128)(2,1)S(1)}, bf16[128,1024]{1,0:T(8,128)(2,1)S(1)}, u32[]{:S(2)}, u32[]{:S(2)}) collective-permute-start(bf16[128,1024]{1,0:T(8,128)(2,1)S(1)} %collective-permute-done.6.refs_3_.refs_2_.refs_5_), channel_id=1, source_target_pairs={{0,4},{1,5},{2,6},{3,7},{4,0},{5,1},{6,2},{7,3},{8,12},{9,13},{10,... | collective-permute-start | bytes 786440 | tf_op jit(solution)/shard_map/ppermute | solution.py:265
  48.1 9.6 %collective-permute-start.23 = (bf16[128,1024]{1,0:T(8,128)(2,1)S(1)}, bf16[128,1024]{1,0:T(8,128)(2,1)S(1)}, u32[]{:S(2)}, u32[]{:S(2)}) collective-permute-start(bf16[128,1024]{1,0:T(8,128)(2,1)S(1)} %collective-permute-done.5.refs_8_.refs_10_), channel_id=1, source_target_pairs={{0,4},{1,5},{2,6},{3,7},{4,0},{5,1},{6,2},{7,3},{8,12},{9,13},{10,... | collective-permute-start | bytes 786440 | tf_op jit(solution)/shard_map/ppermute | solution.py:265
  50.6 7.5 %collective-permute-start.13 = (bf16[128,1024]{1,0:T(8,128)(2,1)S(1)}, bf16[128,1024]{1,0:T(8,128)(2,1)S(1)}, u32[]{:S(2)}, u32[]{:S(2)}) collective-permute-start(bf16[128,1024]{1,0:T(8,128)(2,1)S(1)} %collective-permute-done.1.refs_6_.refs_14_.refs_0_.refs_16_), channel_id=1, source_target_pairs={{0,8},{1,9},{2,10},{3,11},{4,12},{5,13},{6,14},{7,15},{8,0},{9,1},... | collective-permute-start | bytes 786440 | tf_op jit(solution)/shard_map/ppermute | solution.py:254
  57.0 11.3 %collective-permute-start.15 = (bf16[512,1024]{1,0:T(8,128)(2,1)S(1)}, bf16[512,1024]{1,0:T(8,128)(2,1)S(1)}, u32[]{:S(2)}, u32[]{:S(2)}) collective-permute-start(bf16[512,1024]{1,0:T(8,128)(2,1)S(1)} %pad_maximum_fusion), channel_id=1, source_target_pairs={{0,4},{1,5},{2,6},{3,7},{4,0},{5,1},{6,2},{7,3},{8,12},{9,13},{10,... | collective-permute-start | bytes 3145736 | tf_op jit(solution)/shard_map/ppermute | solution.py:260
  57.0 3.0 %collective-permute-start.19 = (bf16[128,1024]{1,0:T(8,128)(2,1)S(1)}, bf16[128,1024]{1,0:T(8,128)(2,1)S(1)}, u32[]{:S(2)}, u32[]{:S(2)}) collective-permute-start(bf16[128,1024]{1,0:T(8,128)(2,1)S(1)} %collective-permute-done.9.refs_4_.refs_6_), channel_id=1, source_target_pairs={{0,4},{1,5},{2,6},{3,7},{4,0},{5,1},{6,2},{7,3},{8,12},{9,13},{10,... | collective-permute-start | bytes 786440 | tf_op jit(solution)/shard_map/ppermute | solution.py:265
  57.6 2.9 %collective-permute-start.20 = (bf16[128,1024]{1,0:T(8,128)(2,1)S(1)}, bf16[128,1024]{1,0:T(8,128)(2,1)S(1)}, u32[]{:S(2)}, u32[]{:S(2)}) collective-permute-start(bf16[128,1024]{1,0:T(8,128)(2,1)S(1)} %collective-permute-done.7.refs_5_.refs_7_), channel_id=1, source_target_pairs={{0,4},{1,5},{2,6},{3,7},{4,0},{5,1},{6,2},{7,3},{8,12},{9,13},{10,... | collective-permute-start | bytes 786440 | tf_op jit(solution)/shard_map/ppermute | solution.py:265
  57.6 3.2 %collective-permute-start.24 = (bf16[128,1024]{1,0:T(8,128)(2,1)S(1)}, bf16[128,1024]{1,0:T(8,128)(2,1)S(1)}, u32[]{:S(2)}, u32[]{:S(2)}) collective-permute-start(bf16[128,1024]{1,0:T(8,128)(2,1)S(1)} %collective-permute-done.10.refs_9_.refs_11_), channel_id=1, source_target_pairs={{0,4},{1,5},{2,6},{3,7},{4,0},{5,1},{6,2},{7,3},{8,12},{9,13},{10,... | collective-permute-start | bytes 786440 | tf_op jit(solution)/shard_map/ppermute | solution.py:265
  58.1 8.3 %collective-permute-start.14 = (bf16[128,1024]{1,0:T(8,128)(2,1)S(1)}, bf16[128,1024]{1,0:T(8,128)(2,1)S(1)}, u32[]{:S(2)}, u32[]{:S(2)}) collective-permute-start(bf16[128,1024]{1,0:T(8,128)(2,1)S(1)} %collective-permute-done.12.refs_7_.refs_15_.refs_1_.refs_17_), channel_id=1, source_target_pairs={{0,8},{1,9},{2,10},{3,11},{4,12},{5,13},{6,14},{7,15},{8,0},{9,1},... | collective-permute-start | bytes 786440 | tf_op jit(solution)/shard_map/ppermute | solution.py:254
  60.1 6.4 %collective-permute-start.16 = (bf16[256,1024]{1,0:T(8,128)(2,1)S(1)}, bf16[256,1024]{1,0:T(8,128)(2,1)S(1)}, u32[]{:S(2)}, u32[]{:S(2)}) collective-permute-start(bf16[256,1024]{1,0:T(8,128)(2,1)S(1)} %pad_maximum_fusion.1), channel_id=1, source_target_pairs={{0,4},{1,5},{2,6},{3,7},{4,0},{5,1},{6,2},{7,3},{8,12},{9,13},{10,... | collective-permute-start | bytes 1572872 | tf_op jit(solution)/shard_map/ppermute | solution.py:260
  66.4 2.0 %collective-permute-start.25 = (bf16[256,1024]{1,0:T(8,128)(2,1)S(1)}, bf16[256,1024]{1,0:T(8,128)(2,1)S(1)}, u32[]{:S(2)}, u32[]{:S(2)}) collective-permute-start(bf16[256,1024]{1,0:T(8,128)(2,1)S(1)} %pad_maximum_fusion.2), channel_id=1, source_target_pairs={{0,4},{1,5},{2,6},{3,7},{4,0},{5,1},{6,2},{7,3},{8,12},{9,13},{10,... | collective-permute-start | bytes 1572872 | tf_op jit(solution)/shard_map/ppermute | solution.py:260
  71.4 26.6 %collective-permute-start.29 = (bf16[128,1024]{1,0:T(8,128)(2,1)S(1)}, bf16[128,1024]{1,0:T(8,128)(2,1)S(1)}, u32[]{:S(2)}, u32[]{:S(2)}) collective-permute-start(bf16[128,1024]{1,0:T(8,128)(2,1)S(1)} %get-tuple-element.66), channel_id=1, source_target_pairs={{0,3},{1,0},{2,1},{3,2},{4,7},{5,4},{6,5},{7,6},{8,11},{9,8},{10,9... | collective-permute-start | bytes 786440 | tf_op jit(solution)/shard_map/ppermute | solution.py:358
  72.9 25.1 %collective-permute-start.30 = (bf16[128,1024]{1,0:T(8,128)(2,1)S(1)}, bf16[128,1024]{1,0:T(8,128)(2,1)S(1)}, u32[]{:S(2)}, u32[]{:S(2)}) collective-permute-start(bf16[128,1024]{1,0:T(8,128)(2,1)S(1)} %get-tuple-element.76), channel_id=1, source_target_pairs={{0,19},{1,16},{2,17},{3,18},{4,23},{5,20},{6,21},{7,22},{8,27},{9,... | collective-permute-start | bytes 786440 | tf_op jit(solution)/shard_map/ppermute | solution.py:358
  79.9 18.5 %collective-permute-start.31 = (bf16[128,1024]{1,0:T(8,128)(2,1)S(1)}, bf16[128,1024]{1,0:T(8,128)(2,1)S(1)}, u32[]{:S(2)}, u32[]{:S(2)}) collective-permute-start(bf16[128,1024]{1,0:T(8,128)(2,1)S(1)} %get-tuple-element.69), channel_id=1, source_target_pairs={{0,1},{1,2},{2,3},{3,0},{4,5},{5,6},{6,7},{7,4},{8,9},{9,10},{10,1... | collective-permute-start | bytes 786440 | tf_op jit(solution)/shard_map/ppermute | solution.py:358
  81.8 16.6 %collective-permute-start.32 = (bf16[128,1024]{1,0:T(8,128)(2,1)S(1)}, bf16[128,1024]{1,0:T(8,128)(2,1)S(1)}, u32[]{:S(2)}, u32[]{:S(2)}) collective-permute-start(bf16[128,1024]{1,0:T(8,128)(2,1)S(1)} %get-tuple-element.77), channel_id=1, source_target_pairs={{0,17},{1,18},{2,19},{3,16},{4,21},{5,22},{6,23},{7,20},{8,25},{9,... | collective-permute-start | bytes 786440 | tf_op jit(solution)/shard_map/ppermute | solution.py:358
  93.4 20.2 %collective-permute-start.26 = (bf16[128,1024]{1,0:T(8,128)(2,1)}, bf16[128,1024]{1,0:T(8,128)(2,1)S(1)}, u32[]{:S(2)}, u32[]{:S(2)}) collective-permute-start(bf16[128,1024]{1,0:T(8,128)(2,1)} %get-tuple-element.72), channel_id=1, source_target_pairs={{0,2},{1,3},{2,0},{3,1},{4,6},{5,7},{6,4},{7,5},{8,10},{9,11},{10,... | collective-permute-start | bytes 786440 | tf_op jit(solution)/shard_map/ppermute | solution.py:358
  98.0 21.9 %collective-permute-start.27 = (bf16[128,1024]{1,0:T(8,128)(2,1)S(1)}, bf16[128,1024]{1,0:T(8,128)(2,1)S(1)}, u32[]{:S(2)}, u32[]{:S(2)}) collective-permute-start(bf16[128,1024]{1,0:T(8,128)(2,1)S(1)} %get-tuple-element.73), channel_id=1, source_target_pairs={{0,18},{1,19},{2,16},{3,17},{4,22},{5,23},{6,20},{7,21},{8,26},{9,... | collective-permute-start | bytes 786440 | tf_op jit(solution)/shard_map/ppermute | solution.py:358
  98.0 21.9 %collective-permute-start.28 = (bf16[128,1024]{1,0:T(8,128)(2,1)S(1)}, bf16[128,1024]{1,0:T(8,128)(2,1)S(1)}, u32[]{:S(2)}, u32[]{:S(2)}) collective-permute-start(bf16[128,1024]{1,0:T(8,128)(2,1)S(1)} %get-tuple-element.74), channel_id=1, source_target_pairs={{0,16},{1,17},{2,18},{3,19},{4,20},{5,21},{6,22},{7,23},{8,24},{9,... | collective-permute-start | bytes 786440 | tf_op jit(solution)/shard_map/ppermute | solution.py:358
  99.4 20.5 %all-to-all-start = ((f32[8,1,128]{2,1,0:T(1,128)}), f32[8,1,128]{2,1,0:T(1,128)S(1)}, u32[]{:S(2)}, u32[]{:S(2)}) async-start(f32[8,1,128]{2,1,0:T(1,128)} %bitcast.2), calls=%async_computation | async-start | bytes 8192 | tf_op jit(solution)/shard_map/all_to_all | solution.py:379

commit v5 on v4

--- a/solution.py
+++ b/solution.py
@@ -328,7 +328,7 @@
     across(1, 1, *side[0, 0])
     send(2, 1, *own[1, 0])
     send(3, 0, *own[1, 1])
-    send(3, 1, *own[2, 0])
+    send(3, 1, *own[1, 0], *own[1, 1])
     across(2, 0, *side[1, 0], *side[0, 1])
     across(2, 1, *side[1, 1])
     across(3, 0, *side[2, 0])

time: 123 us -> 123 us (level)
  no operation moved by 1% of the time
where the time goes in v5:
time: 123 us; the launch traced here: 122 us
  waiting for transfers between devices  51.5 us (42%)
  starting transfers between devices  39.6 us (32%)
  Pallas kernels  27.9 us (23%)
  local copies, waits for them, and re-layouts  2.27 us (2%)
    pallas_call x4, Pallas kernels, weigh(): pl.pallas_call(functools.partial(weigh_kernel, layout, row_stage, unit, s...  22.9 us
    ppermute x7, waiting for transfers between devices, local(): back[b] = lax.ppermute(result[b], AXES, to_owner(*hops[b], -1))  17.9 us
    ppermute x8, waiting for transfers between devices, across(): lax.ppermute(after(src, *deps) if deps else src, AXES, beside(2))  16.5 us
    ppermute x7, waiting for transfers between devices, send(): lax.ppermute(after(src, *deps) if deps else src, AXES, to_owner(*hops[k],...  13.8 us
    ppermute x7, starting transfers between devices, send(): lax.ppermute(after(src, *deps) if deps else src, AXES, to_owner(*hops[k],...  13.4 us
    ppermute x8, starting transfers between devices, across(): lax.ppermute(after(src, *deps) if deps else src, AXES, beside(2))  11.2 us
    ppermute x7, starting transfers between devices, local(): back[b] = lax.ppermute(result[b], AXES, to_owner(*hops[b], -1))  7.41 us
    all_to_all x1, starting transfers between devices, local(): lax.all_to_all(after(*dups, near), AXES, 0, 0, tiled=True, axis_index_gro...  5.28 us
  transfers between devices with their start and end apart: 34, of which 18 were waited for; matrix products, arithmetic and copies ran while one was open for 0% of the time, Pallas kernels for 18%

profile of v5, /device:TPU:0, one launch (start us, length us, event | category | flops | bytes accessed | tf_op | source)
XLA Modules:
  0.0 122.4 jit_solution(7024582010449503374)
XLA Ops:
  0.6 1.6 %copy-done = f32[512,1024]{1,0:T(8,128)S(1)} copy-done((f32[512,1024]{1,0:T(8,128)S(1)}, f32[512,1024]{1,0:T(8,128)}, u32[]{:S(2)}) %copy-start) | copy-done | bytes 2097176
  2.2 0.7 copy-done.1
  2.9 0.7 pack.1
  3.6 3.1 %collective-permute-start.3 = (bf16[128,1024]{1,0:T(8,128)(2,1)S(1)}, bf16[128,1024]{1,0:T(8,128)(2,1)S(1)}, u32[]{:S(2)}, u32[]{:S(2)}) collective-permute-start(bf16[128,1024]{1,0:T(8,128)(2,1)S(1)} %get-tuple-element.49), channel_id=1, source_target_pairs={{0,1},{1,2},{2,3},{3,0},{4,5},{5,6},{6,7},{7,4},{8,9},{9,10},{10,1... | collective-permute-start | bytes 786440 | tf_op jit(solution)/shard_map/ppermute | solution.py:244
  6.7 2.5 %collective-permute-start = (bf16[128,1024]{1,0:T(8,128)(2,1)S(1)}, bf16[128,1024]{1,0:T(8,128)(2,1)S(1)}, u32[]{:S(2)}, u32[]{:S(2)}) collective-permute-start(bf16[128,1024]{1,0:T(8,128)(2,1)S(1)} %get-tuple-element.46), channel_id=1, source_target_pairs={{0,17},{1,18},{2,19},{3,16},{4,21},{5,22},{6,23},{7,20},{8,25},{9,... | collective-permute-start | bytes 786440 | tf_op jit(solution)/shard_map/ppermute | solution.py:244
  9.2 1.0 pack_rest.1
  10.3 0.6 collective-permute-start.6
  10.8 5.0 %collective-permute-done.3.refs_0_.refs_6_.refs_8_ = bf16[128,1024]{1,0:T(8,128)(2,1)S(1)} collective-permute-done((bf16[128,1024]{1,0:T(8,128)(2,1)S(1)}, bf16[128,1024]{1,0:T(8,128)(2,1)S(1)}, u32[]{:S(2)}, u32[]{:S(2)}) %collective-permute-start.3) | collective-permute-done | bytes 262176 | tf_op jit(solution)/shard_map/ppermute | solution.py:244
  15.8 1.7 %collective-permute-start.9 = (bf16[128,1024]{1,0:T(8,128)(2,1)S(1)}, bf16[128,1024]{1,0:T(8,128)(2,1)S(1)}, u32[]{:S(2)}, u32[]{:S(2)}) collective-permute-start(bf16[128,1024]{1,0:T(8,128)(2,1)S(1)} %get-tuple-element.55.refs_2_.refs_3_.refs_4_), channel_id=1, source_target_pairs={{0,8},{1,9},{2,10},{3,11},{4,12},{5,13},{6,14},{7,15},{8,0},{9,1},... | collective-permute-start | bytes 786440 | tf_op jit(solution)/shard_map/ppermute | solution.py:254
  17.6 1.8 %collective-permute-start.2 = (bf16[128,1024]{1,0:T(8,128)(2,1)S(1)}, bf16[128,1024]{1,0:T(8,128)(2,1)S(1)}, u32[]{:S(2)}, u32[]{:S(2)}) collective-permute-start(bf16[128,1024]{1,0:T(8,128)(2,1)S(1)} %get-tuple-element.48), channel_id=1, source_target_pairs={{0,3},{1,0},{2,1},{3,2},{4,7},{5,4},{6,5},{7,6},{8,11},{9,8},{10,9... | collective-permute-start | bytes 786440 | tf_op jit(solution)/shard_map/ppermute | solution.py:244
  19.4 0.5 collective-permute-start.5
  19.9 3.5 %collective-permute-done.6.refs_3_.refs_2_.refs_5_ = bf16[128,1024]{1,0:T(8,128)(2,1)S(1)} collective-permute-done((bf16[128,1024]{1,0:T(8,128)(2,1)S(1)}, bf16[128,1024]{1,0:T(8,128)(2,1)S(1)}, u32[]{:S(2)}, u32[]{:S(2)}) %collective-permute-start.6) | collective-permute-done | bytes 262176 | tf_op jit(solution)/shard_map/ppermute | solution.py:244
  23.4 1.5 %collective-permute-start.7 = (bf16[128,1024]{1,0:T(8,128)(2,1)S(1)}, bf16[128,1024]{1,0:T(8,128)(2,1)S(1)}, u32[]{:S(2)}, u32[]{:S(2)}) collective-permute-start(bf16[128,1024]{1,0:T(8,128)(2,1)S(1)} %collective-permute-done.6.refs_3_.refs_2_.refs_5_), channel_id=1, source_target_pairs={{0,8},{1,9},{2,10},{3,11},{4,12},{5,13},{6,14},{7,15},{8,0},{9,1},... | collective-permute-start | bytes 786440 | tf_op jit(solution)/shard_map/ppermute | solution.py:254
  24.9 4.0 %collective-permute-start.4 = (bf16[128,1024]{1,0:T(8,128)(2,1)S(1)}, bf16[128,1024]{1,0:T(8,128)(2,1)S(1)}, u32[]{:S(2)}, u32[]{:S(2)}) collective-permute-start(bf16[128,1024]{1,0:T(8,128)(2,1)S(1)} %get-tuple-element.51), channel_id=1, source_target_pairs={{0,19},{1,16},{2,17},{3,18},{4,23},{5,20},{6,21},{7,22},{8,27},{9,... | collective-permute-start | bytes 786440 | tf_op jit(solution)/shard_map/ppermute | solution.py:244
  28.9 1.5 %collective-permute-start.10 = (bf16[128,1024]{1,0:T(8,128)(2,1)S(1)}, bf16[128,1024]{1,0:T(8,128)(2,1)S(1)}, u32[]{:S(2)}, u32[]{:S(2)}) collective-permute-start(bf16[128,1024]{1,0:T(8,128)(2,1)S(1)} %collective-permute-done.refs_1_.refs_7_.refs_9_), channel_id=1, source_target_pairs={{0,8},{1,9},{2,10},{3,11},{4,12},{5,13},{6,14},{7,15},{8,0},{9,1},... | collective-permute-start | bytes 786440 | tf_op jit(solution)/shard_map/ppermute | solution.py:254
  30.4 0.0 collective-permute-done.2.refs_2_.refs_0_.refs_10_.refs_12_
  30.4 0.0 collective-permute-start.1
  30.4 0.3 collective-permute-done.5.refs_8_.refs_10_
  30.7 5.6 %collective-permute-done.7.refs_5_.refs_7_ = bf16[128,1024]{1,0:T(8,128)(2,1)S(1)} collective-permute-done((bf16[128,1024]{1,0:T(8,128)(2,1)S(1)}, bf16[128,1024]{1,0:T(8,128)(2,1)S(1)}, u32[]{:S(2)}, u32[]{:S(2)}) %collective-permute-start.7) | collective-permute-done | bytes 262176 | tf_op jit(solution)/shard_map/ppermute | solution.py:254
  36.3 1.7 %collective-permute-start.8 = (bf16[128,1024]{1,0:T(8,128)(2,1)S(1)}, bf16[128,1024]{1,0:T(8,128)(2,1)S(1)}, u32[]{:S(2)}, u32[]{:S(2)}) collective-permute-start(bf16[128,1024]{1,0:T(8,128)(2,1)S(1)} %collective-permute-done.2.refs_2_.refs_0_.refs_10_.refs_12_), channel_id=1, source_target_pairs={{0,8},{1,9},{2,10},{3,11},{4,12},{5,13},{6,14},{7,15},{8,0},{9,1},... | collective-permute-start | bytes 786440 | tf_op jit(solution)/shard_map/ppermute | solution.py:254
  38.1 0.0 collective-permute-start.17
  38.1 0.0 collective-permute-done.4.refs_3_.refs_1_.refs_11_.refs_13_
  38.1 0.5 collective-permute-start.22
  38.6 3.4 %collective-permute-done.10.refs_9_.refs_11_ = bf16[128,1024]{1,0:T(8,128)(2,1)S(1)} collective-permute-done((bf16[128,1024]{1,0:T(8,128)(2,1)S(1)}, bf16[128,1024]{1,0:T(8,128)(2,1)S(1)}, u32[]{:S(2)}, u32[]{:S(2)}) %collective-permute-start.10) | collective-permute-done | bytes 262176 | tf_op jit(solution)/shard_map/ppermute | solution.py:254
  41.9 1.7 %collective-permute-start.11 = (bf16[128,1024]{1,0:T(8,128)(2,1)S(1)}, bf16[128,1024]{1,0:T(8,128)(2,1)S(1)}, u32[]{:S(2)}, u32[]{:S(2)}) collective-permute-start(bf16[128,1024]{1,0:T(8,128)(2,1)S(1)} %collective-permute-done.4.refs_3_.refs_1_.refs_11_.refs_13_), channel_id=1, source_target_pairs={{0,8},{1,9},{2,10},{3,11},{4,12},{5,13},{6,14},{7,15},{8,0},{9,1},... | collective-permute-start | bytes 786440 | tf_op jit(solution)/shard_map/ppermute | solution.py:254
  43.7 0.2 collective-permute-done.1.refs_6_.refs_14_.refs_0_.refs_16_
  43.9 1.4 %collective-permute-start.12 = (bf16[128,1024]{1,0:T(8,128)(2,1)S(1)}, bf16[128,1024]{1,0:T(8,128)(2,1)S(1)}, u32[]{:S(2)}, u32[]{:S(2)}) collective-permute-start(bf16[128,1024]{1,0:T(8,128)(2,1)S(1)} %get-tuple-element.59), channel_id=1, source_target_pairs={{0,18},{1,19},{2,16},{3,17},{4,22},{5,23},{6,20},{7,21},{8,26},{9,... | collective-permute-start | bytes 786440 | tf_op jit(solution)/shard_map/ppermute | solution.py:244
  45.2 2.3 %collective-permute-done.8.refs_4_.refs_12_.refs_14_ = bf16[128,1024]{1,0:T(8,128)(2,1)S(1)} collective-permute-done((bf16[128,1024]{1,0:T(8,128)(2,1)S(1)}, bf16[128,1024]{1,0:T(8,128)(2,1)S(1)}, u32[]{:S(2)}, u32[]{:S(2)}) %collective-permute-start.8) | collective-permute-done | bytes 262176 | tf_op jit(solution)/shard_map/ppermute | solution.py:254
  47.6 0.5 collective-permute-start.18
  48.1 0.1 collective-permute-start.23
  48.1 2.5 %collective-permute-done.11.refs_5_.refs_13_.refs_15_ = bf16[128,1024]{1,0:T(8,128)(2,1)S(1)} collective-permute-done((bf16[128,1024]{1,0:T(8,128)(2,1)S(1)}, bf16[128,1024]{1,0:T(8,128)(2,1)S(1)}, u32[]{:S(2)}, u32[]{:S(2)}) %collective-permute-start.11) | collective-permute-done | bytes 262176 | tf_op jit(solution)/shard_map/ppermute | solution.py:254
  50.6 1.2 %collective-permute-start.13 = (bf16[128,1024]{1,0:T(8,128)(2,1)S(1)}, bf16[128,1024]{1,0:T(8,128)(2,1)S(1)}, u32[]{:S(2)}, u32[]{:S(2)}) collective-permute-start(bf16[128,1024]{1,0:T(8,128)(2,1)S(1)} %collective-permute-done.1.refs_6_.refs_14_.refs_0_.refs_16_), channel_id=1, source_target_pairs={{0,8},{1,9},{2,10},{3,11},{4,12},{5,13},{6,14},{7,15},{8,0},{9,1},... | collective-permute-start | bytes 786440 | tf_op jit(solution)/shard_map/ppermute | solution.py:254
  51.8 0.1 pad_maximum_fusion
  51.9 5.1 %collective-permute-done.12.refs_7_.refs_15_.refs_1_.refs_17_ = bf16[128,1024]{1,0:T(8,128)(2,1)S(1)} collective-permute-done((bf16[128,1024]{1,0:T(8,128)(2,1)S(1)}, bf16[128,1024]{1,0:T(8,128)(2,1)S(1)}, u32[]{:S(2)}, u32[]{:S(2)}) %collective-permute-start.12) | collective-permute-done | bytes 262176 | tf_op jit(solution)/shard_map/ppermute | solution.py:244
  57.0 0.0 collective-permute-start.15
  57.0 0.5 collective-permute-start.19
  57.6 0.1 collective-permute-start.20
  57.6 0.0 collective-permute-done.23.refs_16_.refs_24_.refs_26_
  57.6 0.4 collective-permute-start.24
  58.1 1.2 %collective-permute-start.14 = (bf16[128,1024]{1,0:T(8,128)(2,1)S(1)}, bf16[128,1024]{1,0:T(8,128)(2,1)S(1)}, u32[]{:S(2)}, u32[]{:S(2)}) collective-permute-start(bf16[128,1024]{1,0:T(8,128)(2,1)S(1)} %collective-permute-done.12.refs_7_.refs_15_.refs_1_.refs_17_), channel_id=1, source_target_pairs={{0,8},{1,9},{2,10},{3,11},{4,12},{5,13},{6,14},{7,15},{8,0},{9,1},... | collective-permute-start | bytes 786440 | tf_op jit(solution)/shard_map/ppermute | solution.py:254
  59.4 0.7 collective-permute-done.19.refs_12_.refs_20_.refs_22_
  60.1 0.1 collective-permute-start.16
  60.2 0.2 collective-permute-done.20.refs_13_.refs_21_.refs_23_
  60.4 0.4 collective-permute-done.24.refs_17_.refs_25_.refs_27_
  60.8 3.0 %weigh.4 = (f32[256,1024]{1,0:T(8,128)S(1)}, f32[256,128]{1,0:T(8,128)S(1)}) custom-call(bf16[128,1024]{1,0:T(8,128)(2,1)S(1)} %collective-permute-done.3.refs_0_.refs_6_.refs_8_, bf16[128,1024]{1,0:T(8,128)(2,1)S(1)} %collective-permute-done.refs_1_.refs_7_.refs_9_, bf16[128,1024]{1,0:T(8,128)(2,1)S(1)} %get-tuple-element.55.refs_2_.refs_3_.refs_4_, ...), custom_call_target="tpu_custom_call" | custom-call | tf_op jit(solution)/shard_map/weigh/pallas_call | solution.py:294
  63.9 2.5 %collective-permute-done.14.refs_9_.refs_17_.refs_19_ = bf16[128,1024]{1,0:T(8,128)(2,1)S(1)} collective-permute-done((bf16[128,1024]{1,0:T(8,128)(2,1)S(1)}, bf16[128,1024]{1,0:T(8,128)(2,1)S(1)}, u32[]{:S(2)}, u32[]{:S(2)}) %collective-permute-start.14) | collective-permute-done | bytes 262176 | tf_op jit(solution)/shard_map/ppermute | solution.py:254
  66.4 0.1 collective-permute-start.25
  66.5 1.9 %collective-permute-done.25.refs_12_.refs_28_.refs_30_ = bf16[256,1024]{1,0:T(8,128)(2,1)S(1)} collective-permute-done((bf16[256,1024]{1,0:T(8,128)(2,1)S(1)}, bf16[256,1024]{1,0:T(8,128)(2,1)S(1)}, u32[]{:S(2)}, u32[]{:S(2)}) %collective-permute-start.25) | collective-permute-done | bytes 524320 | tf_op jit(solution)/shard_map/ppermute | solution.py:260
  68.4 3.1 %weigh.5 = (bf16[128,1024]{1,0:T(8,128)(2,1)S(1)}, bf16[128,1024]{1,0:T(8,128)(2,1)S(1)}, f32[8,128]{1,0:T(8,128)S(1)}) custom-call(bf16[128,1024]{1,0:T(8,128)(2,1)S(1)} %collective-permute-done.3.refs_0_.refs_6_.refs_8_, bf16[128,1024]{1,0:T(8,128)(2,1)S(1)} %collective-permute-done.refs_1_.refs_7_.refs_9_, ...), custom_call_target="tpu_custom_call" | custom-call | flops 2147483648 | bytes 4194304 | tf_op jit(solution)/shard_map/weigh/pallas_call | solution.py:294
  71.4 1.4 %collective-permute-start.29 = (bf16[128,1024]{1,0:T(8,128)(2,1)S(1)}, bf16[128,1024]{1,0:T(8,128)(2,1)S(1)}, u32[]{:S(2)}, u32[]{:S(2)}) collective-permute-start(bf16[128,1024]{1,0:T(8,128)(2,1)S(1)} %get-tuple-element.66), channel_id=1, source_target_pairs={{0,3},{1,0},{2,1},{3,2},{4,7},{5,4},{6,5},{7,6},{8,11},{9,8},{10,9... | collective-permute-start | bytes 786440 | tf_op jit(solution)/shard_map/ppermute | solution.py:358
  72.9 1.2 collective-permute-start.30
  74.1 5.8 %weigh.6 = (bf16[128,1024]{1,0:T(8,128)(2,1)S(1)}, bf16[128,1024]{1,0:T(8,128)(2,1)S(1)}, f32[8,128]{1,0:T(8,128)S(1)}) custom-call(bf16[128,1024]{1,0:T(8,128)(2,1)S(1)} %collective-permute-done.2.refs_2_.refs_0_.refs_10_.refs_12_, bf16[128,1024]{1,0:T(8,128)(2,1)S(1)} %collective-permute-done.4.refs_3_.refs_1_.refs_11_.refs_13_, ...), custom_call_target="tpu_custom_call" | custom-call | flops 4294967296 | bytes 8388608 | tf_op jit(solution)/shard_map/weigh/pallas_call | solution.py:294
  79.9 1.8 %collective-permute-start.31 = (bf16[128,1024]{1,0:T(8,128)(2,1)S(1)}, bf16[128,1024]{1,0:T(8,128)(2,1)S(1)}, u32[]{:S(2)}, u32[]{:S(2)}) collective-permute-start(bf16[128,1024]{1,0:T(8,128)(2,1)S(1)} %get-tuple-element.69), channel_id=1, source_target_pairs={{0,1},{1,2},{2,3},{3,0},{4,5},{5,6},{6,7},{7,4},{8,9},{9,10},{10,1... | collective-permute-start | bytes 786440 | tf_op jit(solution)/shard_map/ppermute | solution.py:358
  81.8 0.6 collective-permute-start.32
  82.4 11.0 %weigh.7 = (bf16[128,1024]{1,0:T(8,128)(2,1)}, bf16[128,1024]{1,0:T(8,128)(2,1)S(1)}, bf16[128,1024]{1,0:T(8,128)(2,1)S(1)}, bf16[128,1024]{1,0:T(8,128)(2,1)S(1)}, f32[8,128]{1,0:T(8,128)}) custom-call(bf16[128,1024]{1,0:T(8,128)(2,1)S(1)} %collective-permute-done.1.refs_6_.refs_14_.refs_0_.refs_16_, ...), custom_call_target="tpu_custom_call" | custom-call | flops 8589934592 | bytes 8388608 | tf_op jit(solution)/shard_map/weigh/pallas_call | solution.py:294
  93.4 1.9 %collective-permute-start.26 = (bf16[128,1024]{1,0:T(8,128)(2,1)}, bf16[128,1024]{1,0:T(8,128)(2,1)S(1)}, u32[]{:S(2)}, u32[]{:S(2)}) collective-permute-start(bf16[128,1024]{1,0:T(8,128)(2,1)} %get-tuple-element.72), channel_id=1, source_target_pairs={{0,2},{1,3},{2,0},{3,1},{4,6},{5,7},{6,4},{7,5},{8,10},{9,11},{10,... | collective-permute-start | bytes 786440 | tf_op jit(solution)/shard_map/ppermute | solution.py:358
  95.3 2.7 %collective-permute-done.30.refs_2_ = bf16[128,1024]{1,0:T(8,128)(2,1)S(1)} collective-permute-done((bf16[128,1024]{1,0:T(8,128)(2,1)S(1)}, bf16[128,1024]{1,0:T(8,128)(2,1)S(1)}, u32[]{:S(2)}, u32[]{:S(2)}) %collective-permute-start.30) | collective-permute-done | bytes 262176 | tf_op jit(solution)/shard_map/ppermute | solution.py:358
  98.0 0.4 collective-permute-start.28
  98.4 1.0 unpack.2.refs_3_
  99.4 5.3 %all-to-all-start = ((f32[8,1,128]{2,1,0:T(1,128)}), f32[8,1,128]{2,1,0:T(1,128)S(1)}, u32[]{:S(2)}, u32[]{:S(2)}) async-start(f32[8,1,128]{2,1,0:T(1,128)} %bitcast.2), calls=%async_computation | async-start | bytes 8192 | tf_op jit(solution)/shard_map/all_to_all | solution.py:379
  104.7 8.8 %collective-permute-done.26.refs_0_ = bf16[128,1024]{1,0:T(8,128)(2,1)S(1)} collective-permute-done((bf16[128,1024]{1,0:T(8,128)(2,1)}, bf16[128,1024]{1,0:T(8,128)(2,1)S(1)}, u32[]{:S(2)}, u32[]{:S(2)}) %collective-permute-start.26) | collective-permute-done | bytes 262176 | tf_op jit(solution)/shard_map/ppermute | solution.py:358
  113.5 6.4 %collective-permute-done.27.refs_1_ = bf16[128,1024]{1,0:T(8,128)(2,1)S(1)} collective-permute-done((bf16[128,1024]{1,0:T(8,128)(2,1)S(1)}, bf16[128,1024]{1,0:T(8,128)(2,1)S(1)}, u32[]{:S(2)}, u32[]{:S(2)}) %collective-permute-start.27) | collective-permute-done | bytes 262176 | tf_op jit(solution)/shard_map/ppermute | solution.py:358
  119.9 0.1 all-to-all-done
  120.0 2.3 %unpack.3 = (f32[512,1024]{1,0:T(8,128)}, f32[1,512]{1,0:T(1,128)}) custom-call(s32[1,512]{1,0:T(1,128)S(1)} %get-tuple-element.42.pos_ref, bf16[128,1024]{1,0:T(8,128)(2,1)S(1)} %collective-permute-done.26.refs_0_, bf16[128,1024]{1,0:T(8,128)(2,1)S(1)} %collective-permute-done.27.refs_1_, bf16[128,1024]{1,0:T(8,128)(2,1)S(1)} %collective-permute-done.28.refs_2_, ...), custom_call_target="tpu_custom_call" | custom-call | tf_op jit(solution)/shard_map/unpack/pallas_call | solution.py:367
  (19 shorter events, 0.1 us)
Async XLA Ops:
  0.6 1.6 %copy-start = (f32[512,1024]{1,0:T(8,128)S(1)}, f32[512,1024]{1,0:T(8,128)}, u32[]{:S(2)}) copy-start(f32[512,1024]{1,0:T(8,128)} %emb_ref.1) | copy-start | bytes 6291460
  2.2 0.7 copy-start.1
  3.6 12.2 %collective-permute-start.3 = (bf16[128,1024]{1,0:T(8,128)(2,1)S(1)}, bf16[128,1024]{1,0:T(8,128)(2,1)S(1)}, u32[]{:S(2)}, u32[]{:S(2)}) collective-permute-start(bf16[128,1024]{1,0:T(8,128)(2,1)S(1)} %get-tuple-element.49), channel_id=1, source_target_pairs={{0,1},{1,2},{2,3},{3,0},{4,5},{5,6},{6,7},{7,4},{8,9},{9,10},{10,1... | collective-permute-start | bytes 786440 | tf_op jit(solution)/shard_map/ppermute | solution.py:244
  6.7 18.2 %collective-permute-start = (bf16[128,1024]{1,0:T(8,128)(2,1)S(1)}, bf16[128,1024]{1,0:T(8,128)(2,1)S(1)}, u32[]{:S(2)}, u32[]{:S(2)}) collective-permute-start(bf16[128,1024]{1,0:T(8,128)(2,1)S(1)} %get-tuple-element.46), channel_id=1, source_target_pairs={{0,17},{1,18},{2,19},{3,16},{4,21},{5,22},{6,23},{7,20},{8,25},{9,... | collective-permute-start | bytes 786440 | tf_op jit(solution)/shard_map/ppermute | solution.py:244
  10.3 13.2 %collective-permute-start.6 = (bf16[128,1024]{1,0:T(8,128)(2,1)S(1)}, bf16[128,1024]{1,0:T(8,128)(2,1)S(1)}, u32[]{:S(2)}, u32[]{:S(2)}) collective-permute-start(bf16[128,1024]{1,0:T(8,128)(2,1)S(1)} %get-tuple-element.52), channel_id=1, source_target_pairs={{0,16},{1,17},{2,18},{3,19},{4,20},{5,21},{6,22},{7,23},{8,24},{9,... | collective-permute-start | bytes 786440 | tf_op jit(solution)/shard_map/ppermute | solution.py:244
  15.8 13.1 %collective-permute-start.9 = (bf16[128,1024]{1,0:T(8,128)(2,1)S(1)}, bf16[128,1024]{1,0:T(8,128)(2,1)S(1)}, u32[]{:S(2)}, u32[]{:S(2)}) collective-permute-start(bf16[128,1024]{1,0:T(8,128)(2,1)S(1)} %get-tuple-element.55.refs_2_.refs_3_.refs_4_), channel_id=1, source_target_pairs={{0,8},{1,9},{2,10},{3,11},{4,12},{5,13},{6,14},{7,15},{8,0},{9,1},... | collective-permute-start | bytes 786440 | tf_op jit(solution)/shard_map/ppermute | solution.py:254
  17.6 12.9 %collective-permute-start.2 = (bf16[128,1024]{1,0:T(8,128)(2,1)S(1)}, bf16[128,1024]{1,0:T(8,128)(2,1)S(1)}, u32[]{:S(2)}, u32[]{:S(2)}) collective-permute-start(bf16[128,1024]{1,0:T(8,128)(2,1)S(1)} %get-tuple-element.48), channel_id=1, source_target_pairs={{0,3},{1,0},{2,1},{3,2},{4,7},{5,4},{6,5},{7,6},{8,11},{9,8},{10,9... | collective-permute-start | bytes 786440 | tf_op jit(solution)/shard_map/ppermute | solution.py:244
  19.4 11.3 %collective-permute-start.5 = (bf16[128,1024]{1,0:T(8,128)(2,1)S(1)}, bf16[128,1024]{1,0:T(8,128)(2,1)S(1)}, u32[]{:S(2)}, u32[]{:S(2)}) collective-permute-start(bf16[128,1024]{1,0:T(8,128)(2,1)S(1)} %collective-permute-done.3.refs_0_.refs_6_.refs_8_), channel_id=1, source_target_pairs={{0,8},{1,9},{2,10},{3,11},{4,12},{5,13},{6,14},{7,15},{8,0},{9,1},... | collective-permute-start | bytes 786440 | tf_op jit(solution)/shard_map/ppermute | solution.py:254
  23.4 12.9 %collective-permute-start.7 = (bf16[128,1024]{1,0:T(8,128)(2,1)S(1)}, bf16[128,1024]{1,0:T(8,128)(2,1)S(1)}, u32[]{:S(2)}, u32[]{:S(2)}) collective-permute-start(bf16[128,1024]{1,0:T(8,128)(2,1)S(1)} %collective-permute-done.6.refs_3_.refs_2_.refs_5_), channel_id=1, source_target_pairs={{0,8},{1,9},{2,10},{3,11},{4,12},{5,13},{6,14},{7,15},{8,0},{9,1},... | collective-permute-start | bytes 786440 | tf_op jit(solution)/shard_map/ppermute | solution.py:254
  24.9 13.1 %collective-permute-start.4 = (bf16[128,1024]{1,0:T(8,128)(2,1)S(1)}, bf16[128,1024]{1,0:T(8,128)(2,1)S(1)}, u32[]{:S(2)}, u32[]{:S(2)}) collective-permute-start(bf16[128,1024]{1,0:T(8,128)(2,1)S(1)} %get-tuple-element.51), channel_id=1, source_target_pairs={{0,19},{1,16},{2,17},{3,18},{4,23},{5,20},{6,21},{7,22},{8,27},{9,... | collective-permute-start | bytes 786440 | tf_op jit(solution)/shard_map/ppermute | solution.py:244
  28.9 13.0 %collective-permute-start.10 = (bf16[128,1024]{1,0:T(8,128)(2,1)S(1)}, bf16[128,1024]{1,0:T(8,128)(2,1)S(1)}, u32[]{:S(2)}, u32[]{:S(2)}) collective-permute-start(bf16[128,1024]{1,0:T(8,128)(2,1)S(1)} %collective-permute-done.refs_1_.refs_7_.refs_9_), channel_id=1, source_target_pairs={{0,8},{1,9},{2,10},{3,11},{4,12},{5,13},{6,14},{7,15},{8,0},{9,1},... | collective-permute-start | bytes 786440 | tf_op jit(solution)/shard_map/ppermute | solution.py:254
  30.4 13.4 %collective-permute-start.1 = (bf16[128,1024]{1,0:T(8,128)(2,1)S(1)}, bf16[128,1024]{1,0:T(8,128)(2,1)S(1)}, u32[]{:S(2)}, u32[]{:S(2)}) collective-permute-start(bf16[128,1024]{1,0:T(8,128)(2,1)S(1)} %get-tuple-element.47), channel_id=1, source_target_pairs={{0,2},{1,3},{2,0},{3,1},{4,6},{5,7},{6,4},{7,5},{8,10},{9,11},{10,... | collective-permute-start | bytes 786440 | tf_op jit(solution)/shard_map/ppermute | solution.py:244
  36.3 11.2 %collective-permute-start.8 = (bf16[128,1024]{1,0:T(8,128)(2,1)S(1)}, bf16[128,1024]{1,0:T(8,128)(2,1)S(1)}, u32[]{:S(2)}, u32[]{:S(2)}) collective-permute-start(bf16[128,1024]{1,0:T(8,128)(2,1)S(1)} %collective-permute-done.2.refs_2_.refs_0_.refs_10_.refs_12_), channel_id=1, source_target_pairs={{0,8},{1,9},{2,10},{3,11},{4,12},{5,13},{6,14},{7,15},{8,0},{9,1},... | collective-permute-start | bytes 786440 | tf_op jit(solution)/shard_map/ppermute | solution.py:254
  38.1 9.5 %collective-permute-start.17 = (bf16[128,1024]{1,0:T(8,128)(2,1)S(1)}, bf16[128,1024]{1,0:T(8,128)(2,1)S(1)}, u32[]{:S(2)}, u32[]{:S(2)}) collective-permute-start(bf16[128,1024]{1,0:T(8,128)(2,1)S(1)} %get-tuple-element.55.refs_2_.refs_3_.refs_4_), channel_id=1, source_target_pairs={{0,4},{1,5},{2,6},{3,7},{4,0},{5,1},{6,2},{7,3},{8,12},{9,13},{10,... | collective-permute-start | bytes 786440 | tf_op jit(solution)/shard_map/ppermute | solution.py:265
  38.1 10.0 %collective-permute-start.22 = (bf16[128,1024]{1,0:T(8,128)(2,1)S(1)}, bf16[128,1024]{1,0:T(8,128)(2,1)S(1)}, u32[]{:S(2)}, u32[]{:S(2)}) collective-permute-start(bf16[128,1024]{1,0:T(8,128)(2,1)S(1)} %collective-permute-done.refs_1_.refs_7_.refs_9_), channel_id=1, source_target_pairs={{0,4},{1,5},{2,6},{3,7},{4,0},{5,1},{6,2},{7,3},{8,12},{9,13},{10,... | collective-permute-start | bytes 786440 | tf_op jit(solution)/shard_map/ppermute | solution.py:265
  41.9 8.7 %collective-permute-start.11 = (bf16[128,1024]{1,0:T(8,128)(2,1)S(1)}, bf16[128,1024]{1,0:T(8,128)(2,1)S(1)}, u32[]{:S(2)}, u32[]{:S(2)}) collective-permute-start(bf16[128,1024]{1,0:T(8,128)(2,1)S(1)} %collective-permute-done.4.refs_3_.refs_1_.refs_11_.refs_13_), channel_id=1, source_target_pairs={{0,8},{1,9},{2,10},{3,11},{4,12},{5,13},{6,14},{7,15},{8,0},{9,1},... | collective-permute-start | bytes 786440 | tf_op jit(solution)/shard_map/ppermute | solution.py:254
  43.9 13.2 %collective-permute-start.12 = (bf16[128,1024]{1,0:T(8,128)(2,1)S(1)}, bf16[128,1024]{1,0:T(8,128)(2,1)S(1)}, u32[]{:S(2)}, u32[]{:S(2)}) collective-permute-start(bf16[128,1024]{1,0:T(8,128)(2,1)S(1)} %get-tuple-element.59), channel_id=1, source_target_pairs={{0,18},{1,19},{2,16},{3,17},{4,22},{5,23},{6,20},{7,21},{8,26},{9,... | collective-permute-start | bytes 786440 | tf_op jit(solution)/shard_map/ppermute | solution.py:244
  47.5 9.5 %collective-permute-start.21 = (bf16[128,1024]{1,0:T(8,128)(2,1)S(1)}, bf16[128,1024]{1,0:T(8,128)(2,1)S(1)}, u32[]{:S(2)}, u32[]{:S(2)}) collective-permute-start(bf16[128,1024]{1,0:T(8,128)(2,1)S(1)} %collective-permute-done.3.refs_0_.refs_6_.refs_8_), channel_id=1, source_target_pairs={{0,4},{1,5},{2,6},{3,7},{4,0},{5,1},{6,2},{7,3},{8,12},{9,13},{10,... | collective-permute-start | bytes 786440 | tf_op jit(solution)/shard_map/ppermute | solution.py:265
  47.6 10.0 %collective-permute-start.18 = (bf16[128,1024]{1,0:T(8,128)(2,1)S(1)}, bf16[128,1024]{1,0:T(8,128)(2,1)S(1)}, u32[]{:S(2)}, u32[]{:S(2)}) collective-permute-start(bf16[128,1024]{1,0:T(8,128)(2,1)S(1)} %collective-permute-done.6.refs_3_.refs_2_.refs_5_), channel_id=1, source_target_pairs={{0,4},{1,5},{2,6},{3,7},{4,0},{5,1},{6,2},{7,3},{8,12},{9,13},{10,... | collective-permute-start | bytes 786440 | tf_op jit(solution)/shard_map/ppermute | solution.py:265
  48.1 9.6 %collective-permute-start.23 = (bf16[128,1024]{1,0:T(8,128)(2,1)S(1)}, bf16[128,1024]{1,0:T(8,128)(2,1)S(1)}, u32[]{:S(2)}, u32[]{:S(2)}) collective-permute-start(bf16[128,1024]{1,0:T(8,128)(2,1)S(1)} %collective-permute-done.5.refs_8_.refs_10_), channel_id=1, source_target_pairs={{0,4},{1,5},{2,6},{3,7},{4,0},{5,1},{6,2},{7,3},{8,12},{9,13},{10,... | collective-permute-start | bytes 786440 | tf_op jit(solution)/shard_map/ppermute | solution.py:265
  50.6 7.5 %collective-permute-start.13 = (bf16[128,1024]{1,0:T(8,128)(2,1)S(1)}, bf16[128,1024]{1,0:T(8,128)(2,1)S(1)}, u32[]{:S(2)}, u32[]{:S(2)}) collective-permute-start(bf16[128,1024]{1,0:T(8,128)(2,1)S(1)} %collective-permute-done.1.refs_6_.refs_14_.refs_0_.refs_16_), channel_id=1, source_target_pairs={{0,8},{1,9},{2,10},{3,11},{4,12},{5,13},{6,14},{7,15},{8,0},{9,1},... | collective-permute-start | bytes 786440 | tf_op jit(solution)/shard_map/ppermute | solution.py:254
  57.0 11.3 %collective-permute-start.15 = (bf16[512,1024]{1,0:T(8,128)(2,1)S(1)}, bf16[512,1024]{1,0:T(8,128)(2,1)S(1)}, u32[]{:S(2)}, u32[]{:S(2)}) collective-permute-start(bf16[512,1024]{1,0:T(8,128)(2,1)S(1)} %pad_maximum_fusion), channel_id=1, source_target_pairs={{0,4},{1,5},{2,6},{3,7},{4,0},{5,1},{6,2},{7,3},{8,12},{9,13},{10,... | collective-permute-start | bytes 3145736 | tf_op jit(solution)/shard_map/ppermute | solution.py:260
  57.0 3.0 %collective-permute-start.19 = (bf16[128,1024]{1,0:T(8,128)(2,1)S(1)}, bf16[128,1024]{1,0:T(8,128)(2,1)S(1)}, u32[]{:S(2)}, u32[]{:S(2)}) collective-permute-start(bf16[128,1024]{1,0:T(8,128)(2,1)S(1)} %collective-permute-done.9.refs_4_.refs_6_), channel_id=1, source_target_pairs={{0,4},{1,5},{2,6},{3,7},{4,0},{5,1},{6,2},{7,3},{8,12},{9,13},{10,... | collective-permute-start | bytes 786440 | tf_op jit(solution)/shard_map/ppermute | solution.py:265
  57.6 2.9 %collective-permute-start.20 = (bf16[128,1024]{1,0:T(8,128)(2,1)S(1)}, bf16[128,1024]{1,0:T(8,128)(2,1)S(1)}, u32[]{:S(2)}, u32[]{:S(2)}) collective-permute-start(bf16[128,1024]{1,0:T(8,128)(2,1)S(1)} %collective-permute-done.7.refs_5_.refs_7_), channel_id=1, source_target_pairs={{0,4},{1,5},{2,6},{3,7},{4,0},{5,1},{6,2},{7,3},{8,12},{9,13},{10,... | collective-permute-start | bytes 786440 | tf_op jit(solution)/shard_map/ppermute | solution.py:265
  57.6 3.2 %collective-permute-start.24 = (bf16[128,1024]{1,0:T(8,128)(2,1)S(1)}, bf16[128,1024]{1,0:T(8,128)(2,1)S(1)}, u32[]{:S(2)}, u32[]{:S(2)}) collective-permute-start(bf16[128,1024]{1,0:T(8,128)(2,1)S(1)} %collective-permute-done.10.refs_9_.refs_11_), channel_id=1, source_target_pairs={{0,4},{1,5},{2,6},{3,7},{4,0},{5,1},{6,2},{7,3},{8,12},{9,13},{10,... | collective-permute-start | bytes 786440 | tf_op jit(solution)/shard_map/ppermute | solution.py:265
  58.1 8.3 %collective-permute-start.14 = (bf16[128,1024]{1,0:T(8,128)(2,1)S(1)}, bf16[128,1024]{1,0:T(8,128)(2,1)S(1)}, u32[]{:S(2)}, u32[]{:S(2)}) collective-permute-start(bf16[128,1024]{1,0:T(8,128)(2,1)S(1)} %collective-permute-done.12.refs_7_.refs_15_.refs_1_.refs_17_), channel_id=1, source_target_pairs={{0,8},{1,9},{2,10},{3,11},{4,12},{5,13},{6,14},{7,15},{8,0},{9,1},... | collective-permute-start | bytes 786440 | tf_op jit(solution)/shard_map/ppermute | solution.py:254
  60.1 6.4 %collective-permute-start.16 = (bf16[256,1024]{1,0:T(8,128)(2,1)S(1)}, bf16[256,1024]{1,0:T(8,128)(2,1)S(1)}, u32[]{:S(2)}, u32[]{:S(2)}) collective-permute-start(bf16[256,1024]{1,0:T(8,128)(2,1)S(1)} %pad_maximum_fusion.1), channel_id=1, source_target_pairs={{0,4},{1,5},{2,6},{3,7},{4,0},{5,1},{6,2},{7,3},{8,12},{9,13},{10,... | collective-permute-start | bytes 1572872 | tf_op jit(solution)/shard_map/ppermute | solution.py:260
  66.4 2.0 %collective-permute-start.25 = (bf16[256,1024]{1,0:T(8,128)(2,1)S(1)}, bf16[256,1024]{1,0:T(8,128)(2,1)S(1)}, u32[]{:S(2)}, u32[]{:S(2)}) collective-permute-start(bf16[256,1024]{1,0:T(8,128)(2,1)S(1)} %pad_maximum_fusion.2), channel_id=1, source_target_pairs={{0,4},{1,5},{2,6},{3,7},{4,0},{5,1},{6,2},{7,3},{8,12},{9,13},{10,... | collective-permute-start | bytes 1572872 | tf_op jit(solution)/shard_map/ppermute | solution.py:260
  71.4 26.6 %collective-permute-start.29 = (bf16[128,1024]{1,0:T(8,128)(2,1)S(1)}, bf16[128,1024]{1,0:T(8,128)(2,1)S(1)}, u32[]{:S(2)}, u32[]{:S(2)}) collective-permute-start(bf16[128,1024]{1,0:T(8,128)(2,1)S(1)} %get-tuple-element.66), channel_id=1, source_target_pairs={{0,3},{1,0},{2,1},{3,2},{4,7},{5,4},{6,5},{7,6},{8,11},{9,8},{10,9... | collective-permute-start | bytes 786440 | tf_op jit(solution)/shard_map/ppermute | solution.py:358
  72.9 25.1 %collective-permute-start.30 = (bf16[128,1024]{1,0:T(8,128)(2,1)S(1)}, bf16[128,1024]{1,0:T(8,128)(2,1)S(1)}, u32[]{:S(2)}, u32[]{:S(2)}) collective-permute-start(bf16[128,1024]{1,0:T(8,128)(2,1)S(1)} %get-tuple-element.76), channel_id=1, source_target_pairs={{0,19},{1,16},{2,17},{3,18},{4,23},{5,20},{6,21},{7,22},{8,27},{9,... | collective-permute-start | bytes 786440 | tf_op jit(solution)/shard_map/ppermute | solution.py:358
  79.9 18.5 %collective-permute-start.31 = (bf16[128,1024]{1,0:T(8,128)(2,1)S(1)}, bf16[128,1024]{1,0:T(8,128)(2,1)S(1)}, u32[]{:S(2)}, u32[]{:S(2)}) collective-permute-start(bf16[128,1024]{1,0:T(8,128)(2,1)S(1)} %get-tuple-element.69), channel_id=1, source_target_pairs={{0,1},{1,2},{2,3},{3,0},{4,5},{5,6},{6,7},{7,4},{8,9},{9,10},{10,1... | collective-permute-start | bytes 786440 | tf_op jit(solution)/shard_map/ppermute | solution.py:358
  81.8 16.6 %collective-permute-start.32 = (bf16[128,1024]{1,0:T(8,128)(2,1)S(1)}, bf16[128,1024]{1,0:T(8,128)(2,1)S(1)}, u32[]{:S(2)}, u32[]{:S(2)}) collective-permute-start(bf16[128,1024]{1,0:T(8,128)(2,1)S(1)} %get-tuple-element.77), channel_id=1, source_target_pairs={{0,17},{1,18},{2,19},{3,16},{4,21},{5,22},{6,23},{7,20},{8,25},{9,... | collective-permute-start | bytes 786440 | tf_op jit(solution)/shard_map/ppermute | solution.py:358
  93.4 20.2 %collective-permute-start.26 = (bf16[128,1024]{1,0:T(8,128)(2,1)}, bf16[128,1024]{1,0:T(8,128)(2,1)S(1)}, u32[]{:S(2)}, u32[]{:S(2)}) collective-permute-start(bf16[128,1024]{1,0:T(8,128)(2,1)} %get-tuple-element.72), channel_id=1, source_target_pairs={{0,2},{1,3},{2,0},{3,1},{4,6},{5,7},{6,4},{7,5},{8,10},{9,11},{10,... | collective-permute-start | bytes 786440 | tf_op jit(solution)/shard_map/ppermute | solution.py:358
  98.0 21.9 %collective-permute-start.27 = (bf16[128,1024]{1,0:T(8,128)(2,1)S(1)}, bf16[128,1024]{1,0:T(8,128)(2,1)S(1)}, u32[]{:S(2)}, u32[]{:S(2)}) collective-permute-start(bf16[128,1024]{1,0:T(8,128)(2,1)S(1)} %get-tuple-element.73), channel_id=1, source_target_pairs={{0,18},{1,19},{2,16},{3,17},{4,22},{5,23},{6,20},{7,21},{8,26},{9,... | collective-permute-start | bytes 786440 | tf_op jit(solution)/shard_map/ppermute | solution.py:358
  98.0 21.9 %collective-permute-start.28 = (bf16[128,1024]{1,0:T(8,128)(2,1)S(1)}, bf16[128,1024]{1,0:T(8,128)(2,1)S(1)}, u32[]{:S(2)}, u32[]{:S(2)}) collective-permute-start(bf16[128,1024]{1,0:T(8,128)(2,1)S(1)} %get-tuple-element.74), channel_id=1, source_target_pairs={{0,16},{1,17},{2,18},{3,19},{4,20},{5,21},{6,22},{7,23},{8,24},{9,... | collective-permute-start | bytes 786440 | tf_op jit(solution)/shard_map/ppermute | solution.py:358
  99.4 20.5 %all-to-all-start = ((f32[8,1,128]{2,1,0:T(1,128)}), f32[8,1,128]{2,1,0:T(1,128)S(1)}, u32[]{:S(2)}, u32[]{:S(2)}) async-start(f32[8,1,128]{2,1,0:T(1,128)} %bitcast.2), calls=%async_computation | async-start | bytes 8192 | tf_op jit(solution)/shard_map/all_to_all | solution.py:379
